TPU v7x, 32 devices: a whole 2x2x4 slice. The times are simulated.
32 devices in a mesh: section: 2 (over core), blk: 16 (over z, y, x).
Axes of the slice: x: 2, y: 2, z: 4, core: 2. Of those that a mesh axis runs over, the one named last changes fastest.
Arguments:
- hidden: bfloat16 [2, 48, 3072], P(None, 'blk'), may hold values from -4 to 4
- qkv_weight: bfloat16 [2, 3072, 9216], P('section', None, 'blk'), may hold values from -0.109375 to 0.109375
- out_weight: bfloat16 [2, 3072, 3072], P('section', None, 'blk'), may hold values from -0.109375 to 0.109375
- modulation: float32 [2, 50, 3, 3072], P('section'), may hold values from -3 to 3
- timestep: int32 [1], replicated, may hold values from 0 to 49
- fresh: int32 [2, 2, 16], P('section'), may hold values 0 or 1
- live: int32 [2, 16], replicated, may hold values from 0 to 1, as said below
- k_stale: bfloat16 [2, 2, 48, 3072], P('section', None, 'blk'), may hold values from -6 to 6
- v_stale: bfloat16 [2, 2, 48, 3072], P('section', None, 'blk'), may hold values from -16 to 16
Outputs:
- layer_outputs: bfloat16 [2, 2, 48, 3072], P('section', None, 'blk')
Inputs may be any that keep to these rules, and one draw needn't show every extreme that they name: Block 0 of every request is live.
All inputs are finite; a program needn't handle non-finite values. No bound on the sum of `fresh` on one device may be relied on, other than what follows from the above.
Results may differ from a plain program's by a relative error of at most 0.017.
Values may be sent and summed in bfloat16 or wider, within the bound.
No kernel may reach another device: no remote copies, remote signals or barrier semaphores. Data moves between devices by JAX's collectives and lax.ppermute only.
A program may use at most 64 MiB of HBM per device.

v0:
```python
import functools

import jax
import jax.numpy as jnp
from jax import lax
from jax.experimental import pallas as pl
from jax.experimental.pallas import tpu as pltpu
from jax.sharding import PartitionSpec as P


def from_behind(shard, axis, by):
    count = lax.axis_size(axis)
    pairs = [(i, i + by) for i in range(count) if 0 <= i + by < count]
    return lax.ppermute(shard, axis, pairs)


def attend(layer_in, qkv_cols, out_cols, modulate, fresh_own, old_keys, old_values, live):
    stream = layer_in.astype(jnp.float32)
    center = jnp.mean(stream, axis=-1, keepdims=True)
    variance = jnp.mean((stream - center) ** 2, axis=-1, keepdims=True)
    normed = (stream - center) / jnp.sqrt(variance + 1e-06) * (1.0 + modulate[0]) + modulate[1]
    normed_b = normed.astype(jnp.bfloat16)
    columns = jnp.einsum(
        "rnd,dc->rnc",
        lax.all_gather(normed_b, "blk", axis=1, tiled=True),
        qkv_cols,
        preferred_element_type=jnp.float32,
    ).astype(jnp.bfloat16)
    projected = lax.all_to_all(columns, "blk", split_axis=1, concat_axis=2, tiled=True)
    num_req, num_rows, width = layer_in.shape
    queries = projected[:, :, :width]
    new_keys = projected[:, :, width : 2 * width]
    new_values = projected[:, :, 2 * width :]
    use_fresh = (fresh_own == 1)[:, None, None]
    keys = jnp.where(use_fresh, new_keys, old_keys)
    values = jnp.where(use_fresh, new_values, old_values)
    num_heads = width // 64
    num_blocks = live.shape[1]
    q_heads = queries.reshape(num_req, num_rows, num_heads, 64)
    live_float = live.astype(jnp.float32)
    run_max = jnp.full((num_req, num_heads, num_rows), -1e30, jnp.float32)
    key_piece = lax.all_gather(keys, "blk", axis=1, tiled=True)
    value_piece = lax.all_gather(values, "blk", axis=1, tiled=True)
    piece_rows = key_piece.shape[1]
    key_heads = key_piece.reshape(num_req, piece_rows, num_heads, 64)
    value_heads = value_piece.reshape(num_req, piece_rows, num_heads, 64)
    scores = (
        jnp.einsum("qrhd,qnhd->qhrn", q_heads, key_heads, preferred_element_type=jnp.float32)
        * 0.125
    )
    block_ids = jnp.arange(piece_rows) // num_rows
    one_hot = (block_ids[:, None] == jnp.arange(num_blocks)[None, :]).astype(jnp.float32)
    usable = jnp.einsum("qb,nb->qn", live_float, one_hot) > 0.5
    usable = usable[:, None, None, :]
    scores = jnp.where(usable, scores, -1e30)
    new_max = jnp.maximum(run_max, jnp.max(scores, axis=-1))
    weights = jnp.where(usable, jnp.exp(scores - new_max[..., None]), 0.0)
    new_sum = jnp.sum(weights, axis=-1)
    new_acc = jnp.einsum(
        "qhrn,qnhd->qhrd", weights, value_heads.astype(jnp.float32), precision=lax.Precision.HIGHEST
    )
    attn = new_acc / new_sum[..., None]
    attn = jnp.transpose(attn, (0, 2, 1, 3)).reshape(num_req, num_rows, width).astype(jnp.bfloat16)
    out_part = jnp.einsum(
        "rnd,dc->rnc",
        lax.all_gather(attn, "blk", axis=1, tiled=True),
        out_cols,
        preferred_element_type=jnp.float32,
    ).astype(jnp.bfloat16)
    mixed_back = lax.all_to_all(out_part, "blk", split_axis=1, concat_axis=2, tiled=True)
    return (stream + modulate[2] * mixed_back.astype(jnp.float32)).astype(jnp.bfloat16)


def pick_request(array, req_idx):
    return lax.dynamic_index_in_dim(array, req_idx, 0, keepdims=True)


def per_device_by_token(hidden, qkv_weight, out_weight, modulation, timestep, fresh, live, k_stale, v_stale):
    section_idx = lax.axis_index("section")
    block_idx = lax.axis_index("blk")
    steps_all = modulation.shape[1]
    pick_row = (jnp.arange(steps_all) == timestep[0]).astype(jnp.float32)
    modulate = jnp.einsum("t,tcd->cd", pick_row, modulation[0], precision=lax.Precision.HIGHEST)
    num_blocks = fresh.shape[2]
    own_column = (jnp.arange(num_blocks) == block_idx).astype(jnp.int32)
    fresh_own = jnp.sum(fresh[0] * own_column[None, :], axis=1)
    qkv_cols = qkv_weight[0]
    out_cols = out_weight[0]
    old_keys = k_stale[0]
    old_values = v_stale[0]
    num_req = hidden.shape[0]
    received = jnp.zeros_like(hidden[0:1])
    first_out = []
    second_out = []
    for tick_idx in range(num_req + 1):
        if tick_idx < num_req:
            own_input = hidden[tick_idx : tick_idx + 1]
        else:
            own_input = jnp.zeros_like(hidden[0:1])
        layer_in = jnp.where(section_idx == 0, own_input, received)
        req_idx = jnp.clip(tick_idx - section_idx, 0, num_req - 1)
        layer_out = attend(
            layer_in,
            qkv_cols,
            out_cols,
            modulate,
            pick_request(fresh_own, req_idx),
            pick_request(old_keys, req_idx),
            pick_request(old_values, req_idx),
            pick_request(live, req_idx),
        )
        if tick_idx < num_req:
            first_out.append(layer_out)
            received = from_behind(layer_out, "section", 1)
        if tick_idx >= 1:
            second_out.append(layer_out)
    result = jnp.where(
        section_idx == 0, jnp.concatenate(first_out, axis=0), jnp.concatenate(second_out, axis=0)
    )
    return result[None]


HEAD = 64
BF16 = jnp.bfloat16
F32 = jnp.float32
NT = (((1,), (1,)), ((), ()))
VMEM = pl.BlockSpec(memory_space=pltpu.VMEM)
SMEM = pl.BlockSpec(memory_space=pltpu.SMEM)
HBM = pl.BlockSpec(memory_space=pltpu.HBM)
ANY = pl.BlockSpec(memory_space=pl.ANY)


def call(body, outs, scratch, cost, *args, specs=None, spare=40 << 20):
    flops, moved = cost
    return pl.pallas_call(
        body,
        out_shape=outs,
        in_specs=specs or [VMEM] * len(args),
        out_specs=jax.tree.map(lambda _: VMEM, outs),
        scratch_shapes=scratch,
        compiler_params=pltpu.CompilerParams(vmem_limit_bytes=(64 << 20) - spare),
        cost_estimate=pl.CostEstimate(flops=flops, bytes_accessed=moved, transcendentals=0),
    )(*args)


def pinned(array):
    return pltpu.with_memory_space_constraint(array, pltpu.HBM)


def dot_nt(left, right):
    return lax.dot_general(left, right, NT, preferred_element_type=F32)


def halves(columns):
    mid = columns.shape[0] // 2
    return jnp.concatenate([columns[:mid], columns[mid:]], axis=1)


def pack(cols):
    return jnp.concatenate([cols[:, :128], halves(cols[:, 128:])], axis=0)


def unpack(packed):
    tokens = packed.shape[0] // 3 * 2
    last = packed[tokens:]
    return jnp.concatenate(
        [packed[:tokens], jnp.concatenate([last[:, :HEAD], last[:, HEAD:]], axis=0)], axis=1
    )


def pack_by_parity(cols, odd):
    mid = cols.shape[0] // 2
    even_form = pack(cols)
    odd_form = jnp.concatenate(
        [
            cols[:, HEAD:],
            jnp.concatenate([cols[mid:, :HEAD], cols[:mid, :HEAD]], axis=1),
        ],
        axis=0,
    )
    return jnp.where(odd, odd_form, even_form)


def assemble(blocks, whole, by_heads=False):
    tokens = whole.shape[0]
    n = blocks.shape[0]
    for d in range(0, n, 2):
        even, odd = [group * pow(3, -1, n) % n if by_heads else group for group in (d, d + 1)]
        even_last, odd_last = blocks[even, tokens:].astype(F32), blocks[odd, tokens:].astype(F32)
        left = lax.broadcasted_iota(jnp.int32, even_last.shape, 1) < HEAD
        first = jnp.where(left, even_last, odd_last)
        second = pltpu.roll(jnp.where(left, odd_last, even_last), HEAD, 1)
        at = d // 2 * 384
        whole[:, at : at + 128] = blocks[even, :tokens].astype(whole.dtype)
        whole[:, at + 128 : at + 256] = jnp.concatenate([first, second], axis=0).astype(whole.dtype)
        whole[:, at + 256 : at + 384] = blocks[odd, :tokens].astype(whole.dtype)


def own_columns(ref, rows, me):
    pair = ref[rows, pl.ds(pl.multiple_of(me // 2 * 384, 128), 384)]
    return jnp.where((me & 1) == 1, pair[:, 192:], pair[:, :192])


def norm_into(stream, mod, normed):
    tokens, width = stream.shape
    step = 128
    total = jnp.zeros((tokens, step), F32)
    for at in range(0, width, step):
        total += stream[:, at : at + step]
    center = jnp.sum(total, axis=-1, keepdims=True) / width
    total = jnp.zeros((tokens, step), F32)
    for at in range(0, width, step):
        off = stream[:, at : at + step] - center
        total += off * off
    variance = jnp.sum(total, axis=-1, keepdims=True) / width
    spread = 1.0 / jnp.sqrt(variance + 1e-06)
    for at in range(0, width, step):
        part = (stream[:, at : at + step] - center) * spread
        part = part * (1.0 + mod[0, :, at : at + step]) + mod[1, :, at : at + step]
        normed[:, at : at + step] = part.astype(BF16)


def own_or_other(layer, own, other):
    return jnp.where(lax.axis_index("section") == layer, own, other)


def dot_into(layer, left, own, other, product):
    def into(weight):
        product[...] = dot_nt(left[...], weight[...]).astype(product.dtype)

    held = lax.axis_index("section") == layer
    pl.when(held)(lambda: into(own))
    pl.when(jnp.logical_not(held))(lambda: into(other))


def normalise(layer, stream, mod, other_mod, normed, residual, scales):
    scales[...] = own_or_other(layer, mod[...], other_mod[...])
    norm_into(stream, scales, normed)
    residual[...] = own_columns(stream, slice(None), lax.axis_index("blk")).astype(BF16)


def chunks_of(columns, chunks):
    for j, chunk in enumerate(chunks):
        chunk[...] = pack(columns[:, 192 * j : 192 * j + 192])


def first_projection(arrived, own, other, mod, other_mod, other_out, chunk0, chunk1, chunk2, residual, stream, scales, normed, columns, held, sems):
    holds = lax.axis_index("section") == 0
    parts = sems.shape[0]
    size = held.shape[0] // parts
    copies = [
        pltpu.make_async_copy(own.at[pl.ds(i * size, size)], held.at[pl.ds(i * size, size)], sems.at[i])
        for i in range(parts)
    ]

    @pl.when(holds)
    def _():
        for copy in copies:
            copy.start()

    n = arrived.shape[0]
    rows = stream.shape[0] // n
    for b in range(n):
        stream[rows * b : rows * b + rows, :] = arrived[b, :rows, :].astype(F32)
    normalise(0, stream, mod, other_mod, normed, residual, scales)

    @pl.when(holds)
    def _():
        for copy in copies:
            copy.wait()

    dot_into(0, normed, held, other, columns)
    chunks_of(columns, (chunk0, chunk1, chunk2))


def next_projection(blocks, own, other, mod, other_mod, chunk0, chunk1, chunk2, residual, stream, scales, normed, columns):
    assemble(blocks, stream)
    normalise(1, stream, mod, other_mod, normed, residual, scales)
    dot_into(1, normed, own, other, columns)
    chunks_of(columns, (chunk0, chunk1, chunk2))


def attention(layer, chunk0, chunk1, chunk2, old, fresh, other_fresh, live, attn):
    n = attn.shape[0]
    me, request = lax.axis_index("blk"), lax.axis_index("section")
    first = lax.rem(lax.rem(3 * me, n), 3)
    got = [chunk[...].astype(F32) for chunk in (chunk0, chunk1, chunk2)]

    def kind(of):
        at = lax.rem(first + of, 3)
        return unpack(jnp.where(at == 0, got[0], jnp.where(at == 1, got[1], got[2])))

    queries = kind(0)
    tokens, width = queries.shape
    heads = width // HEAD
    rows = tokens // n
    token = lax.broadcasted_iota(jnp.int32, (tokens, 1), 0)
    is_fresh = jnp.zeros((tokens, 1), jnp.int32)
    for b in range(n):
        flag = own_or_other(layer, fresh[0, request, b], other_fresh[0, request, b])
        is_fresh = jnp.where(token >= b * rows, flag, is_fresh)
    is_fresh = is_fresh == 1
    key = lax.broadcasted_iota(jnp.int32, (1, tokens), 1)
    is_live = jnp.zeros((1, tokens), jnp.int32)
    for b in range(n):
        is_live = jnp.where(key >= b * rows, live[request, b], is_live)
    is_live = is_live == 1
    keys = jnp.where(is_fresh, kind(1), old[layer, :, :width].astype(F32)).astype(BF16)
    values = jnp.where(is_fresh, kind(2), old[layer, :, width:].astype(F32)).astype(BF16)
    head_of = lax.broadcasted_iota(jnp.int32, (tokens, width), 1) // HEAD
    stacked = jnp.concatenate([jnp.where(head_of == h, queries, 0.0) for h in range(heads)], axis=0)
    scores = dot_nt(stacked.astype(BF16), keys) * 0.125
    scores = jnp.where(is_live, scores, -1e30)
    top = jnp.max(scores, axis=-1, keepdims=True)
    weights = jnp.where(is_live, jnp.exp(scores - top), 0.0)
    total = jnp.sum(weights, axis=-1, keepdims=True)
    mixed = jnp.dot(weights.astype(BF16), values, preferred_element_type=F32) * (1.0 / total)
    result = jnp.zeros((tokens, width), F32)
    for h in range(heads):
        result = jnp.where(head_of == h, mixed[h * tokens : (h + 1) * tokens], result)
    packed = pack_by_parity(result, (me & 1) == 1).astype(BF16)
    for d in range(n):
        attn[d] = packed


def layer_columns(layer, blocks, own, other, mod, other_mod, residual, whole, mixed):
    me = lax.axis_index("blk")
    assemble(blocks, whole, by_heads=True)
    dot_into(layer, whole, own, other, mixed)
    gates = own_or_other(layer, mod[2], other_mod[2])
    pairs = [gates[:, at : at + 384] for at in range(0, gates.shape[1], 384)]
    pair = pairs[0]
    for i, other_pair in enumerate(pairs):
        pair = jnp.where(me // 2 == i, other_pair, pair)
    gate = jnp.where((me & 1) == 1, pair[:, 192:], pair[:, :192])
    return (residual[...].astype(F32) + gate * mixed[...].astype(F32)).astype(BF16).astype(F32)


def first_output(blocks, own, other, mod, other_mod, residual, copies, kept, *scratch):
    columns = layer_columns(0, blocks, own, other, mod, other_mod, residual, *scratch)
    packed = pack_by_parity(columns, (lax.axis_index("blk") & 1) == 1).astype(BF16)
    for d in range(copies.shape[0]):
        copies[d] = packed
    kept[...] = columns


def last_output(blocks, own, other, mod, other_mod, residual, kept, by_token, columns, *scratch):
    columns[...] = layer_columns(1, blocks, own, other, mod, other_mod, residual, *scratch)
    n = by_token.shape[0] // 2
    rows = columns.shape[0] // n
    for layer, outs in enumerate((kept, columns)):
        for b in range(n):
            by_token[layer * n + b, :rows, :] = outs[rows * b : rows * b + rows, :].astype(BF16)


def first_exchange(hidden, old_keys, old_values, other_keys, other_values, leaving, held, sems):
    copies = [
        pltpu.make_async_copy(ref, held.at[i], sems.at[i])
        for i, ref in enumerate((hidden, old_keys, old_values, other_keys, other_values))
    ]
    for copy in copies:
        copy.start()
    rows, reqs, width = hidden.shape
    n = leaving.shape[0]
    columns = width // n
    first = lax.axis_index("section") == 0
    for copy in copies:
        copy.wait()

    def of_request(which):
        own = [held[which, i].astype(F32) for i in range(rows)]
        return jnp.concatenate([jnp.where(first, pair[:1], pair[1:]) for pair in own], axis=0)

    mine, *arrays = [of_request(which) for which in range(5)]
    mine = mine.astype(BF16)
    own, other = arrays[:2], arrays[2:]
    stale = [jnp.where(first, a, b) for a, b in zip(own, other)] + [jnp.where(first, b, a) for a, b in zip(own, other)]
    for b in range(n):
        at = columns * (3 * b % n)
        block = jnp.concatenate([array[:, at : at + columns] for array in stale], axis=1)
        leaving[b, :rows, :] = mine
        for i in range(rows):
            leaving[b, rows : rows + 1, i * 4 * columns : (i + 1) * 4 * columns] = block[i : i + 1].astype(BF16)


def stale_by_token(arrived, old, rows):
    n = arrived.shape[0]
    per = rows.shape[1] // n
    wide = rows.shape[2]
    for b in range(n):
        flat = arrived[b, per : per + 1, :].astype(F32)
        for i in range(per):
            for layer in range(2):
                at = (i * 2 + layer) * wide
                rows[layer, per * b + i : per * b + i + 1, :] = flat[:, at : at + wide]
    old[...] = rows[...].astype(BF16)


def to_rows(arrived, out, rows):
    n = arrived.shape[0] // 2
    per, columns = out.shape[0], arrived.shape[2]
    for s in range(2):
        for b in range(n):
            rows[s, :per, columns * b : columns * b + columns] = arrived[s * n + b, :per, :].astype(F32)
    for i in range(per):
        out[i] = jnp.concatenate([rows[s, i : i + 1, :] for s in range(2)], axis=0).astype(BF16)


def exchange(blocks, axis):
    return lax.all_to_all(blocks, axis, split_axis=0, concat_axis=0, tiled=True)


def swap_sections(array):
    return lax.ppermute(array, "section", [(0, 1), (1, 0)])


def by_heads(chunks, n):
    inverse = pow(3, -1, n)
    return [
        lax.ppermute(chunk, "blk", [(b, (b + inverse * j) % n) for b in range(n)]) if j else chunk
        for j, chunk in enumerate(chunks)
    ]


def per_device(hidden, qkv_weight, out_weight, modulation, timestep, fresh, live, k_stale, v_stale):
    n = lax.axis_size("blk")
    columns = out_weight.shape[2]
    reqs, rows, width = hidden.shape
    if not (
        columns == 3 * HEAD
        and n % 3 == 1
        and n & (n - 1) == 0
        and reqs == lax.axis_size("section") == 2
        and rows <= 4
    ):
        return per_device_by_token(
            hidden, qkv_weight, out_weight, modulation, timestep, fresh, live, k_stale, v_stale
        )
    tokens = n * rows
    shape = jax.ShapeDtypeStruct
    packed = shape((tokens * 3 // 2, 128), BF16)
    copies = shape((n, tokens * 3 // 2, 128), BF16)
    cols = shape((tokens, columns), BF16)
    own_qkv = jnp.swapaxes(qkv_weight[0], 0, 1)
    own_out = jnp.swapaxes(out_weight[0], 0, 1)
    steps = jnp.transpose(modulation, (1, 2, 0, 3))
    old_keys = jnp.transpose(k_stale[0], (1, 0, 2))
    old_values = jnp.transpose(v_stale[0], (1, 0, 2))

    other_keys, other_values, timestep, sent_fresh = lax.optimization_barrier(
        (swap_sections(old_keys), swap_sections(old_values), timestep, fresh)
    )
    mod = lax.dynamic_index_in_dim(steps, timestep[0], 0, keepdims=False)
    other_mod, other_fresh, sent_qkv, sent_out = lax.optimization_barrier(
        (swap_sections(mod), swap_sections(sent_fresh), own_qkv, own_out)
    )
    mods = (mod, other_mod)
    flags = (fresh, other_fresh)
    other_qkv, other_out = swap_sections(sent_qkv), swap_sections(sent_out)
    out = (own_out, other_out)
    leaving = call(
        first_exchange,
        shape((n, 4, width), BF16),
        [pltpu.VMEM((5, rows, reqs, width), BF16), pltpu.SemaphoreType.DMA((5,))],
        (0, 1000000),
        *(pinned(array) for array in (jnp.transpose(hidden, (1, 0, 2)), old_keys, old_values)),
        other_keys,
        other_values,
        specs=[HBM] * 3 + [ANY] * 2,
    )
    arrived = exchange(leaving, "blk")

    blocks = arrived
    for layer in range(2):
        *chunks, residual = call(
            next_projection if layer else first_projection,
            [packed, packed, packed, cols],
            [
                pltpu.VMEM((tokens, width), F32),
                pltpu.VMEM(mod.shape, F32),
                pltpu.VMEM((tokens, width), BF16),
                pltpu.VMEM((tokens, 3 * columns), BF16),
            ]
            + ([] if layer else [pltpu.VMEM(own_qkv.shape, BF16), pltpu.SemaphoreType.DMA((36,))]),
            (2 * tokens * width * 3 * columns, 8 * width * columns),
            blocks,
            *((own_qkv, other_qkv, *mods) if layer else (pinned(own_qkv), other_qkv, *mods, other_out)),
            **({} if layer else {"specs": [VMEM, HBM, VMEM, VMEM, VMEM, ANY]}),
        )
        if layer == 0:
            arrived, chunks[1] = lax.optimization_barrier((arrived, chunks[1]))
            old = call(
                stale_by_token,
                shape((2, tokens, 2 * columns), BF16),
                [pltpu.VMEM((2, tokens, 2 * columns), F32)],
                (0, 200000),
                arrived,
            )
        attn = call(
            functools.partial(attention, layer),
            copies,
            [],
            (8 * tokens * tokens * columns, 300000),
            *by_heads(chunks, n),
            old,
            *flags,
            live,
            specs=[VMEM] * 4 + [SMEM] * 3,
        )
        args = (exchange(attn, "blk"), *out, *mods, residual)
        cost = (2 * tokens * width * columns, 4 * width * columns)
        held = [pltpu.VMEM((tokens, width), BF16), pltpu.VMEM((tokens, columns), BF16)]
        if layer == 0:
            leaving, kept = call(first_output, [copies, shape((tokens, columns), F32)], held, cost, *args)
            blocks = exchange(leaving, "blk")
        else:
            leaving = call(
                last_output,
                shape((2 * n, 4, columns), BF16),
                [pltpu.VMEM((tokens, columns), F32)] + held,
                cost,
                *args,
                kept,
            )
    result = call(
        to_rows,
        shape((rows, reqs, width), BF16),
        [pltpu.VMEM((2, 8, width), F32)],
        (0, 100000),
        exchange(leaving, ("section", "blk")),
    )
    return jnp.transpose(result, (1, 0, 2))[None]


def solution(mesh):
    return jax.shard_map(
        per_device,
        mesh=mesh,
        in_specs=(
            P(None, "blk", None),
            P("section", None, "blk"),
            P("section", None, "blk"),
            P("section", None, None, None),
            P(),
            P("section", None, None),
            P(),
            P("section", None, "blk", None),
            P("section", None, "blk", None),
        ),
        out_specs=P("section", None, "blk", None),
        check_vma=False,
    )
```

profile of v0, /device:TPU:0, one launch (start us, length us, event | category | flops | bytes accessed | tf_op | source)
XLA Modules:
  0.0 98.8 jit_solution(728718297093082633)
XLA Ops:
  0.0 0.0 copy-start
  0.0 0.5 collective-permute-start
  0.5 0.1 collective-permute-start.1
  1.2 0.3 copy-done
  1.5 0.5 collective-permute-start.2
  2.0 0.0 collective-permute-done.other_keys
  2.0 0.0 collective-permute-done.1.other_values
  2.0 0.1 collective-permute-start.3
  2.1 0.8 collective-permute-done.2.other_mod
  2.8 0.5 collective-permute-done.3.other_fresh
  3.3 0.2 collective-permute-start.4
  3.5 0.3 collective-permute-start.5
  3.8 1.1 %shard_map.91 = bf16[16,4,3072]{2,1,0:T(4,128)(2,1)S(1)} custom-call(bf16[3,2,3072]{2,1,0:T(2,128)(2,1)} %bitcast.28, bf16[3,2,3072]{2,1,0:T(2,128)(2,1)} %bitcast.30, bf16[3,2,3072]{2,1,0:T(2,128)(2,1)} %bitcast.32, bf16[3,2,3072]{2,1,0:T(2,128)(2,1)S(1)} %collective-permute-done.other_keys, bf16[3,2,3072]{2,1,0:T(2,128)(2,1)S(1)} %collective-permute-done.1.other_values), custom_call_target="tpu_custom_call" | custom-call | bytes 1000000 | tf_op jit(solution)/shard_map/pallas_call | solution.py:135
  4.9 20.9 %all_to_all.25.arrived = bf16[16,4,3072]{2,1,0:T(4,128)(2,1)S(1)} all-to-all(bf16[16,4,3072]{2,1,0:T(4,128)(2,1)S(1)} %shard_map.91), channel_id=1, replica_groups=mesh['section'=2,'blk'=16] {'blk'}, dimensions={0} | all-to-all | bytes 786432 | tf_op jit(solution)/shard_map/all_to_all | solution.py:410
  25.9 0.0 copy-start.3
  25.9 0.0 copy-start.4
  25.9 0.0 collective-permute-done.5.other_out.other
  25.9 0.0 collective-permute-done.4.other
  25.9 3.7 %shard_map.92 = (bf16[72,128]{1,0:T(8,128)(2,1)S(1)}, bf16[72,128]{1,0:T(8,128)(2,1)S(1)}, bf16[72,128]{1,0:T(8,128)(2,1)S(1)}, bf16[48,192]{1,0:T(8,128)(2,1)S(1)}) custom-call(bf16[16,4,3072]{2,1,0:T(4,128)(2,1)S(1)} %all_to_all.25.arrived, bf16[576,3072]{1,0:T(8,128)(2,1)} %bitcast.23, bf16[576,3072]{1,0:T(8,128)(2,1)S(1)} %collective-permute-done.4.other, ...), custom_call_target="tpu_custom_call" | custom-call | flops 169869312 | bytes 4718592 | tf_op jit(solution)/shard_map/pallas_call | solution.py:135
  29.6 0.0 copy-start.2
  29.6 0.9 collective-permute-start.6
  30.5 2.1 %collective-permute-start.7 = (bf16[72,128]{1,0:T(8,128)(2,1)S(1)}, bf16[72,128]{1,0:T(8,128)(2,1)S(1)}, u32[]{:S(2)}, u32[]{:S(2)}) collective-permute-start(bf16[72,128]{1,0:T(8,128)(2,1)S(1)} %get-tuple-element.35), channel_id=1, source_target_pairs={{0,6},{1,7},{2,8},{3,9},{4,10},{5,11},{6,12},{7,13},{8,14},{9,15},... | collective-permute-start | bytes 55304 | tf_op jit(solution)/shard_map/ppermute | solution.py:420
  32.6 0.1 shard_map.93.old
  32.7 1.6 %collective-permute-done.6.chunk1 = bf16[72,128]{1,0:T(8,128)(2,1)S(1)} collective-permute-done((bf16[72,128]{1,0:T(8,128)(2,1)S(1)}, bf16[72,128]{1,0:T(8,128)(2,1)S(1)}, u32[]{:S(2)}, u32[]{:S(2)}) %collective-permute-start.6) | collective-permute-done | bytes 18464 | tf_op jit(solution)/shard_map/ppermute | solution.py:420
  34.3 1.7 %collective-permute-done.7.chunk2 = bf16[72,128]{1,0:T(8,128)(2,1)S(1)} collective-permute-done((bf16[72,128]{1,0:T(8,128)(2,1)S(1)}, bf16[72,128]{1,0:T(8,128)(2,1)S(1)}, u32[]{:S(2)}, u32[]{:S(2)}) %collective-permute-start.7) | collective-permute-done | bytes 18464 | tf_op jit(solution)/shard_map/ppermute | solution.py:420
  36.0 0.0 copy-done.3
  36.0 0.0 copy-done.4
  36.0 1.3 %shard_map.94 = bf16[16,72,128]{2,1,0:T(8,128)(2,1)S(1)} custom-call(bf16[72,128]{1,0:T(8,128)(2,1)S(1)} %get-tuple-element.32.chunk0, bf16[72,128]{1,0:T(8,128)(2,1)S(1)} %collective-permute-done.6.chunk1, bf16[72,128]{1,0:T(8,128)(2,1)S(1)} %collective-permute-done.7.chunk2, bf16[2,48,384]{2,1,0:T(8,128)(2,1)S(1)} %shard_map.93.old, ...), custom_call_target="tpu_custom_call" | custom-call | flops 3538944 | bytes 300000 | tf_op jit(solution)/shard_map/pallas_call | solution.py:135
  37.4 0.0 copy-start.1
  37.4 14.0 %all_to_all.26.blocks = bf16[16,72,128]{2,1,0:T(8,128)(2,1)S(1)} all-to-all(bf16[16,72,128]{2,1,0:T(8,128)(2,1)S(1)} %shard_map.94), channel_id=1, replica_groups=mesh['section'=2,'blk'=16] {'blk'}, dimensions={0} | all-to-all | bytes 589824 | tf_op jit(solution)/shard_map/all_to_all | solution.py:410
  51.3 0.0 copy-done.2
  51.3 0.9 shard_map.95
  52.2 12.4 %all_to_all.27.blocks = bf16[16,72,128]{2,1,0:T(8,128)(2,1)S(1)} all-to-all(bf16[16,72,128]{2,1,0:T(8,128)(2,1)S(1)} %get-tuple-element.39), channel_id=1, replica_groups=mesh['section'=2,'blk'=16] {'blk'}, dimensions={0} | all-to-all | bytes 589824 | tf_op jit(solution)/shard_map/all_to_all | solution.py:410
  64.6 0.0 copy-done.1
  64.6 1.7 %shard_map.96 = (bf16[72,128]{1,0:T(8,128)(2,1)S(1)}, bf16[72,128]{1,0:T(8,128)(2,1)S(1)}, bf16[72,128]{1,0:T(8,128)(2,1)S(1)}, bf16[48,192]{1,0:T(8,128)(2,1)S(1)}) custom-call(bf16[16,72,128]{2,1,0:T(8,128)(2,1)S(1)} %all_to_all.27.blocks, bf16[576,3072]{1,0:T(8,128)(2,1)S(1)} %bitcast.24, bf16[576,3072]{1,0:T(8,128)(2,1)S(1)} %collective-permute-done.4.other, ...), custom_call_target="tpu_custom_call" | custom-call | flops 169869312 | bytes 4718592 | tf_op jit(solution)/shard_map/pallas_call | solution.py:135
  66.3 1.3 %collective-permute-start.8 = (bf16[72,128]{1,0:T(8,128)(2,1)S(1)}, bf16[72,128]{1,0:T(8,128)(2,1)S(1)}, u32[]{:S(2)}, u32[]{:S(2)}) collective-permute-start(bf16[72,128]{1,0:T(8,128)(2,1)S(1)} %get-tuple-element.41), channel_id=1, source_target_pairs={{0,11},{1,12},{2,13},{3,14},{4,15},{5,0},{6,1},{7,2},{8,3},{9,4},{... | collective-permute-start | bytes 55304 | tf_op jit(solution)/shard_map/ppermute | solution.py:420
  67.6 2.6 %collective-permute-start.9 = (bf16[72,128]{1,0:T(8,128)(2,1)S(1)}, bf16[72,128]{1,0:T(8,128)(2,1)S(1)}, u32[]{:S(2)}, u32[]{:S(2)}) collective-permute-start(bf16[72,128]{1,0:T(8,128)(2,1)S(1)} %get-tuple-element.42), channel_id=1, source_target_pairs={{0,6},{1,7},{2,8},{3,9},{4,10},{5,11},{6,12},{7,13},{8,14},{9,15},... | collective-permute-start | bytes 55304 | tf_op jit(solution)/shard_map/ppermute | solution.py:420
  70.1 0.9 collective-permute-done.8.chunk1
  71.0 2.2 %collective-permute-done.9.chunk2 = bf16[72,128]{1,0:T(8,128)(2,1)S(1)} collective-permute-done((bf16[72,128]{1,0:T(8,128)(2,1)S(1)}, bf16[72,128]{1,0:T(8,128)(2,1)S(1)}, u32[]{:S(2)}, u32[]{:S(2)}) %collective-permute-start.9) | collective-permute-done | bytes 18464 | tf_op jit(solution)/shard_map/ppermute | solution.py:420
  73.1 1.3 %shard_map.97 = bf16[16,72,128]{2,1,0:T(8,128)(2,1)S(1)} custom-call(bf16[72,128]{1,0:T(8,128)(2,1)S(1)} %get-tuple-element.40.chunk0, bf16[72,128]{1,0:T(8,128)(2,1)S(1)} %collective-permute-done.8.chunk1, bf16[72,128]{1,0:T(8,128)(2,1)S(1)} %collective-permute-done.9.chunk2, bf16[2,48,384]{2,1,0:T(8,128)(2,1)S(1)} %shard_map.93.old, ...), custom_call_target="tpu_custom_call" | custom-call | flops 3538944 | bytes 300000 | tf_op jit(solution)/shard_map/pallas_call | solution.py:135
  74.4 13.2 %all_to_all.28.blocks = bf16[16,72,128]{2,1,0:T(8,128)(2,1)S(1)} all-to-all(bf16[16,72,128]{2,1,0:T(8,128)(2,1)S(1)} %shard_map.97), channel_id=1, replica_groups=mesh['section'=2,'blk'=16] {'blk'}, dimensions={0} | all-to-all | bytes 589824 | tf_op jit(solution)/shard_map/all_to_all | solution.py:410
  87.6 0.7 shard_map.98
  88.3 9.7 %all_to_all.29.arrived = bf16[32,4,192]{2,1,0:T(4,128)(2,1)S(1)} all-to-all(bf16[32,4,192]{2,1,0:T(4,128)(2,1)S(1)} %shard_map.98), channel_id=1, replica_groups=mesh['section'=2,'blk'=16] {'section','blk'}, dimensions={0} | all-to-all | bytes 98304 | tf_op jit(solution)/shard_map/all_to_all | solution.py:410
  98.0 0.8 shard_map.99
  (1 shorter events, 0.0 us)
Async XLA Ops:
  0.0 1.5 %copy-start = (f32[1,50,3,3072]{3,0,2,1:T(1,128)S(1)}, f32[1,50,3,3072]{3,0,2,1:T(1,128)}, u32[]{:S(2)}) copy-start(f32[1,50,3,3072]{3,0,2,1:T(1,128)} %param.12) | copy-start | bytes 5529604
  0.0 2.0 %collective-permute-start = (bf16[3,2,3072]{2,1,0:T(2,128)(2,1)}, bf16[3,2,3072]{2,1,0:T(2,128)(2,1)S(1)}, u32[]{:S(2)}, u32[]{:S(2)}) collective-permute-start(bf16[3,2,3072]{2,1,0:T(2,128)(2,1)} %bitcast.29), channel_id=1, source_target_pairs={{0,16},{16,0},{1,17},{17,1},{2,18},{18,2},{3,19},{19,3},{4,20},{20... | collective-permute-start | bytes 110600 | tf_op jit(solution)/shard_map/ppermute | solution.py:414
  0.5 1.5 %collective-permute-start.1 = (bf16[3,2,3072]{2,1,0:T(2,128)(2,1)}, bf16[3,2,3072]{2,1,0:T(2,128)(2,1)S(1)}, u32[]{:S(2)}, u32[]{:S(2)}) collective-permute-start(bf16[3,2,3072]{2,1,0:T(2,128)(2,1)} %bitcast.31), channel_id=1, source_target_pairs={{0,16},{16,0},{1,17},{17,1},{2,18},{18,2},{3,19},{19,3},{4,20},{20... | collective-permute-start | bytes 110600 | tf_op jit(solution)/shard_map/ppermute | solution.py:414
  1.5 1.3 %collective-permute-start.2 = (f32[3,1,3072]{2,1,0:T(1,128)S(1)}, f32[3,1,3072]{2,1,0:T(1,128)S(1)}, u32[]{:S(2)}, u32[]{:S(2)}) collective-permute-start(f32[3,1,3072]{2,1,0:T(1,128)S(1)} %dynamic-slice_bitcast_fusion.mod), channel_id=1, source_target_pairs={{0,16},{16,0},{1,17},{17,1},{2,18},{18,2},{3,19},{19,3},{4,20},{20... | collective-permute-start | bytes 110600 | tf_op jit(solution)/shard_map/ppermute | solution.py:414
  2.0 1.4 %collective-permute-start.3 = (s32[1,2,16]{2,1,0:T(2,128)}, s32[1,2,16]{2,1,0:T(2,128)S(1)}, u32[]{:S(2)}, u32[]{:S(2)}) collective-permute-start(s32[1,2,16]{2,1,0:T(2,128)} %fresh.3), channel_id=1, source_target_pairs={{0,16},{16,0},{1,17},{17,1},{2,18},{18,2},{3,19},{19,3},{4,20},{20... | collective-permute-start | bytes 392 | tf_op jit(solution)/shard_map/ppermute | solution.py:414
  3.3 22.6 %collective-permute-start.4 = (bf16[576,3072]{1,0:T(8,128)(2,1)}, bf16[576,3072]{1,0:T(8,128)(2,1)S(1)}, u32[]{:S(2)}, u32[]{:S(2)}) collective-permute-start(bf16[576,3072]{1,0:T(8,128)(2,1)} %bitcast.22), channel_id=1, source_target_pairs={{0,16},{16,0},{1,17},{17,1},{2,18},{18,2},{3,19},{19,3},{4,20},{20... | collective-permute-start | bytes 10616840 | tf_op jit(solution)/shard_map/ppermute | solution.py:414
  3.5 22.4 %collective-permute-start.5 = (bf16[192,3072]{1,0:T(8,128)(2,1)}, bf16[192,3072]{1,0:T(8,128)(2,1)S(1)}, u32[]{:S(2)}, u32[]{:S(2)}) collective-permute-start(bf16[192,3072]{1,0:T(8,128)(2,1)} %bitcast.25), channel_id=1, source_target_pairs={{0,16},{16,0},{1,17},{17,1},{2,18},{18,2},{3,19},{19,3},{4,20},{20... | collective-permute-start | bytes 3538952 | tf_op jit(solution)/shard_map/ppermute | solution.py:414
  25.9 10.2 %copy-start.3 = (s32[1,2,16]{2,1,0:T(2,128)S(1)}, s32[1,2,16]{2,1,0:T(2,128)}, u32[]{:S(2)}) copy-start(s32[1,2,16]{2,1,0:T(2,128)} %fresh.3) | copy-start | bytes 388
  25.9 10.2 %copy-start.4 = (s32[2,16]{1,0:T(2,128)S(1)}, s32[2,16]{1,0:T(2,128)}, u32[]{:S(2)}) copy-start(s32[2,16]{1,0:T(2,128)} %live.3) | copy-start | bytes 388
  29.6 21.7 %copy-start.2 = (bf16[1,3072,192]{1,2,0:T(8,128)(2,1)S(1)}, bf16[1,3072,192]{1,2,0:T(8,128)(2,1)}, u32[]{:S(2)}) copy-start(bf16[1,3072,192]{1,2,0:T(8,128)(2,1)} %param.11) | copy-start | bytes 3538948
  29.6 4.7 %collective-permute-start.6 = (bf16[72,128]{1,0:T(8,128)(2,1)S(1)}, bf16[72,128]{1,0:T(8,128)(2,1)S(1)}, u32[]{:S(2)}, u32[]{:S(2)}) collective-permute-start(bf16[72,128]{1,0:T(8,128)(2,1)S(1)} %get-tuple-element.34), channel_id=1, source_target_pairs={{0,11},{1,12},{2,13},{3,14},{4,15},{5,0},{6,1},{7,2},{8,3},{9,4},{... | collective-permute-start | bytes 55304 | tf_op jit(solution)/shard_map/ppermute | solution.py:420
  30.5 5.6 %collective-permute-start.7 = (bf16[72,128]{1,0:T(8,128)(2,1)S(1)}, bf16[72,128]{1,0:T(8,128)(2,1)S(1)}, u32[]{:S(2)}, u32[]{:S(2)}) collective-permute-start(bf16[72,128]{1,0:T(8,128)(2,1)S(1)} %get-tuple-element.35), channel_id=1, source_target_pairs={{0,6},{1,7},{2,8},{3,9},{4,10},{5,11},{6,12},{7,13},{8,14},{9,15},... | collective-permute-start | bytes 55304 | tf_op jit(solution)/shard_map/ppermute | solution.py:420
  37.4 27.3 %copy-start.1 = (bf16[1,3072,576]{1,2,0:T(8,128)(2,1)S(1)}, bf16[1,3072,576]{1,2,0:T(8,128)(2,1)}, u32[]{:S(2)}) copy-start(bf16[1,3072,576]{1,2,0:T(8,128)(2,1)} %param.10) | copy-start | bytes 10616836
  66.3 4.7 %collective-permute-start.8 = (bf16[72,128]{1,0:T(8,128)(2,1)S(1)}, bf16[72,128]{1,0:T(8,128)(2,1)S(1)}, u32[]{:S(2)}, u32[]{:S(2)}) collective-permute-start(bf16[72,128]{1,0:T(8,128)(2,1)S(1)} %get-tuple-element.41), channel_id=1, source_target_pairs={{0,11},{1,12},{2,13},{3,14},{4,15},{5,0},{6,1},{7,2},{8,3},{9,4},{... | collective-permute-start | bytes 55304 | tf_op jit(solution)/shard_map/ppermute | solution.py:420
  67.6 5.6 %collective-permute-start.9 = (bf16[72,128]{1,0:T(8,128)(2,1)S(1)}, bf16[72,128]{1,0:T(8,128)(2,1)S(1)}, u32[]{:S(2)}, u32[]{:S(2)}) collective-permute-start(bf16[72,128]{1,0:T(8,128)(2,1)S(1)} %get-tuple-element.42), channel_id=1, source_target_pairs={{0,6},{1,7},{2,8},{3,9},{4,10},{5,11},{6,12},{7,13},{8,14},{9,15},... | collective-permute-start | bytes 55304 | tf_op jit(solution)/shard_map/ppermute | solution.py:420
where the time goes:
time: 99.1 us; the launch traced here: 98.8 us
  blocking collectives  70.2 us (71%)
  Pallas kernels  11.5 us (12%)
  starting transfers between devices  8.36 us (8%)
  waiting for transfers between devices  7.62 us (8%)
    all_to_all x5, blocking collectives, exchange(): return lax.all_to_all(blocks, axis, split_axis=0, concat_axis=0, tiled=True)  70.2 us
    pallas_call x9, Pallas kernels, call(): pl.pallas_call(body, out_shape=outs, in_specs=specs or [VMEM] * len(args)...  11.5 us
    ppermute x4, starting transfers between devices, by_heads(): lax.ppermute(chunk, 'blk', [(b, (b + inverse * j) % n) for b in range(n)])  6.79 us
    ppermute x4, waiting for transfers between devices, by_heads(): lax.ppermute(chunk, 'blk', [(b, (b + inverse * j) % n) for b in range(n)])  6.34 us
  transfers between devices with their start and end apart: 10, of which 6 were waited for; matrix products, arithmetic and copies ran while one was open for 0% of the time, Pallas kernels for 1%

commit v1 on v0

--- a/solution.py
+++ b/solution.py
@@ -121,6 +121,7 @@
 
 
 HEAD = 64
+HOME = 1
 BF16 = jnp.bfloat16
 F32 = jnp.float32
 NT = (((1,), (1,)), ((), ()))
@@ -185,7 +186,7 @@
     tokens = whole.shape[0]
     n = blocks.shape[0]
     for d in range(0, n, 2):
-        even, odd = [group * pow(3, -1, n) % n if by_heads else group for group in (d, d + 1)]
+        even, odd = [(group - HOME) * pow(3, -1, n) % n if by_heads else group for group in (d, d + 1)]
         even_last, odd_last = blocks[even, tokens:].astype(F32), blocks[odd, tokens:].astype(F32)
         left = lax.broadcasted_iota(jnp.int32, even_last.shape, 1) < HEAD
         first = jnp.where(left, even_last, odd_last)
@@ -266,10 +267,16 @@
 
     @pl.when(holds)
     def _():
-        for copy in copies:
-            copy.wait()
-
-    dot_into(0, normed, held, other, columns)
+        for at in range(0, held.shape[0], 256):
+            end = min(at + 256, held.shape[0])
+            for copy in copies[at // size : end // size]:
+                copy.wait()
+            columns[:, at:end] = dot_nt(normed[...], held[at:end, :]).astype(BF16)
+
+    @pl.when(jnp.logical_not(holds))
+    def _():
+        columns[...] = dot_nt(normed[...], other[...]).astype(BF16)
+
     chunks_of(columns, (chunk0, chunk1, chunk2))
 
 
@@ -283,7 +290,7 @@
 def attention(layer, chunk0, chunk1, chunk2, old, fresh, other_fresh, live, attn):
     n = attn.shape[0]
     me, request = lax.axis_index("blk"), lax.axis_index("section")
-    first = lax.rem(lax.rem(3 * me, n), 3)
+    first = lax.rem(lax.rem(3 * me + HOME, n), 3)
     got = [chunk[...].astype(F32) for chunk in (chunk0, chunk1, chunk2)]
 
     def kind(of):
@@ -318,7 +325,7 @@
     result = jnp.zeros((tokens, width), F32)
     for h in range(heads):
         result = jnp.where(head_of == h, mixed[h * tokens : (h + 1) * tokens], result)
-    packed = pack_by_parity(result, (me & 1) == 1).astype(BF16)
+    packed = pack_by_parity(result, ((me + HOME) & 1) == 1).astype(BF16)
     for d in range(n):
         attn[d] = packed
 
@@ -376,7 +383,7 @@
     own, other = arrays[:2], arrays[2:]
     stale = [jnp.where(first, a, b) for a, b in zip(own, other)] + [jnp.where(first, b, a) for a, b in zip(own, other)]
     for b in range(n):
-        at = columns * (3 * b % n)
+        at = columns * ((3 * b + HOME) % n)
         block = jnp.concatenate([array[:, at : at + columns] for array in stale], axis=1)
         leaving[b, :rows, :] = mine
         for i in range(rows):
@@ -417,7 +424,7 @@
 def by_heads(chunks, n):
     inverse = pow(3, -1, n)
     return [
-        lax.ppermute(chunk, "blk", [(b, (b + inverse * j) % n) for b in range(n)]) if j else chunk
+        lax.ppermute(chunk, "blk", [(b, (b + inverse * (j - HOME)) % n) for b in range(n)]) if j != HOME else chunk
         for j, chunk in enumerate(chunks)
     ]
 
@@ -481,7 +488,7 @@
                 pltpu.VMEM((tokens, width), BF16),
                 pltpu.VMEM((tokens, 3 * columns), BF16),
             ]
-            + ([] if layer else [pltpu.VMEM(own_qkv.shape, BF16), pltpu.SemaphoreType.DMA((36,))]),
+            + ([] if layer else [pltpu.VMEM(own_qkv.shape, BF16), pltpu.SemaphoreType.DMA((9,))]),
             (2 * tokens * width * 3 * columns, 8 * width * columns),
             blocks,
             *((own_qkv, other_qkv, *mods) if layer else (pinned(own_qkv), other_qkv, *mods, other_out)),

time: 99.1 us -> 105 us (1.060)
  blocking collectives: 70.2 us -> 76.1 us
  waiting for transfers between devices: 7.62 us -> 4.63 us
  starting transfers between devices: 8.36 us -> 11.1 us
    all_to_all x5, blocking collectives: 70.2 us -> 76.1 us  [exchange(): return lax.all_to_all(blocks, axis, split_axis=0, concat_axis=0, tiled=True)]
    ppermute x4, waiting for transfers between devices: 6.34 us -> 3.36 us  [by_heads(): lax.ppermute(chunk, 'blk', [(b, (b + inverse * (j - HOME)) % n) for b in...]
    ppermute x4, starting transfers between devices: 6.79 us -> 9.5 us  [by_heads(): lax.ppermute(chunk, 'blk', [(b, (b + inverse * (j - HOME)) % n) for b in...]
  transfers between devices with their start and end apart: 10 -> 10, of which waited for: 6 -> 4; matrix products, arithmetic and copies ran while one was open for 0% -> 0% of each run, Pallas kernels for 1% -> 1%
where the time goes in v1:
time: 105 us
  blocking collectives  76.1 us (72%)
  Pallas kernels  11.9 us (11%)
  starting transfers between devices  11.1 us (11%)
  waiting for transfers between devices  4.63 us (4%)
    all_to_all x5, blocking collectives, exchange(): return lax.all_to_all(blocks, axis, split_axis=0, concat_axis=0, tiled=True)  76.1 us
    pallas_call x9, Pallas kernels, call(): pl.pallas_call(body, out_shape=outs, in_specs=specs or [VMEM] * len(args)...  11.9 us
    ppermute x4, starting transfers between devices, by_heads(): lax.ppermute(chunk, 'blk', [(b, (b + inverse * (j - HOME)) % n) for b in...  9.5 us
    ppermute x4, waiting for transfers between devices, by_heads(): lax.ppermute(chunk, 'blk', [(b, (b + inverse * (j - HOME)) % n) for b in...  3.36 us
  transfers between devices with their start and end apart: 10, of which 4 were waited for; matrix products, arithmetic and copies ran while one was open for 0% of the time, Pallas kernels for 1%

profile of v1, /device:TPU:0, one launch (start us, length us, event | category | flops | bytes accessed | tf_op | source)
XLA Modules:
  0.0 104.7 jit_solution(6204962361639043881)
XLA Ops:
  0.0 0.0 copy-start
  0.0 0.5 collective-permute-start
  0.5 0.1 collective-permute-start.1
  1.2 0.3 copy-done
  1.5 0.5 collective-permute-start.2
  2.0 0.0 collective-permute-done.other_keys
  2.0 0.0 collective-permute-done.1.other_values
  2.0 0.1 collective-permute-start.3
  2.1 0.8 collective-permute-done.2.other_mod
  2.8 0.5 collective-permute-done.3.other_fresh
  3.3 0.2 collective-permute-start.4
  3.5 0.3 collective-permute-start.5
  3.8 1.1 %shard_map.91 = bf16[16,4,3072]{2,1,0:T(4,128)(2,1)S(1)} custom-call(bf16[3,2,3072]{2,1,0:T(2,128)(2,1)} %bitcast.28, bf16[3,2,3072]{2,1,0:T(2,128)(2,1)} %bitcast.30, bf16[3,2,3072]{2,1,0:T(2,128)(2,1)} %bitcast.32, bf16[3,2,3072]{2,1,0:T(2,128)(2,1)S(1)} %collective-permute-done.other_keys, bf16[3,2,3072]{2,1,0:T(2,128)(2,1)S(1)} %collective-permute-done.1.other_values), custom_call_target="tpu_custom_call" | custom-call | bytes 1000000 | tf_op jit(solution)/shard_map/pallas_call | solution.py:136
  4.9 20.9 %all_to_all.25.arrived = bf16[16,4,3072]{2,1,0:T(4,128)(2,1)S(1)} all-to-all(bf16[16,4,3072]{2,1,0:T(4,128)(2,1)S(1)} %shard_map.91), channel_id=1, replica_groups=mesh['section'=2,'blk'=16] {'blk'}, dimensions={0} | all-to-all | bytes 786432 | tf_op jit(solution)/shard_map/all_to_all | solution.py:417
  25.9 0.0 copy-start.3
  25.9 0.0 copy-start.4
  25.9 0.0 collective-permute-done.5.other_out.other
  25.9 0.0 collective-permute-done.4.other
  25.9 4.0 %shard_map.92 = (bf16[72,128]{1,0:T(8,128)(2,1)S(1)}, bf16[72,128]{1,0:T(8,128)(2,1)S(1)}, bf16[72,128]{1,0:T(8,128)(2,1)S(1)}, bf16[48,192]{1,0:T(8,128)(2,1)S(1)}) custom-call(bf16[16,4,3072]{2,1,0:T(4,128)(2,1)S(1)} %all_to_all.25.arrived, bf16[576,3072]{1,0:T(8,128)(2,1)} %bitcast.23, bf16[576,3072]{1,0:T(8,128)(2,1)S(1)} %collective-permute-done.4.other, ...), custom_call_target="tpu_custom_call" | custom-call | flops 169869312 | bytes 4718592 | tf_op jit(solution)/shard_map/pallas_call | solution.py:136
  29.9 0.0 copy-start.2
  29.9 1.1 %collective-permute-start.6 = (bf16[72,128]{1,0:T(8,128)(2,1)S(1)}, bf16[72,128]{1,0:T(8,128)(2,1)S(1)}, u32[]{:S(2)}, u32[]{:S(2)}) collective-permute-start(bf16[72,128]{1,0:T(8,128)(2,1)S(1)} %get-tuple-element.32), channel_id=1, source_target_pairs={{0,5},{1,6},{2,7},{3,8},{4,9},{5,10},{6,11},{7,12},{8,13},{9,14},{... | collective-permute-start | bytes 55304 | tf_op jit(solution)/shard_map/ppermute | solution.py:427
  31.1 3.6 %collective-permute-start.7 = (bf16[72,128]{1,0:T(8,128)(2,1)S(1)}, bf16[72,128]{1,0:T(8,128)(2,1)S(1)}, u32[]{:S(2)}, u32[]{:S(2)}) collective-permute-start(bf16[72,128]{1,0:T(8,128)(2,1)S(1)} %get-tuple-element.35), channel_id=1, source_target_pairs={{0,11},{1,12},{2,13},{3,14},{4,15},{5,0},{6,1},{7,2},{8,3},{9,4},{... | collective-permute-start | bytes 55304 | tf_op jit(solution)/shard_map/ppermute | solution.py:427
  34.7 0.1 shard_map.93.old
  34.8 1.6 %collective-permute-done.6.chunk0 = bf16[72,128]{1,0:T(8,128)(2,1)S(1)} collective-permute-done((bf16[72,128]{1,0:T(8,128)(2,1)S(1)}, bf16[72,128]{1,0:T(8,128)(2,1)S(1)}, u32[]{:S(2)}, u32[]{:S(2)}) %collective-permute-start.6) | collective-permute-done | bytes 18464 | tf_op jit(solution)/shard_map/ppermute | solution.py:427
  36.4 0.0 collective-permute-done.7.chunk2
  36.4 0.0 copy-done.3
  36.5 0.0 copy-done.4
  36.5 1.3 %shard_map.94 = bf16[16,72,128]{2,1,0:T(8,128)(2,1)S(1)} custom-call(bf16[72,128]{1,0:T(8,128)(2,1)S(1)} %collective-permute-done.6.chunk0, bf16[72,128]{1,0:T(8,128)(2,1)S(1)} %get-tuple-element.34.chunk1, bf16[72,128]{1,0:T(8,128)(2,1)S(1)} %collective-permute-done.7.chunk2, bf16[2,48,384]{2,1,0:T(8,128)(2,1)S(1)} %shard_map.93.old, ...), custom_call_target="tpu_custom_call" | custom-call | flops 3538944 | bytes 300000 | tf_op jit(solution)/shard_map/pallas_call | solution.py:136
  37.8 0.0 copy-start.1
  37.8 16.1 %all_to_all.26.blocks = bf16[16,72,128]{2,1,0:T(8,128)(2,1)S(1)} all-to-all(bf16[16,72,128]{2,1,0:T(8,128)(2,1)S(1)} %shard_map.94), channel_id=1, replica_groups=mesh['section'=2,'blk'=16] {'blk'}, dimensions={0} | all-to-all | bytes 589824 | tf_op jit(solution)/shard_map/all_to_all | solution.py:417
  53.9 0.0 copy-done.2
  53.9 0.9 shard_map.95
  54.7 12.6 %all_to_all.27.blocks = bf16[16,72,128]{2,1,0:T(8,128)(2,1)S(1)} all-to-all(bf16[16,72,128]{2,1,0:T(8,128)(2,1)S(1)} %get-tuple-element.39), channel_id=1, replica_groups=mesh['section'=2,'blk'=16] {'blk'}, dimensions={0} | all-to-all | bytes 589824 | tf_op jit(solution)/shard_map/all_to_all | solution.py:417
  67.3 0.0 copy-done.1
  67.3 1.7 %shard_map.96 = (bf16[72,128]{1,0:T(8,128)(2,1)S(1)}, bf16[72,128]{1,0:T(8,128)(2,1)S(1)}, bf16[72,128]{1,0:T(8,128)(2,1)S(1)}, bf16[48,192]{1,0:T(8,128)(2,1)S(1)}) custom-call(bf16[16,72,128]{2,1,0:T(8,128)(2,1)S(1)} %all_to_all.27.blocks, bf16[576,3072]{1,0:T(8,128)(2,1)S(1)} %bitcast.24, bf16[576,3072]{1,0:T(8,128)(2,1)S(1)} %collective-permute-done.4.other, ...), custom_call_target="tpu_custom_call" | custom-call | flops 169869312 | bytes 4718592 | tf_op jit(solution)/shard_map/pallas_call | solution.py:136
  69.0 0.8 collective-permute-start.8
  69.8 3.9 %collective-permute-start.9 = (bf16[72,128]{1,0:T(8,128)(2,1)S(1)}, bf16[72,128]{1,0:T(8,128)(2,1)S(1)}, u32[]{:S(2)}, u32[]{:S(2)}) collective-permute-start(bf16[72,128]{1,0:T(8,128)(2,1)S(1)} %get-tuple-element.42), channel_id=1, source_target_pairs={{0,11},{1,12},{2,13},{3,14},{4,15},{5,0},{6,1},{7,2},{8,3},{9,4},{... | collective-permute-start | bytes 55304 | tf_op jit(solution)/shard_map/ppermute | solution.py:427
  73.7 1.7 %collective-permute-done.8.chunk0 = bf16[72,128]{1,0:T(8,128)(2,1)S(1)} collective-permute-done((bf16[72,128]{1,0:T(8,128)(2,1)S(1)}, bf16[72,128]{1,0:T(8,128)(2,1)S(1)}, u32[]{:S(2)}, u32[]{:S(2)}) %collective-permute-start.8) | collective-permute-done | bytes 18464 | tf_op jit(solution)/shard_map/ppermute | solution.py:427
  75.5 0.0 collective-permute-done.9.chunk2
  75.5 1.3 %shard_map.97 = bf16[16,72,128]{2,1,0:T(8,128)(2,1)S(1)} custom-call(bf16[72,128]{1,0:T(8,128)(2,1)S(1)} %collective-permute-done.8.chunk0, bf16[72,128]{1,0:T(8,128)(2,1)S(1)} %get-tuple-element.41.chunk1, bf16[72,128]{1,0:T(8,128)(2,1)S(1)} %collective-permute-done.9.chunk2, bf16[2,48,384]{2,1,0:T(8,128)(2,1)S(1)} %shard_map.93.old, ...), custom_call_target="tpu_custom_call" | custom-call | flops 3538944 | bytes 300000 | tf_op jit(solution)/shard_map/pallas_call | solution.py:136
  76.8 16.7 %all_to_all.28.blocks = bf16[16,72,128]{2,1,0:T(8,128)(2,1)S(1)} all-to-all(bf16[16,72,128]{2,1,0:T(8,128)(2,1)S(1)} %shard_map.97), channel_id=1, replica_groups=mesh['section'=2,'blk'=16] {'blk'}, dimensions={0} | all-to-all | bytes 589824 | tf_op jit(solution)/shard_map/all_to_all | solution.py:417
  93.5 0.7 shard_map.98
  94.2 9.7 %all_to_all.29.arrived = bf16[32,4,192]{2,1,0:T(4,128)(2,1)S(1)} all-to-all(bf16[32,4,192]{2,1,0:T(4,128)(2,1)S(1)} %shard_map.98), channel_id=1, replica_groups=mesh['section'=2,'blk'=16] {'section','blk'}, dimensions={0} | all-to-all | bytes 98304 | tf_op jit(solution)/shard_map/all_to_all | solution.py:417
  103.9 0.8 shard_map.99
  (1 shorter events, 0.0 us)
Async XLA Ops:
  0.0 1.5 %copy-start = (f32[1,50,3,3072]{3,0,2,1:T(1,128)S(1)}, f32[1,50,3,3072]{3,0,2,1:T(1,128)}, u32[]{:S(2)}) copy-start(f32[1,50,3,3072]{3,0,2,1:T(1,128)} %param.12) | copy-start | bytes 5529604
  0.0 2.0 %collective-permute-start = (bf16[3,2,3072]{2,1,0:T(2,128)(2,1)}, bf16[3,2,3072]{2,1,0:T(2,128)(2,1)S(1)}, u32[]{:S(2)}, u32[]{:S(2)}) collective-permute-start(bf16[3,2,3072]{2,1,0:T(2,128)(2,1)} %bitcast.29), channel_id=1, source_target_pairs={{0,16},{16,0},{1,17},{17,1},{2,18},{18,2},{3,19},{19,3},{4,20},{20... | collective-permute-start | bytes 110600 | tf_op jit(solution)/shard_map/ppermute | solution.py:421
  0.5 1.5 %collective-permute-start.1 = (bf16[3,2,3072]{2,1,0:T(2,128)(2,1)}, bf16[3,2,3072]{2,1,0:T(2,128)(2,1)S(1)}, u32[]{:S(2)}, u32[]{:S(2)}) collective-permute-start(bf16[3,2,3072]{2,1,0:T(2,128)(2,1)} %bitcast.31), channel_id=1, source_target_pairs={{0,16},{16,0},{1,17},{17,1},{2,18},{18,2},{3,19},{19,3},{4,20},{20... | collective-permute-start | bytes 110600 | tf_op jit(solution)/shard_map/ppermute | solution.py:421
  1.5 1.3 %collective-permute-start.2 = (f32[3,1,3072]{2,1,0:T(1,128)S(1)}, f32[3,1,3072]{2,1,0:T(1,128)S(1)}, u32[]{:S(2)}, u32[]{:S(2)}) collective-permute-start(f32[3,1,3072]{2,1,0:T(1,128)S(1)} %dynamic-slice_bitcast_fusion.mod), channel_id=1, source_target_pairs={{0,16},{16,0},{1,17},{17,1},{2,18},{18,2},{3,19},{19,3},{4,20},{20... | collective-permute-start | bytes 110600 | tf_op jit(solution)/shard_map/ppermute | solution.py:421
  2.0 1.4 %collective-permute-start.3 = (s32[1,2,16]{2,1,0:T(2,128)}, s32[1,2,16]{2,1,0:T(2,128)S(1)}, u32[]{:S(2)}, u32[]{:S(2)}) collective-permute-start(s32[1,2,16]{2,1,0:T(2,128)} %fresh.3), channel_id=1, source_target_pairs={{0,16},{16,0},{1,17},{17,1},{2,18},{18,2},{3,19},{19,3},{4,20},{20... | collective-permute-start | bytes 392 | tf_op jit(solution)/shard_map/ppermute | solution.py:421
  3.3 22.6 %collective-permute-start.4 = (bf16[576,3072]{1,0:T(8,128)(2,1)}, bf16[576,3072]{1,0:T(8,128)(2,1)S(1)}, u32[]{:S(2)}, u32[]{:S(2)}) collective-permute-start(bf16[576,3072]{1,0:T(8,128)(2,1)} %bitcast.22), channel_id=1, source_target_pairs={{0,16},{16,0},{1,17},{17,1},{2,18},{18,2},{3,19},{19,3},{4,20},{20... | collective-permute-start | bytes 10616840 | tf_op jit(solution)/shard_map/ppermute | solution.py:421
  3.5 22.4 %collective-permute-start.5 = (bf16[192,3072]{1,0:T(8,128)(2,1)}, bf16[192,3072]{1,0:T(8,128)(2,1)S(1)}, u32[]{:S(2)}, u32[]{:S(2)}) collective-permute-start(bf16[192,3072]{1,0:T(8,128)(2,1)} %bitcast.25), channel_id=1, source_target_pairs={{0,16},{16,0},{1,17},{17,1},{2,18},{18,2},{3,19},{19,3},{4,20},{20... | collective-permute-start | bytes 3538952 | tf_op jit(solution)/shard_map/ppermute | solution.py:421
  25.9 10.6 %copy-start.3 = (s32[1,2,16]{2,1,0:T(2,128)S(1)}, s32[1,2,16]{2,1,0:T(2,128)}, u32[]{:S(2)}) copy-start(s32[1,2,16]{2,1,0:T(2,128)} %fresh.3) | copy-start | bytes 388
  25.9 10.6 %copy-start.4 = (s32[2,16]{1,0:T(2,128)S(1)}, s32[2,16]{1,0:T(2,128)}, u32[]{:S(2)}) copy-start(s32[2,16]{1,0:T(2,128)} %live.3) | copy-start | bytes 388
  29.9 23.9 %copy-start.2 = (bf16[1,3072,192]{1,2,0:T(8,128)(2,1)S(1)}, bf16[1,3072,192]{1,2,0:T(8,128)(2,1)}, u32[]{:S(2)}) copy-start(bf16[1,3072,192]{1,2,0:T(8,128)(2,1)} %param.11) | copy-start | bytes 3538948
  29.9 6.5 %collective-permute-start.6 = (bf16[72,128]{1,0:T(8,128)(2,1)S(1)}, bf16[72,128]{1,0:T(8,128)(2,1)S(1)}, u32[]{:S(2)}, u32[]{:S(2)}) collective-permute-start(bf16[72,128]{1,0:T(8,128)(2,1)S(1)} %get-tuple-element.32), channel_id=1, source_target_pairs={{0,5},{1,6},{2,7},{3,8},{4,9},{5,10},{6,11},{7,12},{8,13},{9,14},{... | collective-permute-start | bytes 55304 | tf_op jit(solution)/shard_map/ppermute | solution.py:427
  31.1 5.4 %collective-permute-start.7 = (bf16[72,128]{1,0:T(8,128)(2,1)S(1)}, bf16[72,128]{1,0:T(8,128)(2,1)S(1)}, u32[]{:S(2)}, u32[]{:S(2)}) collective-permute-start(bf16[72,128]{1,0:T(8,128)(2,1)S(1)} %get-tuple-element.35), channel_id=1, source_target_pairs={{0,11},{1,12},{2,13},{3,14},{4,15},{5,0},{6,1},{7,2},{8,3},{9,4},{... | collective-permute-start | bytes 55304 | tf_op jit(solution)/shard_map/ppermute | solution.py:427
  37.8 29.5 %copy-start.1 = (bf16[1,3072,576]{1,2,0:T(8,128)(2,1)S(1)}, bf16[1,3072,576]{1,2,0:T(8,128)(2,1)}, u32[]{:S(2)}) copy-start(bf16[1,3072,576]{1,2,0:T(8,128)(2,1)} %param.10) | copy-start | bytes 10616836
  69.0 6.5 %collective-permute-start.8 = (bf16[72,128]{1,0:T(8,128)(2,1)S(1)}, bf16[72,128]{1,0:T(8,128)(2,1)S(1)}, u32[]{:S(2)}, u32[]{:S(2)}) collective-permute-start(bf16[72,128]{1,0:T(8,128)(2,1)S(1)} %get-tuple-element.40), channel_id=1, source_target_pairs={{0,5},{1,6},{2,7},{3,8},{4,9},{5,10},{6,11},{7,12},{8,13},{9,14},{... | collective-permute-start | bytes 55304 | tf_op jit(solution)/shard_map/ppermute | solution.py:427
  69.8 5.7 %collective-permute-start.9 = (bf16[72,128]{1,0:T(8,128)(2,1)S(1)}, bf16[72,128]{1,0:T(8,128)(2,1)S(1)}, u32[]{:S(2)}, u32[]{:S(2)}) collective-permute-start(bf16[72,128]{1,0:T(8,128)(2,1)S(1)} %get-tuple-element.42), channel_id=1, source_target_pairs={{0,11},{1,12},{2,13},{3,14},{4,15},{5,0},{6,1},{7,2},{8,3},{9,4},{... | collective-permute-start | bytes 55304 | tf_op jit(solution)/shard_map/ppermute | solution.py:427

commit v2 on v0

--- a/solution.py
+++ b/solution.py
@@ -156,6 +156,14 @@
     return jnp.concatenate([columns[:mid], columns[mid:]], axis=1)
 
 
+def group_of(device, n):
+    return (3 * device + 2 * (device % 2)) % n
+
+
+def owner_of(group, n):
+    return (group - 2 * (group % 2)) * pow(3, -1, n) % n
+
+
 def pack(cols):
     return jnp.concatenate([cols[:, :128], halves(cols[:, 128:])], axis=0)
 
@@ -185,7 +193,7 @@
     tokens = whole.shape[0]
     n = blocks.shape[0]
     for d in range(0, n, 2):
-        even, odd = [group * pow(3, -1, n) % n if by_heads else group for group in (d, d + 1)]
+        even, odd = [owner_of(group, n) if by_heads else group for group in (d, d + 1)]
         even_last, odd_last = blocks[even, tokens:].astype(F32), blocks[odd, tokens:].astype(F32)
         left = lax.broadcasted_iota(jnp.int32, even_last.shape, 1) < HEAD
         first = jnp.where(left, even_last, odd_last)
@@ -240,8 +248,10 @@
 
 
 def chunks_of(columns, chunks):
-    for j, chunk in enumerate(chunks):
-        chunk[...] = pack(columns[:, 192 * j : 192 * j + 192])
+    odd = (lax.axis_index("blk") & 1) == 1
+    first, middle, last = [pack(columns[:, at : at + 192].astype(F32)) for at in range(0, 576, 192)]
+    for chunk, value in zip(chunks, (jnp.where(odd, last, first), middle, jnp.where(odd, first, last))):
+        chunk[...] = value.astype(BF16)
 
 
 def first_projection(arrived, own, other, mod, other_mod, other_out, chunk0, chunk1, chunk2, residual, stream, scales, normed, columns, held, sems):
@@ -283,12 +293,16 @@
 def attention(layer, chunk0, chunk1, chunk2, old, fresh, other_fresh, live, attn):
     n = attn.shape[0]
     me, request = lax.axis_index("blk"), lax.axis_index("section")
-    first = lax.rem(lax.rem(3 * me, n), 3)
+    inverse = pow(3, -1, n)
+    odd = me & 1
+    sign = 1 - 2 * odd
+    sender1 = lax.rem(me - sign * inverse + 2 * n, n)
+    sender2 = lax.rem(me - sign * 2 * inverse + 2 * n, n)
+    kinds = ((3 * me + 2 * odd) // n, (3 * sender1 + 1) // n, (3 * sender2 + 2 - 2 * odd) // n)
     got = [chunk[...].astype(F32) for chunk in (chunk0, chunk1, chunk2)]
 
-    def kind(of):
-        at = lax.rem(first + of, 3)
-        return unpack(jnp.where(at == 0, got[0], jnp.where(at == 1, got[1], got[2])))
+    def kind(which):
+        return unpack(jnp.where(kinds[0] == which, got[0], jnp.where(kinds[1] == which, got[1], got[2])))
 
     queries = kind(0)
     tokens, width = queries.shape
@@ -376,7 +390,7 @@
     own, other = arrays[:2], arrays[2:]
     stale = [jnp.where(first, a, b) for a, b in zip(own, other)] + [jnp.where(first, b, a) for a, b in zip(own, other)]
     for b in range(n):
-        at = columns * (3 * b % n)
+        at = columns * group_of(b, n)
         block = jnp.concatenate([array[:, at : at + columns] for array in stale], axis=1)
         leaving[b, :rows, :] = mine
         for i in range(rows):
@@ -416,10 +430,10 @@
 
 def by_heads(chunks, n):
     inverse = pow(3, -1, n)
-    return [
-        lax.ppermute(chunk, "blk", [(b, (b + inverse * j) % n) for b in range(n)]) if j else chunk
-        for j, chunk in enumerate(chunks)
-    ]
+    kept, middle, other = chunks
+    pairs1 = [(b, (b + (inverse if b % 2 else -inverse)) % n) for b in range(n)]
+    pairs2 = [(b, (b + (-2 * inverse if b % 2 else 2 * inverse)) % n) for b in range(n)]
+    return kept, lax.ppermute(middle, "blk", pairs1), lax.ppermute(other, "blk", pairs2)
 
 
 def per_device(hidden, qkv_weight, out_weight, modulation, timestep, fresh, live, k_stale, v_stale):

time: 99.1 us -> 98.7 us (level)
  starting transfers between devices: 8.36 us -> 5.05 us
  waiting for transfers between devices: 7.62 us -> 10.7 us
    ppermute x4, starting transfers between devices: 6.79 us -> 3.48 us  [the longest x2 1.93 us: by_heads(): lax.ppermute(middle, 'blk', pairs1)]
    ppermute x4, waiting for transfers between devices: 6.34 us -> 9.45 us  [the longest x2 5.8 us: by_heads(): lax.ppermute(middle, 'blk', pairs1)]
where the time goes in v2:
time: 98.7 us; the launch traced here: 98.3 us
  blocking collectives  69.9 us (71%)
  Pallas kernels  11.5 us (12%)
  waiting for transfers between devices  10.7 us (11%)
  starting transfers between devices  5.05 us (5%)
    all_to_all x5, blocking collectives, exchange(): return lax.all_to_all(blocks, axis, split_axis=0, concat_axis=0, tiled=True)  69.9 us
    pallas_call x9, Pallas kernels, call(): pl.pallas_call(body, out_shape=outs, in_specs=specs or [VMEM] * len(args)...  11.5 us
    ppermute x2, waiting for transfers between devices, by_heads(): lax.ppermute(middle, 'blk', pairs1)  5.8 us
    ppermute x2, waiting for transfers between devices, by_heads(): lax.ppermute(other, 'blk', pairs2)  3.65 us
  transfers between devices with their start and end apart: 10, of which 6 were waited for; matrix products, arithmetic and copies ran while one was open for 0% of the time, Pallas kernels for 1%

profile of v2, /device:TPU:0, one launch (start us, length us, event | category | flops | bytes accessed | tf_op | source)
XLA Modules:
  0.0 98.3 jit_solution(1982847612175029980)
XLA Ops:
  0.0 0.0 copy-start
  0.0 0.5 collective-permute-start
  0.5 0.1 collective-permute-start.1
  1.2 0.3 copy-done
  1.5 0.5 collective-permute-start.2
  2.0 0.0 collective-permute-done.other_keys
  2.0 0.0 collective-permute-done.1.other_values
  2.0 0.1 collective-permute-start.3
  2.1 0.8 collective-permute-done.2.other_mod
  2.8 0.5 collective-permute-done.3.other_fresh
  3.3 0.2 collective-permute-start.4
  3.5 0.3 collective-permute-start.5
  3.8 1.1 %shard_map.91 = bf16[16,4,3072]{2,1,0:T(4,128)(2,1)S(1)} custom-call(bf16[3,2,3072]{2,1,0:T(2,128)(2,1)} %bitcast.28, bf16[3,2,3072]{2,1,0:T(2,128)(2,1)} %bitcast.30, bf16[3,2,3072]{2,1,0:T(2,128)(2,1)} %bitcast.32, bf16[3,2,3072]{2,1,0:T(2,128)(2,1)S(1)} %collective-permute-done.other_keys, bf16[3,2,3072]{2,1,0:T(2,128)(2,1)S(1)} %collective-permute-done.1.other_values), custom_call_target="tpu_custom_call" | custom-call | bytes 1000000 | tf_op jit(solution)/shard_map/pallas_call | solution.py:135
  4.9 20.9 %all_to_all.25.arrived = bf16[16,4,3072]{2,1,0:T(4,128)(2,1)S(1)} all-to-all(bf16[16,4,3072]{2,1,0:T(4,128)(2,1)S(1)} %shard_map.91), channel_id=1, replica_groups=mesh['section'=2,'blk'=16] {'blk'}, dimensions={0} | all-to-all | bytes 786432 | tf_op jit(solution)/shard_map/all_to_all | solution.py:424
  25.9 0.0 copy-start.3
  25.9 0.0 copy-start.4
  25.9 0.0 collective-permute-done.5.other_out.other
  25.9 0.0 collective-permute-done.4.other
  25.9 3.7 %shard_map.92 = (bf16[72,128]{1,0:T(8,128)(2,1)S(1)}, bf16[72,128]{1,0:T(8,128)(2,1)S(1)}, bf16[72,128]{1,0:T(8,128)(2,1)S(1)}, bf16[48,192]{1,0:T(8,128)(2,1)S(1)}) custom-call(bf16[16,4,3072]{2,1,0:T(4,128)(2,1)S(1)} %all_to_all.25.arrived, bf16[576,3072]{1,0:T(8,128)(2,1)} %bitcast.23, bf16[576,3072]{1,0:T(8,128)(2,1)S(1)} %collective-permute-done.4.other, ...), custom_call_target="tpu_custom_call" | custom-call | flops 169869312 | bytes 4718592 | tf_op jit(solution)/shard_map/pallas_call | solution.py:135
  29.6 0.0 copy-start.2
  29.6 1.2 %collective-permute-start.6 = (bf16[72,128]{1,0:T(8,128)(2,1)S(1)}, bf16[72,128]{1,0:T(8,128)(2,1)S(1)}, u32[]{:S(2)}, u32[]{:S(2)}) collective-permute-start(bf16[72,128]{1,0:T(8,128)(2,1)S(1)} %get-tuple-element.34), channel_id=1, source_target_pairs={{0,5},{1,12},{2,7},{3,14},{4,9},{5,0},{6,11},{7,2},{8,13},{9,4},{1... | collective-permute-start | bytes 55304 | tf_op jit(solution)/shard_map/ppermute | solution.py:436
  30.8 0.3 collective-permute-start.7
  31.1 0.1 shard_map.93.old
  31.2 3.1 %collective-permute-done.6.chunk1 = bf16[72,128]{1,0:T(8,128)(2,1)S(1)} collective-permute-done((bf16[72,128]{1,0:T(8,128)(2,1)S(1)}, bf16[72,128]{1,0:T(8,128)(2,1)S(1)}, u32[]{:S(2)}, u32[]{:S(2)}) %collective-permute-start.6) | collective-permute-done | bytes 18464 | tf_op jit(solution)/shard_map/ppermute | solution.py:436
  34.3 2.0 %collective-permute-done.7.chunk2 = bf16[72,128]{1,0:T(8,128)(2,1)S(1)} collective-permute-done((bf16[72,128]{1,0:T(8,128)(2,1)S(1)}, bf16[72,128]{1,0:T(8,128)(2,1)S(1)}, u32[]{:S(2)}, u32[]{:S(2)}) %collective-permute-start.7) | collective-permute-done | bytes 18464 | tf_op jit(solution)/shard_map/ppermute | solution.py:436
  36.3 0.0 copy-done.3
  36.3 0.0 copy-done.4
  36.3 1.3 %shard_map.94 = bf16[16,72,128]{2,1,0:T(8,128)(2,1)S(1)} custom-call(bf16[72,128]{1,0:T(8,128)(2,1)S(1)} %get-tuple-element.32.chunk0, bf16[72,128]{1,0:T(8,128)(2,1)S(1)} %collective-permute-done.6.chunk1, bf16[72,128]{1,0:T(8,128)(2,1)S(1)} %collective-permute-done.7.chunk2, bf16[2,48,384]{2,1,0:T(8,128)(2,1)S(1)} %shard_map.93.old, ...), custom_call_target="tpu_custom_call" | custom-call | flops 3538944 | bytes 300000 | tf_op jit(solution)/shard_map/pallas_call | solution.py:135
  37.6 0.0 copy-start.1
  37.6 12.9 %all_to_all.26.blocks = bf16[16,72,128]{2,1,0:T(8,128)(2,1)S(1)} all-to-all(bf16[16,72,128]{2,1,0:T(8,128)(2,1)S(1)} %shard_map.94), channel_id=1, replica_groups=mesh['section'=2,'blk'=16] {'blk'}, dimensions={0} | all-to-all | bytes 589824 | tf_op jit(solution)/shard_map/all_to_all | solution.py:424
  50.6 0.0 copy-done.2
  50.6 0.9 shard_map.95
  51.5 12.4 %all_to_all.27.blocks = bf16[16,72,128]{2,1,0:T(8,128)(2,1)S(1)} all-to-all(bf16[16,72,128]{2,1,0:T(8,128)(2,1)S(1)} %get-tuple-element.39), channel_id=1, replica_groups=mesh['section'=2,'blk'=16] {'blk'}, dimensions={0} | all-to-all | bytes 589824 | tf_op jit(solution)/shard_map/all_to_all | solution.py:424
  63.8 0.0 copy-done.1
  63.8 1.7 %shard_map.96 = (bf16[72,128]{1,0:T(8,128)(2,1)S(1)}, bf16[72,128]{1,0:T(8,128)(2,1)S(1)}, bf16[72,128]{1,0:T(8,128)(2,1)S(1)}, bf16[48,192]{1,0:T(8,128)(2,1)S(1)}) custom-call(bf16[16,72,128]{2,1,0:T(8,128)(2,1)S(1)} %all_to_all.27.blocks, bf16[576,3072]{1,0:T(8,128)(2,1)S(1)} %bitcast.24, bf16[576,3072]{1,0:T(8,128)(2,1)S(1)} %collective-permute-done.4.other, ...), custom_call_target="tpu_custom_call" | custom-call | flops 169869312 | bytes 4718592 | tf_op jit(solution)/shard_map/pallas_call | solution.py:135
  65.5 0.8 collective-permute-start.8
  66.3 1.2 %collective-permute-start.9 = (bf16[72,128]{1,0:T(8,128)(2,1)S(1)}, bf16[72,128]{1,0:T(8,128)(2,1)S(1)}, u32[]{:S(2)}, u32[]{:S(2)}) collective-permute-start(bf16[72,128]{1,0:T(8,128)(2,1)S(1)} %get-tuple-element.42), channel_id=1, source_target_pairs={{0,6},{1,11},{2,8},{3,13},{4,10},{5,15},{6,12},{7,1},{8,14},{9,3},... | collective-permute-start | bytes 55304 | tf_op jit(solution)/shard_map/ppermute | solution.py:436
  67.5 2.7 %collective-permute-done.8.chunk1 = bf16[72,128]{1,0:T(8,128)(2,1)S(1)} collective-permute-done((bf16[72,128]{1,0:T(8,128)(2,1)S(1)}, bf16[72,128]{1,0:T(8,128)(2,1)S(1)}, u32[]{:S(2)}, u32[]{:S(2)}) %collective-permute-start.8) | collective-permute-done | bytes 18464 | tf_op jit(solution)/shard_map/ppermute | solution.py:436
  70.2 1.7 %collective-permute-done.9.chunk2 = bf16[72,128]{1,0:T(8,128)(2,1)S(1)} collective-permute-done((bf16[72,128]{1,0:T(8,128)(2,1)S(1)}, bf16[72,128]{1,0:T(8,128)(2,1)S(1)}, u32[]{:S(2)}, u32[]{:S(2)}) %collective-permute-start.9) | collective-permute-done | bytes 18464 | tf_op jit(solution)/shard_map/ppermute | solution.py:436
  71.9 1.3 %shard_map.97 = bf16[16,72,128]{2,1,0:T(8,128)(2,1)S(1)} custom-call(bf16[72,128]{1,0:T(8,128)(2,1)S(1)} %get-tuple-element.40.chunk0, bf16[72,128]{1,0:T(8,128)(2,1)S(1)} %collective-permute-done.8.chunk1, bf16[72,128]{1,0:T(8,128)(2,1)S(1)} %collective-permute-done.9.chunk2, bf16[2,48,384]{2,1,0:T(8,128)(2,1)S(1)} %shard_map.93.old, ...), custom_call_target="tpu_custom_call" | custom-call | flops 3538944 | bytes 300000 | tf_op jit(solution)/shard_map/pallas_call | solution.py:135
  73.2 13.9 %all_to_all.28.blocks = bf16[16,72,128]{2,1,0:T(8,128)(2,1)S(1)} all-to-all(bf16[16,72,128]{2,1,0:T(8,128)(2,1)S(1)} %shard_map.97), channel_id=1, replica_groups=mesh['section'=2,'blk'=16] {'blk'}, dimensions={0} | all-to-all | bytes 589824 | tf_op jit(solution)/shard_map/all_to_all | solution.py:424
  87.1 0.7 shard_map.98
  87.8 9.7 %all_to_all.29.arrived = bf16[32,4,192]{2,1,0:T(4,128)(2,1)S(1)} all-to-all(bf16[32,4,192]{2,1,0:T(4,128)(2,1)S(1)} %shard_map.98), channel_id=1, replica_groups=mesh['section'=2,'blk'=16] {'section','blk'}, dimensions={0} | all-to-all | bytes 98304 | tf_op jit(solution)/shard_map/all_to_all | solution.py:424
  97.5 0.8 shard_map.99
  (1 shorter events, 0.0 us)
Async XLA Ops:
  0.0 1.5 %copy-start = (f32[1,50,3,3072]{3,0,2,1:T(1,128)S(1)}, f32[1,50,3,3072]{3,0,2,1:T(1,128)}, u32[]{:S(2)}) copy-start(f32[1,50,3,3072]{3,0,2,1:T(1,128)} %param.12) | copy-start | bytes 5529604
  0.0 2.0 %collective-permute-start = (bf16[3,2,3072]{2,1,0:T(2,128)(2,1)}, bf16[3,2,3072]{2,1,0:T(2,128)(2,1)S(1)}, u32[]{:S(2)}, u32[]{:S(2)}) collective-permute-start(bf16[3,2,3072]{2,1,0:T(2,128)(2,1)} %bitcast.29), channel_id=1, source_target_pairs={{0,16},{16,0},{1,17},{17,1},{2,18},{18,2},{3,19},{19,3},{4,20},{20... | collective-permute-start | bytes 110600 | tf_op jit(solution)/shard_map/ppermute | solution.py:428
  0.5 1.5 %collective-permute-start.1 = (bf16[3,2,3072]{2,1,0:T(2,128)(2,1)}, bf16[3,2,3072]{2,1,0:T(2,128)(2,1)S(1)}, u32[]{:S(2)}, u32[]{:S(2)}) collective-permute-start(bf16[3,2,3072]{2,1,0:T(2,128)(2,1)} %bitcast.31), channel_id=1, source_target_pairs={{0,16},{16,0},{1,17},{17,1},{2,18},{18,2},{3,19},{19,3},{4,20},{20... | collective-permute-start | bytes 110600 | tf_op jit(solution)/shard_map/ppermute | solution.py:428
  1.5 1.3 %collective-permute-start.2 = (f32[3,1,3072]{2,1,0:T(1,128)S(1)}, f32[3,1,3072]{2,1,0:T(1,128)S(1)}, u32[]{:S(2)}, u32[]{:S(2)}) collective-permute-start(f32[3,1,3072]{2,1,0:T(1,128)S(1)} %dynamic-slice_bitcast_fusion.mod), channel_id=1, source_target_pairs={{0,16},{16,0},{1,17},{17,1},{2,18},{18,2},{3,19},{19,3},{4,20},{20... | collective-permute-start | bytes 110600 | tf_op jit(solution)/shard_map/ppermute | solution.py:428
  2.0 1.4 %collective-permute-start.3 = (s32[1,2,16]{2,1,0:T(2,128)}, s32[1,2,16]{2,1,0:T(2,128)S(1)}, u32[]{:S(2)}, u32[]{:S(2)}) collective-permute-start(s32[1,2,16]{2,1,0:T(2,128)} %fresh.3), channel_id=1, source_target_pairs={{0,16},{16,0},{1,17},{17,1},{2,18},{18,2},{3,19},{19,3},{4,20},{20... | collective-permute-start | bytes 392 | tf_op jit(solution)/shard_map/ppermute | solution.py:428
  3.3 22.6 %collective-permute-start.4 = (bf16[576,3072]{1,0:T(8,128)(2,1)}, bf16[576,3072]{1,0:T(8,128)(2,1)S(1)}, u32[]{:S(2)}, u32[]{:S(2)}) collective-permute-start(bf16[576,3072]{1,0:T(8,128)(2,1)} %bitcast.22), channel_id=1, source_target_pairs={{0,16},{16,0},{1,17},{17,1},{2,18},{18,2},{3,19},{19,3},{4,20},{20... | collective-permute-start | bytes 10616840 | tf_op jit(solution)/shard_map/ppermute | solution.py:428
  3.5 22.4 %collective-permute-start.5 = (bf16[192,3072]{1,0:T(8,128)(2,1)}, bf16[192,3072]{1,0:T(8,128)(2,1)S(1)}, u32[]{:S(2)}, u32[]{:S(2)}) collective-permute-start(bf16[192,3072]{1,0:T(8,128)(2,1)} %bitcast.25), channel_id=1, source_target_pairs={{0,16},{16,0},{1,17},{17,1},{2,18},{18,2},{3,19},{19,3},{4,20},{20... | collective-permute-start | bytes 3538952 | tf_op jit(solution)/shard_map/ppermute | solution.py:428
  25.9 10.5 %copy-start.3 = (s32[1,2,16]{2,1,0:T(2,128)S(1)}, s32[1,2,16]{2,1,0:T(2,128)}, u32[]{:S(2)}) copy-start(s32[1,2,16]{2,1,0:T(2,128)} %fresh.3) | copy-start | bytes 388
  25.9 10.5 %copy-start.4 = (s32[2,16]{1,0:T(2,128)S(1)}, s32[2,16]{1,0:T(2,128)}, u32[]{:S(2)}) copy-start(s32[2,16]{1,0:T(2,128)} %live.3) | copy-start | bytes 388
  29.6 21.0 %copy-start.2 = (bf16[1,3072,192]{1,2,0:T(8,128)(2,1)S(1)}, bf16[1,3072,192]{1,2,0:T(8,128)(2,1)}, u32[]{:S(2)}) copy-start(bf16[1,3072,192]{1,2,0:T(8,128)(2,1)} %param.11) | copy-start | bytes 3538948
  29.6 4.7 %collective-permute-start.6 = (bf16[72,128]{1,0:T(8,128)(2,1)S(1)}, bf16[72,128]{1,0:T(8,128)(2,1)S(1)}, u32[]{:S(2)}, u32[]{:S(2)}) collective-permute-start(bf16[72,128]{1,0:T(8,128)(2,1)S(1)} %get-tuple-element.34), channel_id=1, source_target_pairs={{0,5},{1,12},{2,7},{3,14},{4,9},{5,0},{6,11},{7,2},{8,13},{9,4},{1... | collective-permute-start | bytes 55304 | tf_op jit(solution)/shard_map/ppermute | solution.py:436
  30.8 5.6 %collective-permute-start.7 = (bf16[72,128]{1,0:T(8,128)(2,1)S(1)}, bf16[72,128]{1,0:T(8,128)(2,1)S(1)}, u32[]{:S(2)}, u32[]{:S(2)}) collective-permute-start(bf16[72,128]{1,0:T(8,128)(2,1)S(1)} %get-tuple-element.35), channel_id=1, source_target_pairs={{0,6},{1,11},{2,8},{3,13},{4,10},{5,15},{6,12},{7,1},{8,14},{9,3},... | collective-permute-start | bytes 55304 | tf_op jit(solution)/shard_map/ppermute | solution.py:436
  37.6 26.2 %copy-start.1 = (bf16[1,3072,576]{1,2,0:T(8,128)(2,1)S(1)}, bf16[1,3072,576]{1,2,0:T(8,128)(2,1)}, u32[]{:S(2)}) copy-start(bf16[1,3072,576]{1,2,0:T(8,128)(2,1)} %param.10) | copy-start | bytes 10616836
  65.5 4.7 %collective-permute-start.8 = (bf16[72,128]{1,0:T(8,128)(2,1)S(1)}, bf16[72,128]{1,0:T(8,128)(2,1)S(1)}, u32[]{:S(2)}, u32[]{:S(2)}) collective-permute-start(bf16[72,128]{1,0:T(8,128)(2,1)S(1)} %get-tuple-element.41), channel_id=1, source_target_pairs={{0,5},{1,12},{2,7},{3,14},{4,9},{5,0},{6,11},{7,2},{8,13},{9,4},{1... | collective-permute-start | bytes 55304 | tf_op jit(solution)/shard_map/ppermute | solution.py:436
  66.3 5.6 %collective-permute-start.9 = (bf16[72,128]{1,0:T(8,128)(2,1)S(1)}, bf16[72,128]{1,0:T(8,128)(2,1)S(1)}, u32[]{:S(2)}, u32[]{:S(2)}) collective-permute-start(bf16[72,128]{1,0:T(8,128)(2,1)S(1)} %get-tuple-element.42), channel_id=1, source_target_pairs={{0,6},{1,11},{2,8},{3,13},{4,10},{5,15},{6,12},{7,1},{8,14},{9,3},... | collective-permute-start | bytes 55304 | tf_op jit(solution)/shard_map/ppermute | solution.py:436

commit v3 on v2

--- a/solution.py
+++ b/solution.py
@@ -241,9 +241,8 @@
     pl.when(jnp.logical_not(held))(lambda: into(other))
 
 
-def normalise(layer, stream, mod, other_mod, normed, residual, scales):
-    scales[...] = own_or_other(layer, mod[...], other_mod[...])
-    norm_into(stream, scales, normed)
+def normalise(stream, mod, normed, residual):
+    norm_into(stream, mod, normed)
     residual[...] = own_columns(stream, slice(None), lax.axis_index("blk")).astype(BF16)
 
 
@@ -254,7 +253,7 @@
         chunk[...] = value.astype(BF16)
 
 
-def first_projection(arrived, own, other, mod, other_mod, other_out, chunk0, chunk1, chunk2, residual, stream, scales, normed, columns, held, sems):
+def first_projection(arrived, own, other, mod, other_out, chunk0, chunk1, chunk2, residual, stream, normed, columns, held, sems):
     holds = lax.axis_index("section") == 0
     parts = sems.shape[0]
     size = held.shape[0] // parts
@@ -272,7 +271,7 @@
     rows = stream.shape[0] // n
     for b in range(n):
         stream[rows * b : rows * b + rows, :] = arrived[b, :rows, :].astype(F32)
-    normalise(0, stream, mod, other_mod, normed, residual, scales)
+    normalise(stream, mod, normed, residual)
 
     @pl.when(holds)
     def _():
@@ -283,9 +282,9 @@
     chunks_of(columns, (chunk0, chunk1, chunk2))
 
 
-def next_projection(blocks, own, other, mod, other_mod, chunk0, chunk1, chunk2, residual, stream, scales, normed, columns):
+def next_projection(blocks, own, other, mod, chunk0, chunk1, chunk2, residual, stream, normed, columns):
     assemble(blocks, stream)
-    normalise(1, stream, mod, other_mod, normed, residual, scales)
+    normalise(stream, mod, normed, residual)
     dot_into(1, normed, own, other, columns)
     chunks_of(columns, (chunk0, chunk1, chunk2))
 
@@ -337,29 +336,23 @@
         attn[d] = packed
 
 
-def layer_columns(layer, blocks, own, other, mod, other_mod, residual, whole, mixed):
-    me = lax.axis_index("blk")
+def layer_columns(layer, blocks, own, other, mod, residual, whole, mixed):
     assemble(blocks, whole, by_heads=True)
     dot_into(layer, whole, own, other, mixed)
-    gates = own_or_other(layer, mod[2], other_mod[2])
-    pairs = [gates[:, at : at + 384] for at in range(0, gates.shape[1], 384)]
-    pair = pairs[0]
-    for i, other_pair in enumerate(pairs):
-        pair = jnp.where(me // 2 == i, other_pair, pair)
-    gate = jnp.where((me & 1) == 1, pair[:, 192:], pair[:, :192])
+    gate = own_columns(mod.at[2], slice(None), lax.axis_index("blk"))
     return (residual[...].astype(F32) + gate * mixed[...].astype(F32)).astype(BF16).astype(F32)
 
 
-def first_output(blocks, own, other, mod, other_mod, residual, copies, kept, *scratch):
-    columns = layer_columns(0, blocks, own, other, mod, other_mod, residual, *scratch)
+def first_output(blocks, own, other, mod, residual, copies, kept, *scratch):
+    columns = layer_columns(0, blocks, own, other, mod, residual, *scratch)
     packed = pack_by_parity(columns, (lax.axis_index("blk") & 1) == 1).astype(BF16)
     for d in range(copies.shape[0]):
         copies[d] = packed
     kept[...] = columns
 
 
-def last_output(blocks, own, other, mod, other_mod, residual, kept, by_token, columns, *scratch):
-    columns[...] = layer_columns(1, blocks, own, other, mod, other_mod, residual, *scratch)
+def last_output(blocks, own, other, mod, residual, kept, by_token, columns, *scratch):
+    columns[...] = layer_columns(1, blocks, own, other, mod, residual, *scratch)
     n = by_token.shape[0] // 2
     rows = columns.shape[0] // n
     for layer, outs in enumerate((kept, columns)):
@@ -367,7 +360,7 @@
             by_token[layer * n + b, :rows, :] = outs[rows * b : rows * b + rows, :].astype(BF16)
 
 
-def first_exchange(hidden, old_keys, old_values, other_keys, other_values, leaving, held, sems):
+def first_exchange(hidden, old_keys, old_values, other_keys, other_values, mod, other_mod, leaving, first_mod, held, sems):
     copies = [
         pltpu.make_async_copy(ref, held.at[i], sems.at[i])
         for i, ref in enumerate((hidden, old_keys, old_values, other_keys, other_values))
@@ -378,6 +371,7 @@
     n = leaving.shape[0]
     columns = width // n
     first = lax.axis_index("section") == 0
+    first_mod[...] = own_or_other(0, mod[...], other_mod[...])
     for copy in copies:
         copy.wait()
 
@@ -397,7 +391,7 @@
             leaving[b, rows : rows + 1, i * 4 * columns : (i + 1) * 4 * columns] = block[i : i + 1].astype(BF16)
 
 
-def stale_by_token(arrived, old, rows):
+def stale_by_token(arrived, mod, other_mod, old, second_mod, rows):
     n = arrived.shape[0]
     per = rows.shape[1] // n
     wide = rows.shape[2]
@@ -408,6 +402,7 @@
                 at = (i * 2 + layer) * wide
                 rows[layer, per * b + i : per * b + i + 1, :] = flat[:, at : at + wide]
     old[...] = rows[...].astype(BF16)
+    second_mod[...] = own_or_other(1, mod[...], other_mod[...])
 
 
 def to_rows(arrived, out, rows):
@@ -472,15 +467,16 @@
     flags = (fresh, other_fresh)
     other_qkv, other_out = swap_sections(sent_qkv), swap_sections(sent_out)
     out = (own_out, other_out)
-    leaving = call(
+    leaving, layer_mod = call(
         first_exchange,
-        shape((n, 4, width), BF16),
+        [shape((n, 4, width), BF16), shape(mod.shape, F32)],
         [pltpu.VMEM((5, rows, reqs, width), BF16), pltpu.SemaphoreType.DMA((5,))],
         (0, 1000000),
         *(pinned(array) for array in (jnp.transpose(hidden, (1, 0, 2)), old_keys, old_values)),
         other_keys,
         other_values,
-        specs=[HBM] * 3 + [ANY] * 2,
+        *mods,
+        specs=[HBM] * 3 + [ANY] * 2 + [VMEM] * 2,
     )
     arrived = exchange(leaving, "blk")
 
@@ -491,24 +487,24 @@
             [packed, packed, packed, cols],
             [
                 pltpu.VMEM((tokens, width), F32),
-                pltpu.VMEM(mod.shape, F32),
                 pltpu.VMEM((tokens, width), BF16),
                 pltpu.VMEM((tokens, 3 * columns), BF16),
             ]
-            + ([] if layer else [pltpu.VMEM(own_qkv.shape, BF16), pltpu.SemaphoreType.DMA((36,))]),
+            + ([] if layer else [pltpu.VMEM(own_qkv.shape, BF16), pltpu.SemaphoreType.DMA((12,))]),
             (2 * tokens * width * 3 * columns, 8 * width * columns),
             blocks,
-            *((own_qkv, other_qkv, *mods) if layer else (pinned(own_qkv), other_qkv, *mods, other_out)),
-            **({} if layer else {"specs": [VMEM, HBM, VMEM, VMEM, VMEM, ANY]}),
+            *((own_qkv, other_qkv, layer_mod) if layer else (pinned(own_qkv), other_qkv, layer_mod, other_out)),
+            **({} if layer else {"specs": [VMEM, HBM, VMEM, VMEM, ANY]}),
         )
         if layer == 0:
             arrived, chunks[1] = lax.optimization_barrier((arrived, chunks[1]))
-            old = call(
+            old, next_mod = call(
                 stale_by_token,
-                shape((2, tokens, 2 * columns), BF16),
+                [shape((2, tokens, 2 * columns), BF16), shape(mod.shape, F32)],
                 [pltpu.VMEM((2, tokens, 2 * columns), F32)],
                 (0, 200000),
                 arrived,
+                *mods,
             )
         attn = call(
             functools.partial(attention, layer),
@@ -521,12 +517,12 @@
             live,
             specs=[VMEM] * 4 + [SMEM] * 3,
         )
-        args = (exchange(attn, "blk"), *out, *mods, residual)
+        args = (exchange(attn, "blk"), *out, layer_mod, residual)
         cost = (2 * tokens * width * columns, 4 * width * columns)
         held = [pltpu.VMEM((tokens, width), BF16), pltpu.VMEM((tokens, columns), BF16)]
         if layer == 0:
             leaving, kept = call(first_output, [copies, shape((tokens, columns), F32)], held, cost, *args)
-            blocks = exchange(leaving, "blk")
+            blocks, layer_mod = exchange(leaving, "blk"), next_mod
         else:
             leaving = call(
                 last_output,

time: 98.7 us -> 98.6 us (level)
  no operation moved by 1% of the time
where the time goes in v3:
time: 98.6 us; the launch traced here: 98.2 us
  blocking collectives  70 us (71%)
  Pallas kernels  11.4 us (12%)
  waiting for transfers between devices  10.8 us (11%)
  starting transfers between devices  5 us (5%)
    all_to_all x5, blocking collectives, exchange(): return lax.all_to_all(blocks, axis, split_axis=0, concat_axis=0, tiled=True)  70 us
    pallas_call x9, Pallas kernels, call(): pl.pallas_call(body, out_shape=outs, in_specs=specs or [VMEM] * len(args)...  11.4 us
    ppermute x2, waiting for transfers between devices, by_heads(): lax.ppermute(middle, 'blk', pairs1)  5.85 us
    ppermute x2, waiting for transfers between devices, by_heads(): lax.ppermute(other, 'blk', pairs2)  3.65 us
  transfers between devices with their start and end apart: 10, of which 6 were waited for; matrix products, arithmetic and copies ran while one was open for 0% of the time, Pallas kernels for 1%

profile of v3, /device:TPU:0, one launch (start us, length us, event | category | flops | bytes accessed | tf_op | source)
XLA Modules:
  0.0 98.2 jit_solution(10660252867642826633)
XLA Ops:
  0.0 0.0 copy-start
  0.0 0.5 collective-permute-start
  0.5 0.1 collective-permute-start.1
  1.2 0.3 copy-done
  1.5 0.5 collective-permute-start.2
  2.0 0.0 collective-permute-done.other_keys
  2.0 0.0 collective-permute-done.1.other_values
  2.0 0.1 collective-permute-start.3
  2.1 0.8 collective-permute-done.2.other_mod
  2.8 0.5 collective-permute-done.3.other_fresh
  3.3 0.2 collective-permute-start.4
  3.5 0.3 collective-permute-start.5
  3.8 1.1 %shard_map.91 = (bf16[16,4,3072]{2,1,0:T(4,128)(2,1)S(1)}, f32[3,1,3072]{2,1,0:T(1,128)S(1)}) custom-call(bf16[3,2,3072]{2,1,0:T(2,128)(2,1)} %bitcast.28, bf16[3,2,3072]{2,1,0:T(2,128)(2,1)} %bitcast.30, bf16[3,2,3072]{2,1,0:T(2,128)(2,1)} %bitcast.32, bf16[3,2,3072]{2,1,0:T(2,128)(2,1)S(1)} %collective-permute-done.other_keys, ...), custom_call_target="tpu_custom_call" | custom-call | bytes 1000000 | tf_op jit(solution)/shard_map/pallas_call | solution.py:135
  4.9 20.9 %all_to_all.25.arrived = bf16[16,4,3072]{2,1,0:T(4,128)(2,1)S(1)} all-to-all(bf16[16,4,3072]{2,1,0:T(4,128)(2,1)S(1)} %get-tuple-element.34), channel_id=1, replica_groups=mesh['section'=2,'blk'=16] {'blk'}, dimensions={0} | all-to-all | bytes 786432 | tf_op jit(solution)/shard_map/all_to_all | solution.py:419
  25.9 0.0 collective-permute-done.5.other_out.other
  25.9 0.0 collective-permute-done.4.other
  25.9 0.0 copy-start.3
  25.9 0.0 copy-start.4
  25.9 3.6 %shard_map.92 = (bf16[72,128]{1,0:T(8,128)(2,1)S(1)}, bf16[72,128]{1,0:T(8,128)(2,1)S(1)}, bf16[72,128]{1,0:T(8,128)(2,1)S(1)}, bf16[48,192]{1,0:T(8,128)(2,1)S(1)}) custom-call(bf16[16,4,3072]{2,1,0:T(4,128)(2,1)S(1)} %all_to_all.25.arrived, bf16[576,3072]{1,0:T(8,128)(2,1)} %bitcast.23, bf16[576,3072]{1,0:T(8,128)(2,1)S(1)} %collective-permute-done.4.other, ...), custom_call_target="tpu_custom_call" | custom-call | flops 169869312 | bytes 4718592 | tf_op jit(solution)/shard_map/pallas_call | solution.py:135
  29.4 0.0 copy-start.2
  29.5 1.2 %collective-permute-start.6 = (bf16[72,128]{1,0:T(8,128)(2,1)S(1)}, bf16[72,128]{1,0:T(8,128)(2,1)S(1)}, u32[]{:S(2)}, u32[]{:S(2)}) collective-permute-start(bf16[72,128]{1,0:T(8,128)(2,1)S(1)} %get-tuple-element.40), channel_id=1, source_target_pairs={{0,5},{1,12},{2,7},{3,14},{4,9},{5,0},{6,11},{7,2},{8,13},{9,4},{1... | collective-permute-start | bytes 55304 | tf_op jit(solution)/shard_map/ppermute | solution.py:431
  30.6 0.3 collective-permute-start.7
  30.9 0.1 shard_map.93
  31.1 3.1 %collective-permute-done.6.chunk1 = bf16[72,128]{1,0:T(8,128)(2,1)S(1)} collective-permute-done((bf16[72,128]{1,0:T(8,128)(2,1)S(1)}, bf16[72,128]{1,0:T(8,128)(2,1)S(1)}, u32[]{:S(2)}, u32[]{:S(2)}) %collective-permute-start.6) | collective-permute-done | bytes 18464 | tf_op jit(solution)/shard_map/ppermute | solution.py:431
  34.2 2.0 %collective-permute-done.7.chunk2 = bf16[72,128]{1,0:T(8,128)(2,1)S(1)} collective-permute-done((bf16[72,128]{1,0:T(8,128)(2,1)S(1)}, bf16[72,128]{1,0:T(8,128)(2,1)S(1)}, u32[]{:S(2)}, u32[]{:S(2)}) %collective-permute-start.7) | collective-permute-done | bytes 18464 | tf_op jit(solution)/shard_map/ppermute | solution.py:431
  36.2 0.0 copy-done.3
  36.2 0.0 copy-done.4
  36.2 1.3 %shard_map.94 = bf16[16,72,128]{2,1,0:T(8,128)(2,1)S(1)} custom-call(bf16[72,128]{1,0:T(8,128)(2,1)S(1)} %get-tuple-element.38.chunk0, bf16[72,128]{1,0:T(8,128)(2,1)S(1)} %collective-permute-done.6.chunk1, bf16[72,128]{1,0:T(8,128)(2,1)S(1)} %collective-permute-done.7.chunk2, bf16[2,48,384]{2,1,0:T(8,128)(2,1)S(1)} %get-tuple-element.43.old, ...), custom_call_target="tpu_custom_call" | custom-call | flops 3538944 | bytes 300000 | tf_op jit(solution)/shard_map/pallas_call | solution.py:135
  37.5 0.0 copy-start.1
  37.5 12.9 %all_to_all.26.blocks = bf16[16,72,128]{2,1,0:T(8,128)(2,1)S(1)} all-to-all(bf16[16,72,128]{2,1,0:T(8,128)(2,1)S(1)} %shard_map.94), channel_id=1, replica_groups=mesh['section'=2,'blk'=16] {'blk'}, dimensions={0} | all-to-all | bytes 589824 | tf_op jit(solution)/shard_map/all_to_all | solution.py:419
  50.4 0.0 copy-done.2
  50.4 0.9 shard_map.95
  51.3 12.4 %all_to_all.27.blocks = bf16[16,72,128]{2,1,0:T(8,128)(2,1)S(1)} all-to-all(bf16[16,72,128]{2,1,0:T(8,128)(2,1)S(1)} %get-tuple-element.46), channel_id=1, replica_groups=mesh['section'=2,'blk'=16] {'blk'}, dimensions={0} | all-to-all | bytes 589824 | tf_op jit(solution)/shard_map/all_to_all | solution.py:419
  63.7 0.0 copy-done.1
  63.7 1.7 %shard_map.96 = (bf16[72,128]{1,0:T(8,128)(2,1)S(1)}, bf16[72,128]{1,0:T(8,128)(2,1)S(1)}, bf16[72,128]{1,0:T(8,128)(2,1)S(1)}, bf16[48,192]{1,0:T(8,128)(2,1)S(1)}) custom-call(bf16[16,72,128]{2,1,0:T(8,128)(2,1)S(1)} %all_to_all.27.blocks, bf16[576,3072]{1,0:T(8,128)(2,1)S(1)} %bitcast.24, bf16[576,3072]{1,0:T(8,128)(2,1)S(1)} %collective-permute-done.4.other, ...), custom_call_target="tpu_custom_call" | custom-call | flops 169869312 | bytes 4718592 | tf_op jit(solution)/shard_map/pallas_call | solution.py:135
  65.4 0.8 collective-permute-start.8
  66.1 1.2 %collective-permute-start.9 = (bf16[72,128]{1,0:T(8,128)(2,1)S(1)}, bf16[72,128]{1,0:T(8,128)(2,1)S(1)}, u32[]{:S(2)}, u32[]{:S(2)}) collective-permute-start(bf16[72,128]{1,0:T(8,128)(2,1)S(1)} %get-tuple-element.50), channel_id=1, source_target_pairs={{0,6},{1,11},{2,8},{3,13},{4,10},{5,15},{6,12},{7,1},{8,14},{9,3},... | collective-permute-start | bytes 55304 | tf_op jit(solution)/shard_map/ppermute | solution.py:431
  67.3 2.7 %collective-permute-done.8.chunk1 = bf16[72,128]{1,0:T(8,128)(2,1)S(1)} collective-permute-done((bf16[72,128]{1,0:T(8,128)(2,1)S(1)}, bf16[72,128]{1,0:T(8,128)(2,1)S(1)}, u32[]{:S(2)}, u32[]{:S(2)}) %collective-permute-start.8) | collective-permute-done | bytes 18464 | tf_op jit(solution)/shard_map/ppermute | solution.py:431
  70.0 1.7 %collective-permute-done.9.chunk2 = bf16[72,128]{1,0:T(8,128)(2,1)S(1)} collective-permute-done((bf16[72,128]{1,0:T(8,128)(2,1)S(1)}, bf16[72,128]{1,0:T(8,128)(2,1)S(1)}, u32[]{:S(2)}, u32[]{:S(2)}) %collective-permute-start.9) | collective-permute-done | bytes 18464 | tf_op jit(solution)/shard_map/ppermute | solution.py:431
  71.7 1.3 %shard_map.97 = bf16[16,72,128]{2,1,0:T(8,128)(2,1)S(1)} custom-call(bf16[72,128]{1,0:T(8,128)(2,1)S(1)} %get-tuple-element.48.chunk0, bf16[72,128]{1,0:T(8,128)(2,1)S(1)} %collective-permute-done.8.chunk1, bf16[72,128]{1,0:T(8,128)(2,1)S(1)} %collective-permute-done.9.chunk2, bf16[2,48,384]{2,1,0:T(8,128)(2,1)S(1)} %get-tuple-element.43.old, ...), custom_call_target="tpu_custom_call" | custom-call | flops 3538944 | bytes 300000 | tf_op jit(solution)/shard_map/pallas_call | solution.py:135
  73.0 14.0 %all_to_all.28.blocks = bf16[16,72,128]{2,1,0:T(8,128)(2,1)S(1)} all-to-all(bf16[16,72,128]{2,1,0:T(8,128)(2,1)S(1)} %shard_map.97), channel_id=1, replica_groups=mesh['section'=2,'blk'=16] {'blk'}, dimensions={0} | all-to-all | bytes 589824 | tf_op jit(solution)/shard_map/all_to_all | solution.py:419
  87.0 0.7 shard_map.98
  87.7 9.7 %all_to_all.29.arrived = bf16[32,4,192]{2,1,0:T(4,128)(2,1)S(1)} all-to-all(bf16[32,4,192]{2,1,0:T(4,128)(2,1)S(1)} %shard_map.98), channel_id=1, replica_groups=mesh['section'=2,'blk'=16] {'section','blk'}, dimensions={0} | all-to-all | bytes 98304 | tf_op jit(solution)/shard_map/all_to_all | solution.py:419
  97.4 0.8 shard_map.99
  (1 shorter events, 0.0 us)
Async XLA Ops:
  0.0 1.5 %copy-start = (f32[1,50,3,3072]{3,0,2,1:T(1,128)S(1)}, f32[1,50,3,3072]{3,0,2,1:T(1,128)}, u32[]{:S(2)}) copy-start(f32[1,50,3,3072]{3,0,2,1:T(1,128)} %param.12) | copy-start | bytes 5529604
  0.0 2.0 %collective-permute-start = (bf16[3,2,3072]{2,1,0:T(2,128)(2,1)}, bf16[3,2,3072]{2,1,0:T(2,128)(2,1)S(1)}, u32[]{:S(2)}, u32[]{:S(2)}) collective-permute-start(bf16[3,2,3072]{2,1,0:T(2,128)(2,1)} %bitcast.29), channel_id=1, source_target_pairs={{0,16},{16,0},{1,17},{17,1},{2,18},{18,2},{3,19},{19,3},{4,20},{20... | collective-permute-start | bytes 110600 | tf_op jit(solution)/shard_map/ppermute | solution.py:423
  0.5 1.5 %collective-permute-start.1 = (bf16[3,2,3072]{2,1,0:T(2,128)(2,1)}, bf16[3,2,3072]{2,1,0:T(2,128)(2,1)S(1)}, u32[]{:S(2)}, u32[]{:S(2)}) collective-permute-start(bf16[3,2,3072]{2,1,0:T(2,128)(2,1)} %bitcast.31), channel_id=1, source_target_pairs={{0,16},{16,0},{1,17},{17,1},{2,18},{18,2},{3,19},{19,3},{4,20},{20... | collective-permute-start | bytes 110600 | tf_op jit(solution)/shard_map/ppermute | solution.py:423
  1.5 1.3 %collective-permute-start.2 = (f32[3,1,3072]{2,1,0:T(1,128)S(1)}, f32[3,1,3072]{2,1,0:T(1,128)S(1)}, u32[]{:S(2)}, u32[]{:S(2)}) collective-permute-start(f32[3,1,3072]{2,1,0:T(1,128)S(1)} %dynamic-slice_bitcast_fusion.mod), channel_id=1, source_target_pairs={{0,16},{16,0},{1,17},{17,1},{2,18},{18,2},{3,19},{19,3},{4,20},{20... | collective-permute-start | bytes 110600 | tf_op jit(solution)/shard_map/ppermute | solution.py:423
  2.0 1.4 %collective-permute-start.3 = (s32[1,2,16]{2,1,0:T(2,128)}, s32[1,2,16]{2,1,0:T(2,128)S(1)}, u32[]{:S(2)}, u32[]{:S(2)}) collective-permute-start(s32[1,2,16]{2,1,0:T(2,128)} %fresh.3), channel_id=1, source_target_pairs={{0,16},{16,0},{1,17},{17,1},{2,18},{18,2},{3,19},{19,3},{4,20},{20... | collective-permute-start | bytes 392 | tf_op jit(solution)/shard_map/ppermute | solution.py:423
  3.3 22.6 %collective-permute-start.4 = (bf16[576,3072]{1,0:T(8,128)(2,1)}, bf16[576,3072]{1,0:T(8,128)(2,1)S(1)}, u32[]{:S(2)}, u32[]{:S(2)}) collective-permute-start(bf16[576,3072]{1,0:T(8,128)(2,1)} %bitcast.22), channel_id=1, source_target_pairs={{0,16},{16,0},{1,17},{17,1},{2,18},{18,2},{3,19},{19,3},{4,20},{20... | collective-permute-start | bytes 10616840 | tf_op jit(solution)/shard_map/ppermute | solution.py:423
  3.5 22.4 %collective-permute-start.5 = (bf16[192,3072]{1,0:T(8,128)(2,1)}, bf16[192,3072]{1,0:T(8,128)(2,1)S(1)}, u32[]{:S(2)}, u32[]{:S(2)}) collective-permute-start(bf16[192,3072]{1,0:T(8,128)(2,1)} %bitcast.25), channel_id=1, source_target_pairs={{0,16},{16,0},{1,17},{17,1},{2,18},{18,2},{3,19},{19,3},{4,20},{20... | collective-permute-start | bytes 3538952 | tf_op jit(solution)/shard_map/ppermute | solution.py:423
  25.9 10.3 %copy-start.3 = (s32[1,2,16]{2,1,0:T(2,128)S(1)}, s32[1,2,16]{2,1,0:T(2,128)}, u32[]{:S(2)}) copy-start(s32[1,2,16]{2,1,0:T(2,128)} %fresh.3) | copy-start | bytes 388
  25.9 10.3 %copy-start.4 = (s32[2,16]{1,0:T(2,128)S(1)}, s32[2,16]{1,0:T(2,128)}, u32[]{:S(2)}) copy-start(s32[2,16]{1,0:T(2,128)} %live.3) | copy-start | bytes 388
  29.4 21.0 %copy-start.2 = (bf16[1,3072,192]{1,2,0:T(8,128)(2,1)S(1)}, bf16[1,3072,192]{1,2,0:T(8,128)(2,1)}, u32[]{:S(2)}) copy-start(bf16[1,3072,192]{1,2,0:T(8,128)(2,1)} %param.11) | copy-start | bytes 3538948
  29.5 4.7 %collective-permute-start.6 = (bf16[72,128]{1,0:T(8,128)(2,1)S(1)}, bf16[72,128]{1,0:T(8,128)(2,1)S(1)}, u32[]{:S(2)}, u32[]{:S(2)}) collective-permute-start(bf16[72,128]{1,0:T(8,128)(2,1)S(1)} %get-tuple-element.40), channel_id=1, source_target_pairs={{0,5},{1,12},{2,7},{3,14},{4,9},{5,0},{6,11},{7,2},{8,13},{9,4},{1... | collective-permute-start | bytes 55304 | tf_op jit(solution)/shard_map/ppermute | solution.py:431
  30.6 5.6 %collective-permute-start.7 = (bf16[72,128]{1,0:T(8,128)(2,1)S(1)}, bf16[72,128]{1,0:T(8,128)(2,1)S(1)}, u32[]{:S(2)}, u32[]{:S(2)}) collective-permute-start(bf16[72,128]{1,0:T(8,128)(2,1)S(1)} %get-tuple-element.41), channel_id=1, source_target_pairs={{0,6},{1,11},{2,8},{3,13},{4,10},{5,15},{6,12},{7,1},{8,14},{9,3},... | collective-permute-start | bytes 55304 | tf_op jit(solution)/shard_map/ppermute | solution.py:431
  37.5 26.2 %copy-start.1 = (bf16[1,3072,576]{1,2,0:T(8,128)(2,1)S(1)}, bf16[1,3072,576]{1,2,0:T(8,128)(2,1)}, u32[]{:S(2)}) copy-start(bf16[1,3072,576]{1,2,0:T(8,128)(2,1)} %param.10) | copy-start | bytes 10616836
  65.4 4.7 %collective-permute-start.8 = (bf16[72,128]{1,0:T(8,128)(2,1)S(1)}, bf16[72,128]{1,0:T(8,128)(2,1)S(1)}, u32[]{:S(2)}, u32[]{:S(2)}) collective-permute-start(bf16[72,128]{1,0:T(8,128)(2,1)S(1)} %get-tuple-element.49), channel_id=1, source_target_pairs={{0,5},{1,12},{2,7},{3,14},{4,9},{5,0},{6,11},{7,2},{8,13},{9,4},{1... | collective-permute-start | bytes 55304 | tf_op jit(solution)/shard_map/ppermute | solution.py:431
  66.1 5.6 %collective-permute-start.9 = (bf16[72,128]{1,0:T(8,128)(2,1)S(1)}, bf16[72,128]{1,0:T(8,128)(2,1)S(1)}, u32[]{:S(2)}, u32[]{:S(2)}) collective-permute-start(bf16[72,128]{1,0:T(8,128)(2,1)S(1)} %get-tuple-element.50), channel_id=1, source_target_pairs={{0,6},{1,11},{2,8},{3,13},{4,10},{5,15},{6,12},{7,1},{8,14},{9,3},... | collective-permute-start | bytes 55304 | tf_op jit(solution)/shard_map/ppermute | solution.py:431

commit v4 on v3

--- a/solution.py
+++ b/solution.py
@@ -384,11 +384,11 @@
     own, other = arrays[:2], arrays[2:]
     stale = [jnp.where(first, a, b) for a, b in zip(own, other)] + [jnp.where(first, b, a) for a, b in zip(own, other)]
     for b in range(n):
-        at = columns * group_of(b, n)
-        block = jnp.concatenate([array[:, at : at + columns] for array in stale], axis=1)
+        at = columns * group_of(b, n) // 128 * 128
+        block = jnp.concatenate([array[:, at : at + 256] for array in stale], axis=1)
         leaving[b, :rows, :] = mine
         for i in range(rows):
-            leaving[b, rows : rows + 1, i * 4 * columns : (i + 1) * 4 * columns] = block[i : i + 1].astype(BF16)
+            leaving[b, rows : rows + 1, i * 1024 : (i + 1) * 1024] = block[i : i + 1].astype(BF16)
 
 
 def stale_by_token(arrived, mod, other_mod, old, second_mod, rows):
@@ -401,7 +401,10 @@
             for layer in range(2):
                 at = (i * 2 + layer) * wide
                 rows[layer, per * b + i : per * b + i + 1, :] = flat[:, at : at + wide]
-    old[...] = rows[...].astype(BF16)
+    odd = (lax.axis_index("blk") & 1) == 1
+    for layer in range(2):
+        pair = [rows[layer, :, at : at + 256] for at in (0, 256)]
+        old[layer] = jnp.concatenate([jnp.where(odd, part[:, 64:], part[:, :192]) for part in pair], axis=1).astype(BF16)
     second_mod[...] = own_or_other(1, mod[...], other_mod[...])
 
 
@@ -501,7 +504,7 @@
             old, next_mod = call(
                 stale_by_token,
                 [shape((2, tokens, 2 * columns), BF16), shape(mod.shape, F32)],
-                [pltpu.VMEM((2, tokens, 2 * columns), F32)],
+                [pltpu.VMEM((2, tokens, 512), F32)],
                 (0, 200000),
                 arrived,
                 *mods,

time: 98.6 us -> 98.6 us (level)
  no operation moved by 1% of the time
where the time goes in v4:
time: 98.6 us; the launch traced here: 98.2 us
  blocking collectives  70 us (71%)
  Pallas kernels  11.5 us (12%)
  waiting for transfers between devices  10.6 us (11%)
  starting transfers between devices  5 us (5%)
    all_to_all x5, blocking collectives, exchange(): return lax.all_to_all(blocks, axis, split_axis=0, concat_axis=0, tiled=True)  70 us
    pallas_call x9, Pallas kernels, call(): pl.pallas_call(body, out_shape=outs, in_specs=specs or [VMEM] * len(args)...  11.5 us
    ppermute x2, waiting for transfers between devices, by_heads(): lax.ppermute(middle, 'blk', pairs1)  5.71 us
    ppermute x2, waiting for transfers between devices, by_heads(): lax.ppermute(other, 'blk', pairs2)  3.65 us
  transfers between devices with their start and end apart: 10, of which 6 were waited for; matrix products, arithmetic and copies ran while one was open for 0% of the time, Pallas kernels for 1%

profile of v4, /device:TPU:0, one launch (start us, length us, event | category | flops | bytes accessed | tf_op | source)
XLA Modules:
  0.0 98.2 jit_solution(15319509270583832788)
XLA Ops:
  0.0 0.0 copy-start
  0.0 0.5 collective-permute-start
  0.5 0.1 collective-permute-start.1
  1.2 0.3 copy-done
  1.5 0.5 collective-permute-start.2
  2.0 0.0 collective-permute-done.other_keys
  2.0 0.0 collective-permute-done.1.other_values
  2.0 0.1 collective-permute-start.3
  2.1 0.8 collective-permute-done.2.other_mod
  2.8 0.5 collective-permute-done.3.other_fresh
  3.3 0.2 collective-permute-start.4
  3.5 0.3 collective-permute-start.5
  3.8 1.1 %shard_map.91 = (bf16[16,4,3072]{2,1,0:T(4,128)(2,1)S(1)}, f32[3,1,3072]{2,1,0:T(1,128)S(1)}) custom-call(bf16[3,2,3072]{2,1,0:T(2,128)(2,1)} %bitcast.28, bf16[3,2,3072]{2,1,0:T(2,128)(2,1)} %bitcast.30, bf16[3,2,3072]{2,1,0:T(2,128)(2,1)} %bitcast.32, bf16[3,2,3072]{2,1,0:T(2,128)(2,1)S(1)} %collective-permute-done.other_keys, ...), custom_call_target="tpu_custom_call" | custom-call | bytes 1000000 | tf_op jit(solution)/shard_map/pallas_call | solution.py:135
  4.9 20.9 %all_to_all.25.arrived = bf16[16,4,3072]{2,1,0:T(4,128)(2,1)S(1)} all-to-all(bf16[16,4,3072]{2,1,0:T(4,128)(2,1)S(1)} %get-tuple-element.34), channel_id=1, replica_groups=mesh['section'=2,'blk'=16] {'blk'}, dimensions={0} | all-to-all | bytes 786432 | tf_op jit(solution)/shard_map/all_to_all | solution.py:422
  25.9 0.0 collective-permute-done.5.other_out.other
  25.9 0.0 collective-permute-done.4.other
  25.9 0.0 copy-start.3
  25.9 0.0 copy-start.4
  25.9 3.6 %shard_map.92 = (bf16[72,128]{1,0:T(8,128)(2,1)S(1)}, bf16[72,128]{1,0:T(8,128)(2,1)S(1)}, bf16[72,128]{1,0:T(8,128)(2,1)S(1)}, bf16[48,192]{1,0:T(8,128)(2,1)S(1)}) custom-call(bf16[16,4,3072]{2,1,0:T(4,128)(2,1)S(1)} %all_to_all.25.arrived, bf16[576,3072]{1,0:T(8,128)(2,1)} %bitcast.23, bf16[576,3072]{1,0:T(8,128)(2,1)S(1)} %collective-permute-done.4.other, ...), custom_call_target="tpu_custom_call" | custom-call | flops 169869312 | bytes 4718592 | tf_op jit(solution)/shard_map/pallas_call | solution.py:135
  29.4 0.0 copy-start.2
  29.4 1.2 %collective-permute-start.6 = (bf16[72,128]{1,0:T(8,128)(2,1)S(1)}, bf16[72,128]{1,0:T(8,128)(2,1)S(1)}, u32[]{:S(2)}, u32[]{:S(2)}) collective-permute-start(bf16[72,128]{1,0:T(8,128)(2,1)S(1)} %get-tuple-element.40), channel_id=1, source_target_pairs={{0,5},{1,12},{2,7},{3,14},{4,9},{5,0},{6,11},{7,2},{8,13},{9,4},{1... | collective-permute-start | bytes 55304 | tf_op jit(solution)/shard_map/ppermute | solution.py:434
  30.6 0.3 collective-permute-start.7
  30.9 0.3 shard_map.93
  31.2 3.0 %collective-permute-done.6.chunk1 = bf16[72,128]{1,0:T(8,128)(2,1)S(1)} collective-permute-done((bf16[72,128]{1,0:T(8,128)(2,1)S(1)}, bf16[72,128]{1,0:T(8,128)(2,1)S(1)}, u32[]{:S(2)}, u32[]{:S(2)}) %collective-permute-start.6) | collective-permute-done | bytes 18464 | tf_op jit(solution)/shard_map/ppermute | solution.py:434
  34.2 2.0 %collective-permute-done.7.chunk2 = bf16[72,128]{1,0:T(8,128)(2,1)S(1)} collective-permute-done((bf16[72,128]{1,0:T(8,128)(2,1)S(1)}, bf16[72,128]{1,0:T(8,128)(2,1)S(1)}, u32[]{:S(2)}, u32[]{:S(2)}) %collective-permute-start.7) | collective-permute-done | bytes 18464 | tf_op jit(solution)/shard_map/ppermute | solution.py:434
  36.2 0.0 copy-done.3
  36.2 0.0 copy-done.4
  36.2 1.3 %shard_map.94 = bf16[16,72,128]{2,1,0:T(8,128)(2,1)S(1)} custom-call(bf16[72,128]{1,0:T(8,128)(2,1)S(1)} %get-tuple-element.38.chunk0, bf16[72,128]{1,0:T(8,128)(2,1)S(1)} %collective-permute-done.6.chunk1, bf16[72,128]{1,0:T(8,128)(2,1)S(1)} %collective-permute-done.7.chunk2, bf16[2,48,384]{2,1,0:T(8,128)(2,1)S(1)} %get-tuple-element.43.old, ...), custom_call_target="tpu_custom_call" | custom-call | flops 3538944 | bytes 300000 | tf_op jit(solution)/shard_map/pallas_call | solution.py:135
  37.5 0.0 copy-start.1
  37.5 12.9 %all_to_all.26.blocks = bf16[16,72,128]{2,1,0:T(8,128)(2,1)S(1)} all-to-all(bf16[16,72,128]{2,1,0:T(8,128)(2,1)S(1)} %shard_map.94), channel_id=1, replica_groups=mesh['section'=2,'blk'=16] {'blk'}, dimensions={0} | all-to-all | bytes 589824 | tf_op jit(solution)/shard_map/all_to_all | solution.py:422
  50.4 0.0 copy-done.2
  50.4 0.9 shard_map.95
  51.3 12.4 %all_to_all.27.blocks = bf16[16,72,128]{2,1,0:T(8,128)(2,1)S(1)} all-to-all(bf16[16,72,128]{2,1,0:T(8,128)(2,1)S(1)} %get-tuple-element.46), channel_id=1, replica_groups=mesh['section'=2,'blk'=16] {'blk'}, dimensions={0} | all-to-all | bytes 589824 | tf_op jit(solution)/shard_map/all_to_all | solution.py:422
  63.7 0.0 copy-done.1
  63.7 1.7 %shard_map.96 = (bf16[72,128]{1,0:T(8,128)(2,1)S(1)}, bf16[72,128]{1,0:T(8,128)(2,1)S(1)}, bf16[72,128]{1,0:T(8,128)(2,1)S(1)}, bf16[48,192]{1,0:T(8,128)(2,1)S(1)}) custom-call(bf16[16,72,128]{2,1,0:T(8,128)(2,1)S(1)} %all_to_all.27.blocks, bf16[576,3072]{1,0:T(8,128)(2,1)S(1)} %bitcast.24, bf16[576,3072]{1,0:T(8,128)(2,1)S(1)} %collective-permute-done.4.other, ...), custom_call_target="tpu_custom_call" | custom-call | flops 169869312 | bytes 4718592 | tf_op jit(solution)/shard_map/pallas_call | solution.py:135
  65.4 0.8 collective-permute-start.8
  66.1 1.2 %collective-permute-start.9 = (bf16[72,128]{1,0:T(8,128)(2,1)S(1)}, bf16[72,128]{1,0:T(8,128)(2,1)S(1)}, u32[]{:S(2)}, u32[]{:S(2)}) collective-permute-start(bf16[72,128]{1,0:T(8,128)(2,1)S(1)} %get-tuple-element.50), channel_id=1, source_target_pairs={{0,6},{1,11},{2,8},{3,13},{4,10},{5,15},{6,12},{7,1},{8,14},{9,3},... | collective-permute-start | bytes 55304 | tf_op jit(solution)/shard_map/ppermute | solution.py:434
  67.3 2.7 %collective-permute-done.8.chunk1 = bf16[72,128]{1,0:T(8,128)(2,1)S(1)} collective-permute-done((bf16[72,128]{1,0:T(8,128)(2,1)S(1)}, bf16[72,128]{1,0:T(8,128)(2,1)S(1)}, u32[]{:S(2)}, u32[]{:S(2)}) %collective-permute-start.8) | collective-permute-done | bytes 18464 | tf_op jit(solution)/shard_map/ppermute | solution.py:434
  70.0 1.7 %collective-permute-done.9.chunk2 = bf16[72,128]{1,0:T(8,128)(2,1)S(1)} collective-permute-done((bf16[72,128]{1,0:T(8,128)(2,1)S(1)}, bf16[72,128]{1,0:T(8,128)(2,1)S(1)}, u32[]{:S(2)}, u32[]{:S(2)}) %collective-permute-start.9) | collective-permute-done | bytes 18464 | tf_op jit(solution)/shard_map/ppermute | solution.py:434
  71.7 1.3 %shard_map.97 = bf16[16,72,128]{2,1,0:T(8,128)(2,1)S(1)} custom-call(bf16[72,128]{1,0:T(8,128)(2,1)S(1)} %get-tuple-element.48.chunk0, bf16[72,128]{1,0:T(8,128)(2,1)S(1)} %collective-permute-done.8.chunk1, bf16[72,128]{1,0:T(8,128)(2,1)S(1)} %collective-permute-done.9.chunk2, bf16[2,48,384]{2,1,0:T(8,128)(2,1)S(1)} %get-tuple-element.43.old, ...), custom_call_target="tpu_custom_call" | custom-call | flops 3538944 | bytes 300000 | tf_op jit(solution)/shard_map/pallas_call | solution.py:135
  73.0 14.0 %all_to_all.28.blocks = bf16[16,72,128]{2,1,0:T(8,128)(2,1)S(1)} all-to-all(bf16[16,72,128]{2,1,0:T(8,128)(2,1)S(1)} %shard_map.97), channel_id=1, replica_groups=mesh['section'=2,'blk'=16] {'blk'}, dimensions={0} | all-to-all | bytes 589824 | tf_op jit(solution)/shard_map/all_to_all | solution.py:422
  87.0 0.7 shard_map.98
  87.7 9.7 %all_to_all.29.arrived = bf16[32,4,192]{2,1,0:T(4,128)(2,1)S(1)} all-to-all(bf16[32,4,192]{2,1,0:T(4,128)(2,1)S(1)} %shard_map.98), channel_id=1, replica_groups=mesh['section'=2,'blk'=16] {'section','blk'}, dimensions={0} | all-to-all | bytes 98304 | tf_op jit(solution)/shard_map/all_to_all | solution.py:422
  97.4 0.8 shard_map.99
  (1 shorter events, 0.0 us)
Async XLA Ops:
  0.0 1.5 %copy-start = (f32[1,50,3,3072]{3,0,2,1:T(1,128)S(1)}, f32[1,50,3,3072]{3,0,2,1:T(1,128)}, u32[]{:S(2)}) copy-start(f32[1,50,3,3072]{3,0,2,1:T(1,128)} %param.12) | copy-start | bytes 5529604
  0.0 2.0 %collective-permute-start = (bf16[3,2,3072]{2,1,0:T(2,128)(2,1)}, bf16[3,2,3072]{2,1,0:T(2,128)(2,1)S(1)}, u32[]{:S(2)}, u32[]{:S(2)}) collective-permute-start(bf16[3,2,3072]{2,1,0:T(2,128)(2,1)} %bitcast.29), channel_id=1, source_target_pairs={{0,16},{16,0},{1,17},{17,1},{2,18},{18,2},{3,19},{19,3},{4,20},{20... | collective-permute-start | bytes 110600 | tf_op jit(solution)/shard_map/ppermute | solution.py:426
  0.5 1.5 %collective-permute-start.1 = (bf16[3,2,3072]{2,1,0:T(2,128)(2,1)}, bf16[3,2,3072]{2,1,0:T(2,128)(2,1)S(1)}, u32[]{:S(2)}, u32[]{:S(2)}) collective-permute-start(bf16[3,2,3072]{2,1,0:T(2,128)(2,1)} %bitcast.31), channel_id=1, source_target_pairs={{0,16},{16,0},{1,17},{17,1},{2,18},{18,2},{3,19},{19,3},{4,20},{20... | collective-permute-start | bytes 110600 | tf_op jit(solution)/shard_map/ppermute | solution.py:426
  1.5 1.3 %collective-permute-start.2 = (f32[3,1,3072]{2,1,0:T(1,128)S(1)}, f32[3,1,3072]{2,1,0:T(1,128)S(1)}, u32[]{:S(2)}, u32[]{:S(2)}) collective-permute-start(f32[3,1,3072]{2,1,0:T(1,128)S(1)} %dynamic-slice_bitcast_fusion.mod), channel_id=1, source_target_pairs={{0,16},{16,0},{1,17},{17,1},{2,18},{18,2},{3,19},{19,3},{4,20},{20... | collective-permute-start | bytes 110600 | tf_op jit(solution)/shard_map/ppermute | solution.py:426
  2.0 1.4 %collective-permute-start.3 = (s32[1,2,16]{2,1,0:T(2,128)}, s32[1,2,16]{2,1,0:T(2,128)S(1)}, u32[]{:S(2)}, u32[]{:S(2)}) collective-permute-start(s32[1,2,16]{2,1,0:T(2,128)} %fresh.3), channel_id=1, source_target_pairs={{0,16},{16,0},{1,17},{17,1},{2,18},{18,2},{3,19},{19,3},{4,20},{20... | collective-permute-start | bytes 392 | tf_op jit(solution)/shard_map/ppermute | solution.py:426
  3.3 22.5 %collective-permute-start.4 = (bf16[576,3072]{1,0:T(8,128)(2,1)}, bf16[576,3072]{1,0:T(8,128)(2,1)S(1)}, u32[]{:S(2)}, u32[]{:S(2)}) collective-permute-start(bf16[576,3072]{1,0:T(8,128)(2,1)} %bitcast.22), channel_id=1, source_target_pairs={{0,16},{16,0},{1,17},{17,1},{2,18},{18,2},{3,19},{19,3},{4,20},{20... | collective-permute-start | bytes 10616840 | tf_op jit(solution)/shard_map/ppermute | solution.py:426
  3.5 22.3 %collective-permute-start.5 = (bf16[192,3072]{1,0:T(8,128)(2,1)}, bf16[192,3072]{1,0:T(8,128)(2,1)S(1)}, u32[]{:S(2)}, u32[]{:S(2)}) collective-permute-start(bf16[192,3072]{1,0:T(8,128)(2,1)} %bitcast.25), channel_id=1, source_target_pairs={{0,16},{16,0},{1,17},{17,1},{2,18},{18,2},{3,19},{19,3},{4,20},{20... | collective-permute-start | bytes 3538952 | tf_op jit(solution)/shard_map/ppermute | solution.py:426
  25.9 10.3 %copy-start.3 = (s32[1,2,16]{2,1,0:T(2,128)S(1)}, s32[1,2,16]{2,1,0:T(2,128)}, u32[]{:S(2)}) copy-start(s32[1,2,16]{2,1,0:T(2,128)} %fresh.3) | copy-start | bytes 388
  25.9 10.3 %copy-start.4 = (s32[2,16]{1,0:T(2,128)S(1)}, s32[2,16]{1,0:T(2,128)}, u32[]{:S(2)}) copy-start(s32[2,16]{1,0:T(2,128)} %live.3) | copy-start | bytes 388
  29.4 21.0 %copy-start.2 = (bf16[1,3072,192]{1,2,0:T(8,128)(2,1)S(1)}, bf16[1,3072,192]{1,2,0:T(8,128)(2,1)}, u32[]{:S(2)}) copy-start(bf16[1,3072,192]{1,2,0:T(8,128)(2,1)} %param.11) | copy-start | bytes 3538948
  29.4 4.7 %collective-permute-start.6 = (bf16[72,128]{1,0:T(8,128)(2,1)S(1)}, bf16[72,128]{1,0:T(8,128)(2,1)S(1)}, u32[]{:S(2)}, u32[]{:S(2)}) collective-permute-start(bf16[72,128]{1,0:T(8,128)(2,1)S(1)} %get-tuple-element.40), channel_id=1, source_target_pairs={{0,5},{1,12},{2,7},{3,14},{4,9},{5,0},{6,11},{7,2},{8,13},{9,4},{1... | collective-permute-start | bytes 55304 | tf_op jit(solution)/shard_map/ppermute | solution.py:434
  30.6 5.6 %collective-permute-start.7 = (bf16[72,128]{1,0:T(8,128)(2,1)S(1)}, bf16[72,128]{1,0:T(8,128)(2,1)S(1)}, u32[]{:S(2)}, u32[]{:S(2)}) collective-permute-start(bf16[72,128]{1,0:T(8,128)(2,1)S(1)} %get-tuple-element.41), channel_id=1, source_target_pairs={{0,6},{1,11},{2,8},{3,13},{4,10},{5,15},{6,12},{7,1},{8,14},{9,3},... | collective-permute-start | bytes 55304 | tf_op jit(solution)/shard_map/ppermute | solution.py:434
  37.5 26.2 %copy-start.1 = (bf16[1,3072,576]{1,2,0:T(8,128)(2,1)S(1)}, bf16[1,3072,576]{1,2,0:T(8,128)(2,1)}, u32[]{:S(2)}) copy-start(bf16[1,3072,576]{1,2,0:T(8,128)(2,1)} %param.10) | copy-start | bytes 10616836
  65.4 4.7 %collective-permute-start.8 = (bf16[72,128]{1,0:T(8,128)(2,1)S(1)}, bf16[72,128]{1,0:T(8,128)(2,1)S(1)}, u32[]{:S(2)}, u32[]{:S(2)}) collective-permute-start(bf16[72,128]{1,0:T(8,128)(2,1)S(1)} %get-tuple-element.49), channel_id=1, source_target_pairs={{0,5},{1,12},{2,7},{3,14},{4,9},{5,0},{6,11},{7,2},{8,13},{9,4},{1... | collective-permute-start | bytes 55304 | tf_op jit(solution)/shard_map/ppermute | solution.py:434
  66.1 5.6 %collective-permute-start.9 = (bf16[72,128]{1,0:T(8,128)(2,1)S(1)}, bf16[72,128]{1,0:T(8,128)(2,1)S(1)}, u32[]{:S(2)}, u32[]{:S(2)}) collective-permute-start(bf16[72,128]{1,0:T(8,128)(2,1)S(1)} %get-tuple-element.50), channel_id=1, source_target_pairs={{0,6},{1,11},{2,8},{3,13},{4,10},{5,15},{6,12},{7,1},{8,14},{9,3},... | collective-permute-start | bytes 55304 | tf_op jit(solution)/shard_map/ppermute | solution.py:434

commit v5 on v3

--- a/solution.py
+++ b/solution.py
@@ -264,8 +264,8 @@
 
     @pl.when(holds)
     def _():
-        for copy in copies:
-            copy.start()
+        for i, copy in enumerate(copies):
+            copy.start(priority=i % 2)
 
     n = arrived.shape[0]
     rows = stream.shape[0] // n

time: 98.6 us -> 98.5 us (level)
  no operation moved by 1% of the time
where the time goes in v5:
time: 98.5 us; the launch traced here: 98.1 us
  blocking collectives  69.9 us (71%)
  Pallas kernels  11.3 us (11%)
  waiting for transfers between devices  10.8 us (11%)
  starting transfers between devices  5.02 us (5%)
    all_to_all x5, blocking collectives, exchange(): return lax.all_to_all(blocks, axis, split_axis=0, concat_axis=0, tiled=True)  69.9 us
    pallas_call x9, Pallas kernels, call(): pl.pallas_call(body, out_shape=outs, in_specs=specs or [VMEM] * len(args)...  11.3 us
    ppermute x2, waiting for transfers between devices, by_heads(): lax.ppermute(middle, 'blk', pairs1)  5.83 us
    ppermute x2, waiting for transfers between devices, by_heads(): lax.ppermute(other, 'blk', pairs2)  3.65 us
  transfers between devices with their start and end apart: 10, of which 6 were waited for; matrix products, arithmetic and copies ran while one was open for 0% of the time, Pallas kernels for 1%

profile of v5, /device:TPU:0, one launch (start us, length us, event | category | flops | bytes accessed | tf_op | source)
XLA Modules:
  0.0 98.1 jit_solution(7153686162667327771)
XLA Ops:
  0.0 0.0 copy-start
  0.0 0.5 collective-permute-start
  0.5 0.1 collective-permute-start.1
  1.2 0.3 copy-done
  1.5 0.5 collective-permute-start.2
  2.0 0.0 collective-permute-done.other_keys
  2.0 0.0 collective-permute-done.1.other_values
  2.0 0.1 collective-permute-start.3
  2.1 0.8 collective-permute-done.2.other_mod
  2.8 0.5 collective-permute-done.3.other_fresh
  3.3 0.2 collective-permute-start.4
  3.5 0.3 collective-permute-start.5
  3.8 1.1 %shard_map.91 = (bf16[16,4,3072]{2,1,0:T(4,128)(2,1)S(1)}, f32[3,1,3072]{2,1,0:T(1,128)S(1)}) custom-call(bf16[3,2,3072]{2,1,0:T(2,128)(2,1)} %bitcast.28, bf16[3,2,3072]{2,1,0:T(2,128)(2,1)} %bitcast.30, bf16[3,2,3072]{2,1,0:T(2,128)(2,1)} %bitcast.32, bf16[3,2,3072]{2,1,0:T(2,128)(2,1)S(1)} %collective-permute-done.other_keys, ...), custom_call_target="tpu_custom_call" | custom-call | bytes 1000000 | tf_op jit(solution)/shard_map/pallas_call | solution.py:135
  4.9 20.9 %all_to_all.25.arrived = bf16[16,4,3072]{2,1,0:T(4,128)(2,1)S(1)} all-to-all(bf16[16,4,3072]{2,1,0:T(4,128)(2,1)S(1)} %get-tuple-element.34), channel_id=1, replica_groups=mesh['section'=2,'blk'=16] {'blk'}, dimensions={0} | all-to-all | bytes 786432 | tf_op jit(solution)/shard_map/all_to_all | solution.py:419
  25.9 0.0 collective-permute-done.5.other_out.other
  25.9 0.0 collective-permute-done.4.other
  25.9 0.0 copy-start.3
  25.9 0.0 copy-start.4
  25.9 3.5 %shard_map.92 = (bf16[72,128]{1,0:T(8,128)(2,1)S(1)}, bf16[72,128]{1,0:T(8,128)(2,1)S(1)}, bf16[72,128]{1,0:T(8,128)(2,1)S(1)}, bf16[48,192]{1,0:T(8,128)(2,1)S(1)}) custom-call(bf16[16,4,3072]{2,1,0:T(4,128)(2,1)S(1)} %all_to_all.25.arrived, bf16[576,3072]{1,0:T(8,128)(2,1)} %bitcast.23, bf16[576,3072]{1,0:T(8,128)(2,1)S(1)} %collective-permute-done.4.other, ...), custom_call_target="tpu_custom_call" | custom-call | flops 169869312 | bytes 4718592 | tf_op jit(solution)/shard_map/pallas_call | solution.py:135
  29.4 0.0 copy-start.2
  29.4 1.2 %collective-permute-start.6 = (bf16[72,128]{1,0:T(8,128)(2,1)S(1)}, bf16[72,128]{1,0:T(8,128)(2,1)S(1)}, u32[]{:S(2)}, u32[]{:S(2)}) collective-permute-start(bf16[72,128]{1,0:T(8,128)(2,1)S(1)} %get-tuple-element.40), channel_id=1, source_target_pairs={{0,5},{1,12},{2,7},{3,14},{4,9},{5,0},{6,11},{7,2},{8,13},{9,4},{1... | collective-permute-start | bytes 55304 | tf_op jit(solution)/shard_map/ppermute | solution.py:431
  30.6 0.3 collective-permute-start.7
  30.9 0.1 shard_map.93
  31.0 3.1 %collective-permute-done.6.chunk1 = bf16[72,128]{1,0:T(8,128)(2,1)S(1)} collective-permute-done((bf16[72,128]{1,0:T(8,128)(2,1)S(1)}, bf16[72,128]{1,0:T(8,128)(2,1)S(1)}, u32[]{:S(2)}, u32[]{:S(2)}) %collective-permute-start.6) | collective-permute-done | bytes 18464 | tf_op jit(solution)/shard_map/ppermute | solution.py:431
  34.2 2.0 %collective-permute-done.7.chunk2 = bf16[72,128]{1,0:T(8,128)(2,1)S(1)} collective-permute-done((bf16[72,128]{1,0:T(8,128)(2,1)S(1)}, bf16[72,128]{1,0:T(8,128)(2,1)S(1)}, u32[]{:S(2)}, u32[]{:S(2)}) %collective-permute-start.7) | collective-permute-done | bytes 18464 | tf_op jit(solution)/shard_map/ppermute | solution.py:431
  36.1 0.0 copy-done.3
  36.1 0.0 copy-done.4
  36.1 1.3 %shard_map.94 = bf16[16,72,128]{2,1,0:T(8,128)(2,1)S(1)} custom-call(bf16[72,128]{1,0:T(8,128)(2,1)S(1)} %get-tuple-element.38.chunk0, bf16[72,128]{1,0:T(8,128)(2,1)S(1)} %collective-permute-done.6.chunk1, bf16[72,128]{1,0:T(8,128)(2,1)S(1)} %collective-permute-done.7.chunk2, bf16[2,48,384]{2,1,0:T(8,128)(2,1)S(1)} %get-tuple-element.43.old, ...), custom_call_target="tpu_custom_call" | custom-call | flops 3538944 | bytes 300000 | tf_op jit(solution)/shard_map/pallas_call | solution.py:135
  37.5 0.0 copy-start.1
  37.5 12.9 %all_to_all.26.blocks = bf16[16,72,128]{2,1,0:T(8,128)(2,1)S(1)} all-to-all(bf16[16,72,128]{2,1,0:T(8,128)(2,1)S(1)} %shard_map.94), channel_id=1, replica_groups=mesh['section'=2,'blk'=16] {'blk'}, dimensions={0} | all-to-all | bytes 589824 | tf_op jit(solution)/shard_map/all_to_all | solution.py:419
  50.4 0.0 copy-done.2
  50.4 0.9 shard_map.95
  51.3 12.4 %all_to_all.27.blocks = bf16[16,72,128]{2,1,0:T(8,128)(2,1)S(1)} all-to-all(bf16[16,72,128]{2,1,0:T(8,128)(2,1)S(1)} %get-tuple-element.46), channel_id=1, replica_groups=mesh['section'=2,'blk'=16] {'blk'}, dimensions={0} | all-to-all | bytes 589824 | tf_op jit(solution)/shard_map/all_to_all | solution.py:419
  63.6 0.0 copy-done.1
  63.6 1.7 %shard_map.96 = (bf16[72,128]{1,0:T(8,128)(2,1)S(1)}, bf16[72,128]{1,0:T(8,128)(2,1)S(1)}, bf16[72,128]{1,0:T(8,128)(2,1)S(1)}, bf16[48,192]{1,0:T(8,128)(2,1)S(1)}) custom-call(bf16[16,72,128]{2,1,0:T(8,128)(2,1)S(1)} %all_to_all.27.blocks, bf16[576,3072]{1,0:T(8,128)(2,1)S(1)} %bitcast.24, bf16[576,3072]{1,0:T(8,128)(2,1)S(1)} %collective-permute-done.4.other, ...), custom_call_target="tpu_custom_call" | custom-call | flops 169869312 | bytes 4718592 | tf_op jit(solution)/shard_map/pallas_call | solution.py:135
  65.3 0.8 collective-permute-start.8
  66.1 1.2 %collective-permute-start.9 = (bf16[72,128]{1,0:T(8,128)(2,1)S(1)}, bf16[72,128]{1,0:T(8,128)(2,1)S(1)}, u32[]{:S(2)}, u32[]{:S(2)}) collective-permute-start(bf16[72,128]{1,0:T(8,128)(2,1)S(1)} %get-tuple-element.50), channel_id=1, source_target_pairs={{0,6},{1,11},{2,8},{3,13},{4,10},{5,15},{6,12},{7,1},{8,14},{9,3},... | collective-permute-start | bytes 55304 | tf_op jit(solution)/shard_map/ppermute | solution.py:431
  67.3 2.7 %collective-permute-done.8.chunk1 = bf16[72,128]{1,0:T(8,128)(2,1)S(1)} collective-permute-done((bf16[72,128]{1,0:T(8,128)(2,1)S(1)}, bf16[72,128]{1,0:T(8,128)(2,1)S(1)}, u32[]{:S(2)}, u32[]{:S(2)}) %collective-permute-start.8) | collective-permute-done | bytes 18464 | tf_op jit(solution)/shard_map/ppermute | solution.py:431
  70.0 1.7 %collective-permute-done.9.chunk2 = bf16[72,128]{1,0:T(8,128)(2,1)S(1)} collective-permute-done((bf16[72,128]{1,0:T(8,128)(2,1)S(1)}, bf16[72,128]{1,0:T(8,128)(2,1)S(1)}, u32[]{:S(2)}, u32[]{:S(2)}) %collective-permute-start.9) | collective-permute-done | bytes 18464 | tf_op jit(solution)/shard_map/ppermute | solution.py:431
  71.7 1.3 %shard_map.97 = bf16[16,72,128]{2,1,0:T(8,128)(2,1)S(1)} custom-call(bf16[72,128]{1,0:T(8,128)(2,1)S(1)} %get-tuple-element.48.chunk0, bf16[72,128]{1,0:T(8,128)(2,1)S(1)} %collective-permute-done.8.chunk1, bf16[72,128]{1,0:T(8,128)(2,1)S(1)} %collective-permute-done.9.chunk2, bf16[2,48,384]{2,1,0:T(8,128)(2,1)S(1)} %get-tuple-element.43.old, ...), custom_call_target="tpu_custom_call" | custom-call | flops 3538944 | bytes 300000 | tf_op jit(solution)/shard_map/pallas_call | solution.py:135
  73.0 14.0 %all_to_all.28.blocks = bf16[16,72,128]{2,1,0:T(8,128)(2,1)S(1)} all-to-all(bf16[16,72,128]{2,1,0:T(8,128)(2,1)S(1)} %shard_map.97), channel_id=1, replica_groups=mesh['section'=2,'blk'=16] {'blk'}, dimensions={0} | all-to-all | bytes 589824 | tf_op jit(solution)/shard_map/all_to_all | solution.py:419
  86.9 0.7 shard_map.98
  87.6 9.7 %all_to_all.29.arrived = bf16[32,4,192]{2,1,0:T(4,128)(2,1)S(1)} all-to-all(bf16[32,4,192]{2,1,0:T(4,128)(2,1)S(1)} %shard_map.98), channel_id=1, replica_groups=mesh['section'=2,'blk'=16] {'section','blk'}, dimensions={0} | all-to-all | bytes 98304 | tf_op jit(solution)/shard_map/all_to_all | solution.py:419
  97.4 0.8 shard_map.99
  (1 shorter events, 0.0 us)
Async XLA Ops:
  0.0 1.5 %copy-start = (f32[1,50,3,3072]{3,0,2,1:T(1,128)S(1)}, f32[1,50,3,3072]{3,0,2,1:T(1,128)}, u32[]{:S(2)}) copy-start(f32[1,50,3,3072]{3,0,2,1:T(1,128)} %param.12) | copy-start | bytes 5529604
  0.0 2.0 %collective-permute-start = (bf16[3,2,3072]{2,1,0:T(2,128)(2,1)}, bf16[3,2,3072]{2,1,0:T(2,128)(2,1)S(1)}, u32[]{:S(2)}, u32[]{:S(2)}) collective-permute-start(bf16[3,2,3072]{2,1,0:T(2,128)(2,1)} %bitcast.29), channel_id=1, source_target_pairs={{0,16},{16,0},{1,17},{17,1},{2,18},{18,2},{3,19},{19,3},{4,20},{20... | collective-permute-start | bytes 110600 | tf_op jit(solution)/shard_map/ppermute | solution.py:423
  0.5 1.5 %collective-permute-start.1 = (bf16[3,2,3072]{2,1,0:T(2,128)(2,1)}, bf16[3,2,3072]{2,1,0:T(2,128)(2,1)S(1)}, u32[]{:S(2)}, u32[]{:S(2)}) collective-permute-start(bf16[3,2,3072]{2,1,0:T(2,128)(2,1)} %bitcast.31), channel_id=1, source_target_pairs={{0,16},{16,0},{1,17},{17,1},{2,18},{18,2},{3,19},{19,3},{4,20},{20... | collective-permute-start | bytes 110600 | tf_op jit(solution)/shard_map/ppermute | solution.py:423
  1.5 1.3 %collective-permute-start.2 = (f32[3,1,3072]{2,1,0:T(1,128)S(1)}, f32[3,1,3072]{2,1,0:T(1,128)S(1)}, u32[]{:S(2)}, u32[]{:S(2)}) collective-permute-start(f32[3,1,3072]{2,1,0:T(1,128)S(1)} %dynamic-slice_bitcast_fusion.mod), channel_id=1, source_target_pairs={{0,16},{16,0},{1,17},{17,1},{2,18},{18,2},{3,19},{19,3},{4,20},{20... | collective-permute-start | bytes 110600 | tf_op jit(solution)/shard_map/ppermute | solution.py:423
  2.0 1.4 %collective-permute-start.3 = (s32[1,2,16]{2,1,0:T(2,128)}, s32[1,2,16]{2,1,0:T(2,128)S(1)}, u32[]{:S(2)}, u32[]{:S(2)}) collective-permute-start(s32[1,2,16]{2,1,0:T(2,128)} %fresh.3), channel_id=1, source_target_pairs={{0,16},{16,0},{1,17},{17,1},{2,18},{18,2},{3,19},{19,3},{4,20},{20... | collective-permute-start | bytes 392 | tf_op jit(solution)/shard_map/ppermute | solution.py:423
  3.3 22.6 %collective-permute-start.4 = (bf16[576,3072]{1,0:T(8,128)(2,1)}, bf16[576,3072]{1,0:T(8,128)(2,1)S(1)}, u32[]{:S(2)}, u32[]{:S(2)}) collective-permute-start(bf16[576,3072]{1,0:T(8,128)(2,1)} %bitcast.22), channel_id=1, source_target_pairs={{0,16},{16,0},{1,17},{17,1},{2,18},{18,2},{3,19},{19,3},{4,20},{20... | collective-permute-start | bytes 10616840 | tf_op jit(solution)/shard_map/ppermute | solution.py:423
  3.5 22.4 %collective-permute-start.5 = (bf16[192,3072]{1,0:T(8,128)(2,1)}, bf16[192,3072]{1,0:T(8,128)(2,1)S(1)}, u32[]{:S(2)}, u32[]{:S(2)}) collective-permute-start(bf16[192,3072]{1,0:T(8,128)(2,1)} %bitcast.25), channel_id=1, source_target_pairs={{0,16},{16,0},{1,17},{17,1},{2,18},{18,2},{3,19},{19,3},{4,20},{20... | collective-permute-start | bytes 3538952 | tf_op jit(solution)/shard_map/ppermute | solution.py:423
  25.9 10.3 %copy-start.3 = (s32[1,2,16]{2,1,0:T(2,128)S(1)}, s32[1,2,16]{2,1,0:T(2,128)}, u32[]{:S(2)}) copy-start(s32[1,2,16]{2,1,0:T(2,128)} %fresh.3) | copy-start | bytes 388
  25.9 10.3 %copy-start.4 = (s32[2,16]{1,0:T(2,128)S(1)}, s32[2,16]{1,0:T(2,128)}, u32[]{:S(2)}) copy-start(s32[2,16]{1,0:T(2,128)} %live.3) | copy-start | bytes 388
  29.4 21.0 %copy-start.2 = (bf16[1,3072,192]{1,2,0:T(8,128)(2,1)S(1)}, bf16[1,3072,192]{1,2,0:T(8,128)(2,1)}, u32[]{:S(2)}) copy-start(bf16[1,3072,192]{1,2,0:T(8,128)(2,1)} %param.11) | copy-start | bytes 3538948
  29.4 4.7 %collective-permute-start.6 = (bf16[72,128]{1,0:T(8,128)(2,1)S(1)}, bf16[72,128]{1,0:T(8,128)(2,1)S(1)}, u32[]{:S(2)}, u32[]{:S(2)}) collective-permute-start(bf16[72,128]{1,0:T(8,128)(2,1)S(1)} %get-tuple-element.40), channel_id=1, source_target_pairs={{0,5},{1,12},{2,7},{3,14},{4,9},{5,0},{6,11},{7,2},{8,13},{9,4},{1... | collective-permute-start | bytes 55304 | tf_op jit(solution)/shard_map/ppermute | solution.py:431
  30.6 5.6 %collective-permute-start.7 = (bf16[72,128]{1,0:T(8,128)(2,1)S(1)}, bf16[72,128]{1,0:T(8,128)(2,1)S(1)}, u32[]{:S(2)}, u32[]{:S(2)}) collective-permute-start(bf16[72,128]{1,0:T(8,128)(2,1)S(1)} %get-tuple-element.41), channel_id=1, source_target_pairs={{0,6},{1,11},{2,8},{3,13},{4,10},{5,15},{6,12},{7,1},{8,14},{9,3},... | collective-permute-start | bytes 55304 | tf_op jit(solution)/shard_map/ppermute | solution.py:431
  37.5 26.2 %copy-start.1 = (bf16[1,3072,576]{1,2,0:T(8,128)(2,1)S(1)}, bf16[1,3072,576]{1,2,0:T(8,128)(2,1)}, u32[]{:S(2)}) copy-start(bf16[1,3072,576]{1,2,0:T(8,128)(2,1)} %param.10) | copy-start | bytes 10616836
  65.3 4.7 %collective-permute-start.8 = (bf16[72,128]{1,0:T(8,128)(2,1)S(1)}, bf16[72,128]{1,0:T(8,128)(2,1)S(1)}, u32[]{:S(2)}, u32[]{:S(2)}) collective-permute-start(bf16[72,128]{1,0:T(8,128)(2,1)S(1)} %get-tuple-element.49), channel_id=1, source_target_pairs={{0,5},{1,12},{2,7},{3,14},{4,9},{5,0},{6,11},{7,2},{8,13},{9,4},{1... | collective-permute-start | bytes 55304 | tf_op jit(solution)/shard_map/ppermute | solution.py:431
  66.1 5.6 %collective-permute-start.9 = (bf16[72,128]{1,0:T(8,128)(2,1)S(1)}, bf16[72,128]{1,0:T(8,128)(2,1)S(1)}, u32[]{:S(2)}, u32[]{:S(2)}) collective-permute-start(bf16[72,128]{1,0:T(8,128)(2,1)S(1)} %get-tuple-element.50), channel_id=1, source_target_pairs={{0,6},{1,11},{2,8},{3,13},{4,10},{5,15},{6,12},{7,1},{8,14},{9,3},... | collective-permute-start | bytes 55304 | tf_op jit(solution)/shard_map/ppermute | solution.py:431

commit v6 on v3

--- a/solution.py
+++ b/solution.py
@@ -360,23 +360,26 @@
             by_token[layer * n + b, :rows, :] = outs[rows * b : rows * b + rows, :].astype(BF16)
 
 
-def first_exchange(hidden, old_keys, old_values, other_keys, other_values, mod, other_mod, leaving, first_mod, held, sems):
+def stage_rows(hidden, old_keys, old_values, staged, sems):
     copies = [
-        pltpu.make_async_copy(ref, held.at[i], sems.at[i])
-        for i, ref in enumerate((hidden, old_keys, old_values, other_keys, other_values))
+        pltpu.make_async_copy(ref, staged.at[i], sems.at[i]) for i, ref in enumerate((hidden, old_keys, old_values))
     ]
     for copy in copies:
         copy.start()
-    rows, reqs, width = hidden.shape
+    for copy in copies:
+        copy.wait()
+
+
+def first_exchange(staged, other_keys, other_values, mod, other_mod, leaving, first_mod):
+    _, rows, reqs, width = staged.shape
     n = leaving.shape[0]
     columns = width // n
     first = lax.axis_index("section") == 0
     first_mod[...] = own_or_other(0, mod[...], other_mod[...])
-    for copy in copies:
-        copy.wait()
+    held = [staged.at[0], staged.at[1], staged.at[2], other_keys, other_values]
 
     def of_request(which):
-        own = [held[which, i].astype(F32) for i in range(rows)]
+        own = [held[which][i].astype(F32) for i in range(rows)]
         return jnp.concatenate([jnp.where(first, pair[:1], pair[1:]) for pair in own], axis=0)
 
     mine, *arrays = [of_request(which) for which in range(5)]
@@ -460,8 +463,16 @@
         (swap_sections(old_keys), swap_sections(old_values), timestep, fresh)
     )
     mod = lax.dynamic_index_in_dim(steps, timestep[0], 0, keepdims=False)
-    other_mod, other_fresh, sent_qkv, sent_out = lax.optimization_barrier(
-        (swap_sections(mod), swap_sections(sent_fresh), own_qkv, own_out)
+    staged = call(
+        stage_rows,
+        shape((3, rows, reqs, width), BF16),
+        [pltpu.SemaphoreType.DMA((3,))],
+        (0, 200000),
+        *(pinned(array) for array in (jnp.transpose(hidden, (1, 0, 2)), old_keys, old_values)),
+        specs=[HBM] * 3,
+    )
+    other_mod, other_fresh, sent_qkv, sent_out, staged = lax.optimization_barrier(
+        (swap_sections(mod), swap_sections(sent_fresh), own_qkv, own_out, staged)
     )
     mods = (mod, other_mod)
     flags = (fresh, other_fresh)
@@ -470,13 +481,12 @@
     leaving, layer_mod = call(
         first_exchange,
         [shape((n, 4, width), BF16), shape(mod.shape, F32)],
-        [pltpu.VMEM((5, rows, reqs, width), BF16), pltpu.SemaphoreType.DMA((5,))],
+        [],
         (0, 1000000),
-        *(pinned(array) for array in (jnp.transpose(hidden, (1, 0, 2)), old_keys, old_values)),
+        staged,
         other_keys,
         other_values,
         *mods,
-        specs=[HBM] * 3 + [ANY] * 2 + [VMEM] * 2,
     )
     arrived = exchange(leaving, "blk")
 

time: 98.6 us -> 97.7 us (level)
    pallas_call x9 -> x10, Pallas kernels: 11.4 us -> 11.3 us  [call(): pl.pallas_call(body, out_shape=outs, in_specs=specs or [VMEM] * len(args)...]
  transfers between devices with their start and end apart: 10 -> 10, of which waited for: 6 -> 5; matrix products, arithmetic and copies ran while one was open for 0% -> 0% of each run, Pallas kernels for 1% -> 1%
where the time goes in v6:
time: 97.7 us; the launch traced here: 97.4 us
  blocking collectives  70 us (72%)
  Pallas kernels  11.3 us (12%)
  waiting for transfers between devices  9.92 us (10%)
  starting transfers between devices  5 us (5%)
    all_to_all x5, blocking collectives, exchange(): return lax.all_to_all(blocks, axis, split_axis=0, concat_axis=0, tiled=True)  70 us
    pallas_call x10, Pallas kernels, call(): pl.pallas_call(body, out_shape=outs, in_specs=specs or [VMEM] * len(args)...  11.3 us
    ppermute x2, waiting for transfers between devices, by_heads(): lax.ppermute(middle, 'blk', pairs1)  5.85 us
    ppermute x2, waiting for transfers between devices, by_heads(): lax.ppermute(other, 'blk', pairs2)  3.65 us
  transfers between devices with their start and end apart: 10, of which 5 were waited for; matrix products, arithmetic and copies ran while one was open for 0% of the time, Pallas kernels for 1%

profile of v6, /device:TPU:0, one launch (start us, length us, event | category | flops | bytes accessed | tf_op | source)
XLA Modules:
  0.0 97.4 jit_solution(12858297241510349844)
XLA Ops:
  0.0 0.0 copy-start
  0.0 0.5 collective-permute-start
  0.5 0.1 collective-permute-start.1
  1.2 0.3 copy-done
  1.5 0.5 collective-permute-start.2
  2.0 0.0 collective-permute-done.other_keys
  2.0 0.0 collective-permute-done.1.other_values
  2.0 0.1 collective-permute-start.3
  2.1 0.8 shard_map.91.staged
  2.9 0.0 collective-permute-done.2.other_mod
  2.9 0.4 collective-permute-done.3.other_fresh
  3.3 0.2 collective-permute-start.4
  3.5 0.3 collective-permute-start.5
  3.8 0.3 shard_map.92
  4.1 20.9 %all_to_all.25.arrived = bf16[16,4,3072]{2,1,0:T(4,128)(2,1)S(1)} all-to-all(bf16[16,4,3072]{2,1,0:T(4,128)(2,1)S(1)} %get-tuple-element.36), channel_id=1, replica_groups=mesh['section'=2,'blk'=16] {'blk'}, dimensions={0} | all-to-all | bytes 786432 | tf_op jit(solution)/shard_map/all_to_all | solution.py:422
  25.0 0.0 collective-permute-done.5.other_out.other
  25.0 0.0 collective-permute-done.4.other
  25.0 0.0 copy-start.3
  25.0 0.0 copy-start.4
  25.0 3.6 %shard_map.93 = (bf16[72,128]{1,0:T(8,128)(2,1)S(1)}, bf16[72,128]{1,0:T(8,128)(2,1)S(1)}, bf16[72,128]{1,0:T(8,128)(2,1)S(1)}, bf16[48,192]{1,0:T(8,128)(2,1)S(1)}) custom-call(bf16[16,4,3072]{2,1,0:T(4,128)(2,1)S(1)} %all_to_all.25.arrived, bf16[576,3072]{1,0:T(8,128)(2,1)} %bitcast.23, bf16[576,3072]{1,0:T(8,128)(2,1)S(1)} %collective-permute-done.4.other, ...), custom_call_target="tpu_custom_call" | custom-call | flops 169869312 | bytes 4718592 | tf_op jit(solution)/shard_map/pallas_call | solution.py:135
  28.6 0.0 copy-start.2
  28.6 1.2 %collective-permute-start.6 = (bf16[72,128]{1,0:T(8,128)(2,1)S(1)}, bf16[72,128]{1,0:T(8,128)(2,1)S(1)}, u32[]{:S(2)}, u32[]{:S(2)}) collective-permute-start(bf16[72,128]{1,0:T(8,128)(2,1)S(1)} %get-tuple-element.42), channel_id=1, source_target_pairs={{0,5},{1,12},{2,7},{3,14},{4,9},{5,0},{6,11},{7,2},{8,13},{9,4},{1... | collective-permute-start | bytes 55304 | tf_op jit(solution)/shard_map/ppermute | solution.py:434
  29.8 0.3 collective-permute-start.7
  30.1 0.1 shard_map.94
  30.2 3.1 %collective-permute-done.6.chunk1 = bf16[72,128]{1,0:T(8,128)(2,1)S(1)} collective-permute-done((bf16[72,128]{1,0:T(8,128)(2,1)S(1)}, bf16[72,128]{1,0:T(8,128)(2,1)S(1)}, u32[]{:S(2)}, u32[]{:S(2)}) %collective-permute-start.6) | collective-permute-done | bytes 18464 | tf_op jit(solution)/shard_map/ppermute | solution.py:434
  33.3 2.0 %collective-permute-done.7.chunk2 = bf16[72,128]{1,0:T(8,128)(2,1)S(1)} collective-permute-done((bf16[72,128]{1,0:T(8,128)(2,1)S(1)}, bf16[72,128]{1,0:T(8,128)(2,1)S(1)}, u32[]{:S(2)}, u32[]{:S(2)}) %collective-permute-start.7) | collective-permute-done | bytes 18464 | tf_op jit(solution)/shard_map/ppermute | solution.py:434
  35.3 0.0 copy-done.3
  35.3 0.0 copy-done.4
  35.3 1.3 %shard_map.95 = bf16[16,72,128]{2,1,0:T(8,128)(2,1)S(1)} custom-call(bf16[72,128]{1,0:T(8,128)(2,1)S(1)} %get-tuple-element.40.chunk0, bf16[72,128]{1,0:T(8,128)(2,1)S(1)} %collective-permute-done.6.chunk1, bf16[72,128]{1,0:T(8,128)(2,1)S(1)} %collective-permute-done.7.chunk2, bf16[2,48,384]{2,1,0:T(8,128)(2,1)S(1)} %get-tuple-element.45.old, ...), custom_call_target="tpu_custom_call" | custom-call | flops 3538944 | bytes 300000 | tf_op jit(solution)/shard_map/pallas_call | solution.py:135
  36.6 0.0 copy-start.1
  36.7 12.9 %all_to_all.26.blocks = bf16[16,72,128]{2,1,0:T(8,128)(2,1)S(1)} all-to-all(bf16[16,72,128]{2,1,0:T(8,128)(2,1)S(1)} %shard_map.95), channel_id=1, replica_groups=mesh['section'=2,'blk'=16] {'blk'}, dimensions={0} | all-to-all | bytes 589824 | tf_op jit(solution)/shard_map/all_to_all | solution.py:422
  49.6 0.0 copy-done.2
  49.6 0.9 shard_map.96
  50.5 12.4 %all_to_all.27.blocks = bf16[16,72,128]{2,1,0:T(8,128)(2,1)S(1)} all-to-all(bf16[16,72,128]{2,1,0:T(8,128)(2,1)S(1)} %get-tuple-element.48), channel_id=1, replica_groups=mesh['section'=2,'blk'=16] {'blk'}, dimensions={0} | all-to-all | bytes 589824 | tf_op jit(solution)/shard_map/all_to_all | solution.py:422
  62.8 0.0 copy-done.1
  62.8 1.7 %shard_map.97 = (bf16[72,128]{1,0:T(8,128)(2,1)S(1)}, bf16[72,128]{1,0:T(8,128)(2,1)S(1)}, bf16[72,128]{1,0:T(8,128)(2,1)S(1)}, bf16[48,192]{1,0:T(8,128)(2,1)S(1)}) custom-call(bf16[16,72,128]{2,1,0:T(8,128)(2,1)S(1)} %all_to_all.27.blocks, bf16[576,3072]{1,0:T(8,128)(2,1)S(1)} %bitcast.24, bf16[576,3072]{1,0:T(8,128)(2,1)S(1)} %collective-permute-done.4.other, ...), custom_call_target="tpu_custom_call" | custom-call | flops 169869312 | bytes 4718592 | tf_op jit(solution)/shard_map/pallas_call | solution.py:135
  64.5 0.8 collective-permute-start.8
  65.3 1.2 %collective-permute-start.9 = (bf16[72,128]{1,0:T(8,128)(2,1)S(1)}, bf16[72,128]{1,0:T(8,128)(2,1)S(1)}, u32[]{:S(2)}, u32[]{:S(2)}) collective-permute-start(bf16[72,128]{1,0:T(8,128)(2,1)S(1)} %get-tuple-element.52), channel_id=1, source_target_pairs={{0,6},{1,11},{2,8},{3,13},{4,10},{5,15},{6,12},{7,1},{8,14},{9,3},... | collective-permute-start | bytes 55304 | tf_op jit(solution)/shard_map/ppermute | solution.py:434
  66.5 2.7 %collective-permute-done.8.chunk1 = bf16[72,128]{1,0:T(8,128)(2,1)S(1)} collective-permute-done((bf16[72,128]{1,0:T(8,128)(2,1)S(1)}, bf16[72,128]{1,0:T(8,128)(2,1)S(1)}, u32[]{:S(2)}, u32[]{:S(2)}) %collective-permute-start.8) | collective-permute-done | bytes 18464 | tf_op jit(solution)/shard_map/ppermute | solution.py:434
  69.2 1.7 %collective-permute-done.9.chunk2 = bf16[72,128]{1,0:T(8,128)(2,1)S(1)} collective-permute-done((bf16[72,128]{1,0:T(8,128)(2,1)S(1)}, bf16[72,128]{1,0:T(8,128)(2,1)S(1)}, u32[]{:S(2)}, u32[]{:S(2)}) %collective-permute-start.9) | collective-permute-done | bytes 18464 | tf_op jit(solution)/shard_map/ppermute | solution.py:434
  70.9 1.3 %shard_map.98 = bf16[16,72,128]{2,1,0:T(8,128)(2,1)S(1)} custom-call(bf16[72,128]{1,0:T(8,128)(2,1)S(1)} %get-tuple-element.50.chunk0, bf16[72,128]{1,0:T(8,128)(2,1)S(1)} %collective-permute-done.8.chunk1, bf16[72,128]{1,0:T(8,128)(2,1)S(1)} %collective-permute-done.9.chunk2, bf16[2,48,384]{2,1,0:T(8,128)(2,1)S(1)} %get-tuple-element.45.old, ...), custom_call_target="tpu_custom_call" | custom-call | flops 3538944 | bytes 300000 | tf_op jit(solution)/shard_map/pallas_call | solution.py:135
  72.2 14.0 %all_to_all.28.blocks = bf16[16,72,128]{2,1,0:T(8,128)(2,1)S(1)} all-to-all(bf16[16,72,128]{2,1,0:T(8,128)(2,1)S(1)} %shard_map.98), channel_id=1, replica_groups=mesh['section'=2,'blk'=16] {'blk'}, dimensions={0} | all-to-all | bytes 589824 | tf_op jit(solution)/shard_map/all_to_all | solution.py:422
  86.2 0.7 shard_map.99
  86.9 9.7 %all_to_all.29.arrived = bf16[32,4,192]{2,1,0:T(4,128)(2,1)S(1)} all-to-all(bf16[32,4,192]{2,1,0:T(4,128)(2,1)S(1)} %shard_map.99), channel_id=1, replica_groups=mesh['section'=2,'blk'=16] {'section','blk'}, dimensions={0} | all-to-all | bytes 98304 | tf_op jit(solution)/shard_map/all_to_all | solution.py:422
  96.6 0.8 shard_map.100
  (1 shorter events, 0.0 us)
Async XLA Ops:
  0.0 1.5 %copy-start = (f32[1,50,3,3072]{3,0,2,1:T(1,128)S(1)}, f32[1,50,3,3072]{3,0,2,1:T(1,128)}, u32[]{:S(2)}) copy-start(f32[1,50,3,3072]{3,0,2,1:T(1,128)} %param.12) | copy-start | bytes 5529604
  0.0 2.0 %collective-permute-start = (bf16[3,2,3072]{2,1,0:T(2,128)(2,1)}, bf16[3,2,3072]{2,1,0:T(2,128)(2,1)S(1)}, u32[]{:S(2)}, u32[]{:S(2)}) collective-permute-start(bf16[3,2,3072]{2,1,0:T(2,128)(2,1)} %bitcast.29), channel_id=1, source_target_pairs={{0,16},{16,0},{1,17},{17,1},{2,18},{18,2},{3,19},{19,3},{4,20},{20... | collective-permute-start | bytes 110600 | tf_op jit(solution)/shard_map/ppermute | solution.py:426
  0.5 1.5 %collective-permute-start.1 = (bf16[3,2,3072]{2,1,0:T(2,128)(2,1)}, bf16[3,2,3072]{2,1,0:T(2,128)(2,1)S(1)}, u32[]{:S(2)}, u32[]{:S(2)}) collective-permute-start(bf16[3,2,3072]{2,1,0:T(2,128)(2,1)} %bitcast.31), channel_id=1, source_target_pairs={{0,16},{16,0},{1,17},{17,1},{2,18},{18,2},{3,19},{19,3},{4,20},{20... | collective-permute-start | bytes 110600 | tf_op jit(solution)/shard_map/ppermute | solution.py:426
  1.5 1.4 %collective-permute-start.2 = (f32[3,1,3072]{2,1,0:T(1,128)S(1)}, f32[3,1,3072]{2,1,0:T(1,128)S(1)}, u32[]{:S(2)}, u32[]{:S(2)}) collective-permute-start(f32[3,1,3072]{2,1,0:T(1,128)S(1)} %dynamic-slice_bitcast_fusion.mod), channel_id=1, source_target_pairs={{0,16},{16,0},{1,17},{17,1},{2,18},{18,2},{3,19},{19,3},{4,20},{20... | collective-permute-start | bytes 110600 | tf_op jit(solution)/shard_map/ppermute | solution.py:426
  2.0 1.4 %collective-permute-start.3 = (s32[1,2,16]{2,1,0:T(2,128)}, s32[1,2,16]{2,1,0:T(2,128)S(1)}, u32[]{:S(2)}, u32[]{:S(2)}) collective-permute-start(s32[1,2,16]{2,1,0:T(2,128)} %fresh.3), channel_id=1, source_target_pairs={{0,16},{16,0},{1,17},{17,1},{2,18},{18,2},{3,19},{19,3},{4,20},{20... | collective-permute-start | bytes 392 | tf_op jit(solution)/shard_map/ppermute | solution.py:426
  3.3 21.7 %collective-permute-start.4 = (bf16[576,3072]{1,0:T(8,128)(2,1)}, bf16[576,3072]{1,0:T(8,128)(2,1)S(1)}, u32[]{:S(2)}, u32[]{:S(2)}) collective-permute-start(bf16[576,3072]{1,0:T(8,128)(2,1)} %bitcast.22), channel_id=1, source_target_pairs={{0,16},{16,0},{1,17},{17,1},{2,18},{18,2},{3,19},{19,3},{4,20},{20... | collective-permute-start | bytes 10616840 | tf_op jit(solution)/shard_map/ppermute | solution.py:426
  3.5 21.5 %collective-permute-start.5 = (bf16[192,3072]{1,0:T(8,128)(2,1)}, bf16[192,3072]{1,0:T(8,128)(2,1)S(1)}, u32[]{:S(2)}, u32[]{:S(2)}) collective-permute-start(bf16[192,3072]{1,0:T(8,128)(2,1)} %bitcast.25), channel_id=1, source_target_pairs={{0,16},{16,0},{1,17},{17,1},{2,18},{18,2},{3,19},{19,3},{4,20},{20... | collective-permute-start | bytes 3538952 | tf_op jit(solution)/shard_map/ppermute | solution.py:426
  25.0 10.3 %copy-start.3 = (s32[1,2,16]{2,1,0:T(2,128)S(1)}, s32[1,2,16]{2,1,0:T(2,128)}, u32[]{:S(2)}) copy-start(s32[1,2,16]{2,1,0:T(2,128)} %fresh.3) | copy-start | bytes 388
  25.0 10.3 %copy-start.4 = (s32[2,16]{1,0:T(2,128)S(1)}, s32[2,16]{1,0:T(2,128)}, u32[]{:S(2)}) copy-start(s32[2,16]{1,0:T(2,128)} %live.3) | copy-start | bytes 388
  28.6 21.0 %copy-start.2 = (bf16[1,3072,192]{1,2,0:T(8,128)(2,1)S(1)}, bf16[1,3072,192]{1,2,0:T(8,128)(2,1)}, u32[]{:S(2)}) copy-start(bf16[1,3072,192]{1,2,0:T(8,128)(2,1)} %param.11) | copy-start | bytes 3538948
  28.6 4.7 %collective-permute-start.6 = (bf16[72,128]{1,0:T(8,128)(2,1)S(1)}, bf16[72,128]{1,0:T(8,128)(2,1)S(1)}, u32[]{:S(2)}, u32[]{:S(2)}) collective-permute-start(bf16[72,128]{1,0:T(8,128)(2,1)S(1)} %get-tuple-element.42), channel_id=1, source_target_pairs={{0,5},{1,12},{2,7},{3,14},{4,9},{5,0},{6,11},{7,2},{8,13},{9,4},{1... | collective-permute-start | bytes 55304 | tf_op jit(solution)/shard_map/ppermute | solution.py:434
  29.8 5.6 %collective-permute-start.7 = (bf16[72,128]{1,0:T(8,128)(2,1)S(1)}, bf16[72,128]{1,0:T(8,128)(2,1)S(1)}, u32[]{:S(2)}, u32[]{:S(2)}) collective-permute-start(bf16[72,128]{1,0:T(8,128)(2,1)S(1)} %get-tuple-element.43), channel_id=1, source_target_pairs={{0,6},{1,11},{2,8},{3,13},{4,10},{5,15},{6,12},{7,1},{8,14},{9,3},... | collective-permute-start | bytes 55304 | tf_op jit(solution)/shard_map/ppermute | solution.py:434
  36.6 26.2 %copy-start.1 = (bf16[1,3072,576]{1,2,0:T(8,128)(2,1)S(1)}, bf16[1,3072,576]{1,2,0:T(8,128)(2,1)}, u32[]{:S(2)}) copy-start(bf16[1,3072,576]{1,2,0:T(8,128)(2,1)} %param.10) | copy-start | bytes 10616836
  64.5 4.7 %collective-permute-start.8 = (bf16[72,128]{1,0:T(8,128)(2,1)S(1)}, bf16[72,128]{1,0:T(8,128)(2,1)S(1)}, u32[]{:S(2)}, u32[]{:S(2)}) collective-permute-start(bf16[72,128]{1,0:T(8,128)(2,1)S(1)} %get-tuple-element.51), channel_id=1, source_target_pairs={{0,5},{1,12},{2,7},{3,14},{4,9},{5,0},{6,11},{7,2},{8,13},{9,4},{1... | collective-permute-start | bytes 55304 | tf_op jit(solution)/shard_map/ppermute | solution.py:434
  65.3 5.6 %collective-permute-start.9 = (bf16[72,128]{1,0:T(8,128)(2,1)S(1)}, bf16[72,128]{1,0:T(8,128)(2,1)S(1)}, u32[]{:S(2)}, u32[]{:S(2)}) collective-permute-start(bf16[72,128]{1,0:T(8,128)(2,1)S(1)} %get-tuple-element.52), channel_id=1, source_target_pairs={{0,6},{1,11},{2,8},{3,13},{4,10},{5,15},{6,12},{7,1},{8,14},{9,3},... | collective-permute-start | bytes 55304 | tf_op jit(solution)/shard_map/ppermute | solution.py:434

commit v7 on v6

--- a/solution.py
+++ b/solution.py
@@ -264,8 +264,8 @@
 
     @pl.when(holds)
     def _():
-        for copy in copies:
-            copy.start()
+        for i, copy in enumerate(copies):
+            copy.start(priority=i % 2)
 
     n = arrived.shape[0]
     rows = stream.shape[0] // n

time: 97.7 us -> 97.6 us (level)
  no operation moved by 1% of the time
where the time goes in v7:
time: 97.6 us; the launch traced here: 97.3 us
  blocking collectives  69.9 us (72%)
  Pallas kernels  11.3 us (12%)
  waiting for transfers between devices  9.91 us (10%)
  starting transfers between devices  5.02 us (5%)
    all_to_all x5, blocking collectives, exchange(): return lax.all_to_all(blocks, axis, split_axis=0, concat_axis=0, tiled=True)  69.9 us
    pallas_call x10, Pallas kernels, call(): pl.pallas_call(body, out_shape=outs, in_specs=specs or [VMEM] * len(args)...  11.3 us
    ppermute x2, waiting for transfers between devices, by_heads(): lax.ppermute(middle, 'blk', pairs1)  5.83 us
    ppermute x2, waiting for transfers between devices, by_heads(): lax.ppermute(other, 'blk', pairs2)  3.65 us
  transfers between devices with their start and end apart: 10, of which 5 were waited for; matrix products, arithmetic and copies ran while one was open for 0% of the time, Pallas kernels for 1%

profile of v7, /device:TPU:0, one launch (start us, length us, event | category | flops | bytes accessed | tf_op | source)
XLA Modules:
  0.0 97.3 jit_solution(11192496646112934325)
XLA Ops:
  0.0 0.0 copy-start
  0.0 0.5 collective-permute-start
  0.5 0.1 collective-permute-start.1
  1.2 0.3 copy-done
  1.5 0.5 collective-permute-start.2
  2.0 0.0 collective-permute-done.other_keys
  2.0 0.0 collective-permute-done.1.other_values
  2.0 0.1 collective-permute-start.3
  2.1 0.8 shard_map.91.staged
  2.9 0.0 collective-permute-done.2.other_mod
  2.9 0.4 collective-permute-done.3.other_fresh
  3.3 0.2 collective-permute-start.4
  3.5 0.3 collective-permute-start.5
  3.8 0.3 shard_map.92
  4.1 20.9 %all_to_all.25.arrived = bf16[16,4,3072]{2,1,0:T(4,128)(2,1)S(1)} all-to-all(bf16[16,4,3072]{2,1,0:T(4,128)(2,1)S(1)} %get-tuple-element.36), channel_id=1, replica_groups=mesh['section'=2,'blk'=16] {'blk'}, dimensions={0} | all-to-all | bytes 786432 | tf_op jit(solution)/shard_map/all_to_all | solution.py:422
  25.0 0.0 collective-permute-done.5.other_out.other
  25.0 0.0 collective-permute-done.4.other
  25.0 0.0 copy-start.3
  25.0 0.0 copy-start.4
  25.0 3.5 %shard_map.93 = (bf16[72,128]{1,0:T(8,128)(2,1)S(1)}, bf16[72,128]{1,0:T(8,128)(2,1)S(1)}, bf16[72,128]{1,0:T(8,128)(2,1)S(1)}, bf16[48,192]{1,0:T(8,128)(2,1)S(1)}) custom-call(bf16[16,4,3072]{2,1,0:T(4,128)(2,1)S(1)} %all_to_all.25.arrived, bf16[576,3072]{1,0:T(8,128)(2,1)} %bitcast.23, bf16[576,3072]{1,0:T(8,128)(2,1)S(1)} %collective-permute-done.4.other, ...), custom_call_target="tpu_custom_call" | custom-call | flops 169869312 | bytes 4718592 | tf_op jit(solution)/shard_map/pallas_call | solution.py:135
  28.6 0.0 copy-start.2
  28.6 1.2 %collective-permute-start.6 = (bf16[72,128]{1,0:T(8,128)(2,1)S(1)}, bf16[72,128]{1,0:T(8,128)(2,1)S(1)}, u32[]{:S(2)}, u32[]{:S(2)}) collective-permute-start(bf16[72,128]{1,0:T(8,128)(2,1)S(1)} %get-tuple-element.42), channel_id=1, source_target_pairs={{0,5},{1,12},{2,7},{3,14},{4,9},{5,0},{6,11},{7,2},{8,13},{9,4},{1... | collective-permute-start | bytes 55304 | tf_op jit(solution)/shard_map/ppermute | solution.py:434
  29.7 0.3 collective-permute-start.7
  30.1 0.1 shard_map.94
  30.2 3.1 %collective-permute-done.6.chunk1 = bf16[72,128]{1,0:T(8,128)(2,1)S(1)} collective-permute-done((bf16[72,128]{1,0:T(8,128)(2,1)S(1)}, bf16[72,128]{1,0:T(8,128)(2,1)S(1)}, u32[]{:S(2)}, u32[]{:S(2)}) %collective-permute-start.6) | collective-permute-done | bytes 18464 | tf_op jit(solution)/shard_map/ppermute | solution.py:434
  33.3 2.0 %collective-permute-done.7.chunk2 = bf16[72,128]{1,0:T(8,128)(2,1)S(1)} collective-permute-done((bf16[72,128]{1,0:T(8,128)(2,1)S(1)}, bf16[72,128]{1,0:T(8,128)(2,1)S(1)}, u32[]{:S(2)}, u32[]{:S(2)}) %collective-permute-start.7) | collective-permute-done | bytes 18464 | tf_op jit(solution)/shard_map/ppermute | solution.py:434
  35.3 0.0 copy-done.3
  35.3 0.0 copy-done.4
  35.3 1.3 %shard_map.95 = bf16[16,72,128]{2,1,0:T(8,128)(2,1)S(1)} custom-call(bf16[72,128]{1,0:T(8,128)(2,1)S(1)} %get-tuple-element.40.chunk0, bf16[72,128]{1,0:T(8,128)(2,1)S(1)} %collective-permute-done.6.chunk1, bf16[72,128]{1,0:T(8,128)(2,1)S(1)} %collective-permute-done.7.chunk2, bf16[2,48,384]{2,1,0:T(8,128)(2,1)S(1)} %get-tuple-element.45.old, ...), custom_call_target="tpu_custom_call" | custom-call | flops 3538944 | bytes 300000 | tf_op jit(solution)/shard_map/pallas_call | solution.py:135
  36.6 0.0 copy-start.1
  36.6 12.9 %all_to_all.26.blocks = bf16[16,72,128]{2,1,0:T(8,128)(2,1)S(1)} all-to-all(bf16[16,72,128]{2,1,0:T(8,128)(2,1)S(1)} %shard_map.95), channel_id=1, replica_groups=mesh['section'=2,'blk'=16] {'blk'}, dimensions={0} | all-to-all | bytes 589824 | tf_op jit(solution)/shard_map/all_to_all | solution.py:422
  49.5 0.0 copy-done.2
  49.5 0.9 shard_map.96
  50.4 12.4 %all_to_all.27.blocks = bf16[16,72,128]{2,1,0:T(8,128)(2,1)S(1)} all-to-all(bf16[16,72,128]{2,1,0:T(8,128)(2,1)S(1)} %get-tuple-element.48), channel_id=1, replica_groups=mesh['section'=2,'blk'=16] {'blk'}, dimensions={0} | all-to-all | bytes 589824 | tf_op jit(solution)/shard_map/all_to_all | solution.py:422
  62.8 0.0 copy-done.1
  62.8 1.7 %shard_map.97 = (bf16[72,128]{1,0:T(8,128)(2,1)S(1)}, bf16[72,128]{1,0:T(8,128)(2,1)S(1)}, bf16[72,128]{1,0:T(8,128)(2,1)S(1)}, bf16[48,192]{1,0:T(8,128)(2,1)S(1)}) custom-call(bf16[16,72,128]{2,1,0:T(8,128)(2,1)S(1)} %all_to_all.27.blocks, bf16[576,3072]{1,0:T(8,128)(2,1)S(1)} %bitcast.24, bf16[576,3072]{1,0:T(8,128)(2,1)S(1)} %collective-permute-done.4.other, ...), custom_call_target="tpu_custom_call" | custom-call | flops 169869312 | bytes 4718592 | tf_op jit(solution)/shard_map/pallas_call | solution.py:135
  64.5 0.8 collective-permute-start.8
  65.3 1.2 %collective-permute-start.9 = (bf16[72,128]{1,0:T(8,128)(2,1)S(1)}, bf16[72,128]{1,0:T(8,128)(2,1)S(1)}, u32[]{:S(2)}, u32[]{:S(2)}) collective-permute-start(bf16[72,128]{1,0:T(8,128)(2,1)S(1)} %get-tuple-element.52), channel_id=1, source_target_pairs={{0,6},{1,11},{2,8},{3,13},{4,10},{5,15},{6,12},{7,1},{8,14},{9,3},... | collective-permute-start | bytes 55304 | tf_op jit(solution)/shard_map/ppermute | solution.py:434
  66.5 2.7 %collective-permute-done.8.chunk1 = bf16[72,128]{1,0:T(8,128)(2,1)S(1)} collective-permute-done((bf16[72,128]{1,0:T(8,128)(2,1)S(1)}, bf16[72,128]{1,0:T(8,128)(2,1)S(1)}, u32[]{:S(2)}, u32[]{:S(2)}) %collective-permute-start.8) | collective-permute-done | bytes 18464 | tf_op jit(solution)/shard_map/ppermute | solution.py:434
  69.2 1.7 %collective-permute-done.9.chunk2 = bf16[72,128]{1,0:T(8,128)(2,1)S(1)} collective-permute-done((bf16[72,128]{1,0:T(8,128)(2,1)S(1)}, bf16[72,128]{1,0:T(8,128)(2,1)S(1)}, u32[]{:S(2)}, u32[]{:S(2)}) %collective-permute-start.9) | collective-permute-done | bytes 18464 | tf_op jit(solution)/shard_map/ppermute | solution.py:434
  70.8 1.3 %shard_map.98 = bf16[16,72,128]{2,1,0:T(8,128)(2,1)S(1)} custom-call(bf16[72,128]{1,0:T(8,128)(2,1)S(1)} %get-tuple-element.50.chunk0, bf16[72,128]{1,0:T(8,128)(2,1)S(1)} %collective-permute-done.8.chunk1, bf16[72,128]{1,0:T(8,128)(2,1)S(1)} %collective-permute-done.9.chunk2, bf16[2,48,384]{2,1,0:T(8,128)(2,1)S(1)} %get-tuple-element.45.old, ...), custom_call_target="tpu_custom_call" | custom-call | flops 3538944 | bytes 300000 | tf_op jit(solution)/shard_map/pallas_call | solution.py:135
  72.1 14.0 %all_to_all.28.blocks = bf16[16,72,128]{2,1,0:T(8,128)(2,1)S(1)} all-to-all(bf16[16,72,128]{2,1,0:T(8,128)(2,1)S(1)} %shard_map.98), channel_id=1, replica_groups=mesh['section'=2,'blk'=16] {'blk'}, dimensions={0} | all-to-all | bytes 589824 | tf_op jit(solution)/shard_map/all_to_all | solution.py:422
  86.1 0.7 shard_map.99
  86.8 9.7 %all_to_all.29.arrived = bf16[32,4,192]{2,1,0:T(4,128)(2,1)S(1)} all-to-all(bf16[32,4,192]{2,1,0:T(4,128)(2,1)S(1)} %shard_map.99), channel_id=1, replica_groups=mesh['section'=2,'blk'=16] {'section','blk'}, dimensions={0} | all-to-all | bytes 98304 | tf_op jit(solution)/shard_map/all_to_all | solution.py:422
  96.5 0.8 shard_map.100
  (1 shorter events, 0.0 us)
Async XLA Ops:
  0.0 1.5 %copy-start = (f32[1,50,3,3072]{3,0,2,1:T(1,128)S(1)}, f32[1,50,3,3072]{3,0,2,1:T(1,128)}, u32[]{:S(2)}) copy-start(f32[1,50,3,3072]{3,0,2,1:T(1,128)} %param.12) | copy-start | bytes 5529604
  0.0 2.0 %collective-permute-start = (bf16[3,2,3072]{2,1,0:T(2,128)(2,1)}, bf16[3,2,3072]{2,1,0:T(2,128)(2,1)S(1)}, u32[]{:S(2)}, u32[]{:S(2)}) collective-permute-start(bf16[3,2,3072]{2,1,0:T(2,128)(2,1)} %bitcast.29), channel_id=1, source_target_pairs={{0,16},{16,0},{1,17},{17,1},{2,18},{18,2},{3,19},{19,3},{4,20},{20... | collective-permute-start | bytes 110600 | tf_op jit(solution)/shard_map/ppermute | solution.py:426
  0.5 1.5 %collective-permute-start.1 = (bf16[3,2,3072]{2,1,0:T(2,128)(2,1)}, bf16[3,2,3072]{2,1,0:T(2,128)(2,1)S(1)}, u32[]{:S(2)}, u32[]{:S(2)}) collective-permute-start(bf16[3,2,3072]{2,1,0:T(2,128)(2,1)} %bitcast.31), channel_id=1, source_target_pairs={{0,16},{16,0},{1,17},{17,1},{2,18},{18,2},{3,19},{19,3},{4,20},{20... | collective-permute-start | bytes 110600 | tf_op jit(solution)/shard_map/ppermute | solution.py:426
  1.5 1.4 %collective-permute-start.2 = (f32[3,1,3072]{2,1,0:T(1,128)S(1)}, f32[3,1,3072]{2,1,0:T(1,128)S(1)}, u32[]{:S(2)}, u32[]{:S(2)}) collective-permute-start(f32[3,1,3072]{2,1,0:T(1,128)S(1)} %dynamic-slice_bitcast_fusion.mod), channel_id=1, source_target_pairs={{0,16},{16,0},{1,17},{17,1},{2,18},{18,2},{3,19},{19,3},{4,20},{20... | collective-permute-start | bytes 110600 | tf_op jit(solution)/shard_map/ppermute | solution.py:426
  2.0 1.4 %collective-permute-start.3 = (s32[1,2,16]{2,1,0:T(2,128)}, s32[1,2,16]{2,1,0:T(2,128)S(1)}, u32[]{:S(2)}, u32[]{:S(2)}) collective-permute-start(s32[1,2,16]{2,1,0:T(2,128)} %fresh.3), channel_id=1, source_target_pairs={{0,16},{16,0},{1,17},{17,1},{2,18},{18,2},{3,19},{19,3},{4,20},{20... | collective-permute-start | bytes 392 | tf_op jit(solution)/shard_map/ppermute | solution.py:426
  3.3 21.7 %collective-permute-start.4 = (bf16[576,3072]{1,0:T(8,128)(2,1)}, bf16[576,3072]{1,0:T(8,128)(2,1)S(1)}, u32[]{:S(2)}, u32[]{:S(2)}) collective-permute-start(bf16[576,3072]{1,0:T(8,128)(2,1)} %bitcast.22), channel_id=1, source_target_pairs={{0,16},{16,0},{1,17},{17,1},{2,18},{18,2},{3,19},{19,3},{4,20},{20... | collective-permute-start | bytes 10616840 | tf_op jit(solution)/shard_map/ppermute | solution.py:426
  3.5 21.5 %collective-permute-start.5 = (bf16[192,3072]{1,0:T(8,128)(2,1)}, bf16[192,3072]{1,0:T(8,128)(2,1)S(1)}, u32[]{:S(2)}, u32[]{:S(2)}) collective-permute-start(bf16[192,3072]{1,0:T(8,128)(2,1)} %bitcast.25), channel_id=1, source_target_pairs={{0,16},{16,0},{1,17},{17,1},{2,18},{18,2},{3,19},{19,3},{4,20},{20... | collective-permute-start | bytes 3538952 | tf_op jit(solution)/shard_map/ppermute | solution.py:426
  25.0 10.3 %copy-start.3 = (s32[1,2,16]{2,1,0:T(2,128)S(1)}, s32[1,2,16]{2,1,0:T(2,128)}, u32[]{:S(2)}) copy-start(s32[1,2,16]{2,1,0:T(2,128)} %fresh.3) | copy-start | bytes 388
  25.0 10.3 %copy-start.4 = (s32[2,16]{1,0:T(2,128)S(1)}, s32[2,16]{1,0:T(2,128)}, u32[]{:S(2)}) copy-start(s32[2,16]{1,0:T(2,128)} %live.3) | copy-start | bytes 388
  28.6 21.0 %copy-start.2 = (bf16[1,3072,192]{1,2,0:T(8,128)(2,1)S(1)}, bf16[1,3072,192]{1,2,0:T(8,128)(2,1)}, u32[]{:S(2)}) copy-start(bf16[1,3072,192]{1,2,0:T(8,128)(2,1)} %param.11) | copy-start | bytes 3538948
  28.6 4.7 %collective-permute-start.6 = (bf16[72,128]{1,0:T(8,128)(2,1)S(1)}, bf16[72,128]{1,0:T(8,128)(2,1)S(1)}, u32[]{:S(2)}, u32[]{:S(2)}) collective-permute-start(bf16[72,128]{1,0:T(8,128)(2,1)S(1)} %get-tuple-element.42), channel_id=1, source_target_pairs={{0,5},{1,12},{2,7},{3,14},{4,9},{5,0},{6,11},{7,2},{8,13},{9,4},{1... | collective-permute-start | bytes 55304 | tf_op jit(solution)/shard_map/ppermute | solution.py:434
  29.7 5.6 %collective-permute-start.7 = (bf16[72,128]{1,0:T(8,128)(2,1)S(1)}, bf16[72,128]{1,0:T(8,128)(2,1)S(1)}, u32[]{:S(2)}, u32[]{:S(2)}) collective-permute-start(bf16[72,128]{1,0:T(8,128)(2,1)S(1)} %get-tuple-element.43), channel_id=1, source_target_pairs={{0,6},{1,11},{2,8},{3,13},{4,10},{5,15},{6,12},{7,1},{8,14},{9,3},... | collective-permute-start | bytes 55304 | tf_op jit(solution)/shard_map/ppermute | solution.py:434
  36.6 26.2 %copy-start.1 = (bf16[1,3072,576]{1,2,0:T(8,128)(2,1)S(1)}, bf16[1,3072,576]{1,2,0:T(8,128)(2,1)}, u32[]{:S(2)}) copy-start(bf16[1,3072,576]{1,2,0:T(8,128)(2,1)} %param.10) | copy-start | bytes 10616836
  64.5 4.7 %collective-permute-start.8 = (bf16[72,128]{1,0:T(8,128)(2,1)S(1)}, bf16[72,128]{1,0:T(8,128)(2,1)S(1)}, u32[]{:S(2)}, u32[]{:S(2)}) collective-permute-start(bf16[72,128]{1,0:T(8,128)(2,1)S(1)} %get-tuple-element.51), channel_id=1, source_target_pairs={{0,5},{1,12},{2,7},{3,14},{4,9},{5,0},{6,11},{7,2},{8,13},{9,4},{1... | collective-permute-start | bytes 55304 | tf_op jit(solution)/shard_map/ppermute | solution.py:434
  65.3 5.6 %collective-permute-start.9 = (bf16[72,128]{1,0:T(8,128)(2,1)S(1)}, bf16[72,128]{1,0:T(8,128)(2,1)S(1)}, u32[]{:S(2)}, u32[]{:S(2)}) collective-permute-start(bf16[72,128]{1,0:T(8,128)(2,1)S(1)} %get-tuple-element.52), channel_id=1, source_target_pairs={{0,6},{1,11},{2,8},{3,13},{4,10},{5,15},{6,12},{7,1},{8,14},{9,3},... | collective-permute-start | bytes 55304 | tf_op jit(solution)/shard_map/ppermute | solution.py:434
